TPU v7x, 256 devices: a whole 4x4x8 slice. The times are simulated.
256 devices in a mesh: ctx: 32 (over x, z), voc: 8 (over y, core).
Axes of the slice: x: 4, y: 4, z: 8, core: 2. Of those that a mesh axis runs over, the one named last changes fastest.
Arguments:
- hidden: bfloat16 [4096, 896], P('ctx')
- token_weight: bfloat16 [4096], P('ctx'), may hold values from 1 to 16
- head_weight: bfloat16 [896, 131072], P(None, ('ctx', 'voc'))
- teacher_logits: bfloat16 [4096, 65536], P('ctx', 'voc')
- block_coeff: bfloat16 [512, 128, 128], P('voc')
- block_map: int32 [512], replicated, may hold values from 0 to 1023, as said below
Outputs:
- grad_hidden: bfloat16 [4096, 896], P('ctx')
- grad_weight: float32 [896, 131072], P(None, ('ctx', 'voc'))
- row_loss: float32 [4096], P('ctx')
Inputs may be any that keep to these rules, and one draw needn't show every extreme that they name: `block_map`: student block s belongs to voc index (s // 4) modulo the number of voc indices, and teacher block b to voc index b // 64. Of the 64 teacher blocks of one voc index, at most 16 map into the student blocks of any one voc index; in every draw one voc index receives exactly 16 from every voc index.
All inputs are finite; a program needn't handle non-finite values.
Results may differ from a plain program's by a relative error of at most 0.014.
Values may be sent and summed in bfloat16 or wider, within the bound.
No kernel may reach another device: no remote copies, remote signals or barrier semaphores. Data moves between devices by JAX's collectives and lax.ppermute only.
A program may use at most 192 MiB of HBM per device.

v0:
```python
import jax
import jax.numpy as jnp
from jax import lax
from jax.sharding import PartitionSpec as P


def local(hidden, token_weight, head_weight, teacher_logits, block_coeff, block_map):
    ctx_count = lax.axis_size("ctx")
    voc_count = lax.axis_size("voc")
    voc_index = lax.axis_index("voc")
    ctx_index = lax.axis_index("ctx")
    rows_dev = hidden.shape[0]
    half_rows = rows_dev // 2
    block_size = block_coeff.shape[1]
    local_blocks = block_coeff.shape[0]
    cols_dev = head_weight.shape[1]
    dev_blocks = cols_dev // block_size
    voc_blocks = dev_blocks * ctx_count
    capacity = 2 * local_blocks // voc_count
    teacher = teacher_logits.astype(jnp.float32)
    local_top = jnp.max(teacher, axis=1)
    row_max = lax.pmax(local_top, "voc")
    row_total = lax.psum(jnp.sum(jnp.exp(teacher - row_max[:, None]), axis=1), "voc")
    teacher_prob = (jnp.exp(teacher - row_max[:, None]) / row_total[:, None]).astype(jnp.bfloat16)
    mapped = jnp.einsum(
        "rbi,bij->brj",
        teacher_prob.reshape(rows_dev, local_blocks, block_size),
        block_coeff,
        preferred_element_type=jnp.float32,
    ).astype(jnp.bfloat16)
    owner_voc = (block_map // dev_blocks % voc_count).reshape(voc_count, local_blocks)
    owner_block = (
        block_map // (voc_count * dev_blocks) * dev_blocks + block_map % dev_blocks
    ).reshape(voc_count, local_blocks)
    owner_onehot = (
        owner_voc[:, :, None] == jnp.arange(voc_count, dtype=jnp.int32)[None, None, :]
    ).astype(jnp.int32)
    queue_slot = jnp.sum((jnp.cumsum(owner_onehot, axis=1) - 1) * owner_onehot, axis=2)
    mine_owner = lax.dynamic_index_in_dim(owner_voc, voc_index, 0, keepdims=False)
    mine_slot = lax.dynamic_index_in_dim(queue_slot, voc_index, 0, keepdims=False)
    send_slot = mine_owner * capacity + mine_slot
    sender = (
        jnp.arange(voc_count * capacity, dtype=jnp.int32)[:, None] == send_slot[None, :]
    ).astype(jnp.bfloat16)
    outgoing = jnp.einsum("kb,brj->krj", sender, mapped, preferred_element_type=jnp.float32).astype(
        jnp.bfloat16
    )
    outgoing = outgoing.reshape(voc_count, capacity, rows_dev, block_size)
    incoming = lax.all_to_all(outgoing, "voc", split_axis=0, concat_axis=0, tiled=True)
    arriving = jnp.where(owner_voc == voc_index, queue_slot, -1)
    slot_match = (
        arriving[:, None, :] == jnp.arange(capacity, dtype=jnp.int32)[None, :, None]
    ).astype(jnp.float32)
    landing = (
        owner_block[:, :, None] == jnp.arange(voc_blocks, dtype=jnp.int32)[None, None, :]
    ).astype(jnp.float32)
    collect = jnp.einsum("skb,sbl->lsk", slot_match, landing).astype(jnp.bfloat16)
    target = jnp.einsum(
        "lsk,skrj->rlj", collect, incoming, preferred_element_type=jnp.float32
    ).astype(jnp.bfloat16)
    owned = lax.all_to_all(target, "ctx", split_axis=1, concat_axis=0, tiled=True)
    tokens = ctx_count * rows_dev
    in_order = owned.reshape(2 * ctx_count, half_rows, cols_dev)
    folded = jnp.stack([in_order[:ctx_count], in_order[ctx_count:][::-1]], axis=1).reshape(
        tokens, cols_dev
    )
    all_rows, all_weights = (
        lax.all_gather(hidden, "ctx", axis=0, tiled=True),
        lax.all_gather(token_weight, "ctx", axis=0, tiled=True),
    )
    logits = jnp.dot(all_rows, head_weight, preferred_element_type=jnp.float32)
    target_full = folded.astype(jnp.float32)
    mass_part = jnp.sum(target_full, axis=1)
    cross_part = jnp.sum(target_full * logits, axis=1)
    local_top = jnp.max(logits, axis=1)
    row_max = lax.pmax(local_top, ("ctx", "voc"))
    row_total, row_mass, row_cross = lax.psum(
        (jnp.sum(jnp.exp(logits - row_max[:, None]), axis=1), mass_part, cross_part), ("ctx", "voc")
    )
    norm_log = row_max + jnp.log(row_total)
    loss_all = row_mass * norm_log - row_cross
    row_loss = lax.dynamic_slice_in_dim(loss_all, ctx_index * rows_dev, rows_dev, 0)
    grad_logits = (
        all_weights.astype(jnp.float32)[:, None]
        * (row_mass[:, None] * jnp.exp(logits - norm_log[:, None]) - target_full)
    ).astype(jnp.bfloat16)
    grad_weight = lax.dot_general(
        all_rows, grad_logits, (((0,), (0,)), ((), ())), preferred_element_type=jnp.float32
    )
    summed = lax.psum_scatter(
        lax.dot_general(
            grad_logits, head_weight, (((1,), (1,)), ((), ())), preferred_element_type=jnp.float32
        ),
        "ctx",
        scatter_dimension=0,
        tiled=True,
    )
    grad_hidden = lax.psum(summed, "voc").astype(jnp.bfloat16)
    return (grad_hidden, grad_weight, row_loss)


def solution(mesh):
    return jax.shard_map(
        local,
        mesh=mesh,
        in_specs=(
            P("ctx", None),
            P("ctx"),
            P(None, ("ctx", "voc")),
            P("ctx", "voc"),
            P("voc", None, None),
            P(),
        ),
        out_specs=(P("ctx", None), P(None, ("ctx", "voc")), P("ctx")),
        check_vma=False,
    )
```

profile of v0, /device:TPU:1, one launch (start us, length us, event | category | flops | bytes accessed | tf_op | source)
XLA Modules:
  0.0 745.1 jit_solution(14264570025614045395)
XLA Ops:
  7.9 1.9 reduce_max.23
  9.9 15.0 %pmax.14 = f32[128]{0:T(128)S(1)} all-reduce(bf16[128]{0:T(256)(128)(2,1)S(1)} %reduce_max.23), channel_id=1, replica_groups=mesh['ctx'=32,'voc'=8] {'voc'}, use_global_device_ids=true, to_apply=%region_3.0 | all-reduce | flops 128 | bytes 768 | tf_op jit(solution)/shard_map/pmax | solution.py:22
  24.9 2.4 fusion.1
  27.3 13.2 %psum.35 = f32[128]{0:T(128)S(1)} all-reduce(f32[128]{0:T(128)S(1)} %fusion.1), channel_id=1, replica_groups=mesh['ctx'=32,'voc'=8] {'voc'}, use_global_device_ids=true, to_apply=%region_5.6 | all-reduce | flops 128 | bytes 1024 | tf_op jit(solution)/shard_map/psum | solution.py:23
  40.7 4.0 fusion.7
  46.2 3.6 convolution_convert_fusion
  49.8 2.8 copy.35
  52.6 5.8 all-to-all-start
  58.6 48.8 %all-to-all-done = bf16[8,16,128,128]{3,1,2,0:T(8,128)(2,1)} async-done(((bf16[8,16,128,128]{3,1,2,0:T(8,128)(2,1)}), bf16[8,16,128,128]{3,1,2,0:T(8,128)(2,1)}, u32[]{:S(2)}, u32[]{:S(2)}) %all-to-all-start) | async-done | bytes 4194336 | tf_op jit(solution)/shard_map/all_to_all | solution.py:49
  107.4 5.7 fusion
  113.1 6.7 copy.38
  119.8 10.6 %all-to-all-start.1 = ((bf16[128,128,128]{2,0,1:T(8,128)(2,1)}), bf16[128,128,128]{2,0,1:T(8,128)(2,1)}, u32[]{:S(2)}, u32[]{:S(2)}) async-start(bf16[128,128,128]{2,0,1:T(8,128)(2,1)} %copy.38), calls=%async_computation.1 | async-start | bytes 8388608 | tf_op jit(solution)/shard_map/all_to_all | solution.py:61
  130.5 117.6 %all-gather = bf16[32,1,128]{2,1,0:T(2,128)(2,1)S(1)} all-gather(bf16[1,1,128]{2,1,0:T(2,128)(2,1)S(1)} %bitcast.48), channel_id=1, replica_groups=mesh['ctx'=32,'voc'=8] {'ctx'}, dimensions={0}, use_global_device_ids=true | all-gather | bytes 8448 | tf_op jit(solution)/shard_map/all_gather | solution.py:69
  248.2 4.2 fusion.27
  252.3 3.1 copy.39
  255.4 2.7 stack.9
  258.2 4.7 copy.40
  262.8 4.2 slice.12
  270.9 2.1 maximum_convert_fusion
  273.1 4.3 copy.42
  277.4 9.0 %copy.43 = f32[4096,512]{0,1:T(8,128)} copy(f32[4096,512]{1,0:T(8,128)} %bitcast.45) | data formatting | bytes 16777216 | tf_op jit(solution)/shard_map/convert_element_type | solution.py:72
  286.5 9.9 %fusion.29 = (f32[4096]{0:T(1024)S(1)}, f32[4096,512]{0,1:T(8,128)}) fusion(bf16[4096,896]{1,0:T(8,128)(2,1)} %all-gather.3.cloned.1.call-done, bf16[896,512]{1,0:T(8,128)(2,1)S(1)} %copy-done.6), kind=kOutput, calls=%fused_computation.57 | convolution fusion | flops 3760189440 | bytes 16662528 | tf_op jit(solution)/shard_map/dot_general | solution.py:71
  296.4 79.6 %pmax.15 = f32[4096]{0:T(1024)S(1)} all-reduce(f32[4096]{0:T(1024)S(1)} %get-tuple-element.24), channel_id=1, replica_groups=mesh['ctx'=32,'voc'=8] {'ctx','voc'}, use_global_device_ids=true, to_apply=%region_9.10 | all-reduce | flops 4096 | bytes 32768 | tf_op jit(solution)/shard_map/pmax | solution.py:76
  376.0 6.7 multiply_reduce_fusion
  382.7 74.7 %all-reduce = (f32[4096]{0:T(1024)S(1)}, f32[4096]{0:T(1024)S(1)}, f32[4096]{0:T(1024)S(1)}) all-reduce(f32[4096]{0:T(1024)S(1)} %get-tuple-element.16, f32[4096]{0:T(1024)S(1)} %reduce_sum.50, f32[4096]{0:T(1024)S(1)} %get-tuple-element.15), channel_id=1, replica_groups=mesh['ctx'=32,'voc'=8] {'ctx','voc'}, use_global_device_ids=true, to_apply=%region_11.12 | all-reduce | flops 12288 | bytes 98304 | tf_op jit(solution)/shard_map/psum | solution.py:77
  457.4 6.9 multiply_convert_fusion
  464.4 2.0 copy-done.3
  466.4 7.8 %fusion.30 = f32[4096,896]{1,0:T(8,128)} fusion(bf16[4096,512]{0,1:T(8,128)(2,1)S(1)} %multiply_convert_fusion, bf16[896,512]{1,0:T(8,128)(2,1)S(1)} %copy-done.6), kind=kOutput, calls=%fused_computation.58 | convolution fusion | flops 3758096384 | bytes 19791872 | tf_op jit(solution)/shard_map/dot_general | solution.py:91
  474.2 10.2 %convolution_bitcast_fusion = f32[896,512]{0,1:T(8,128)} fusion(bf16[4096,512]{0,1:T(8,128)(2,1)} %copy-done.3, bf16[4096,896]{1,0:T(8,128)(2,1)} %all-gather.3.cloned.1.call-done), kind=kOutput, calls=%fused_computation.17 | convolution fusion | flops 3758096384 | bytes 13369344 | tf_op jit(solution)/shard_map/dot_general | solution.py:87
  484.4 2.7 copy.45
  487.7 220.0 %reduce-scatter.2.cloned.1.call-done = f32[128,896]{1,0:T(8,128)} async-done(((f32[4096,896]{1,0:T(8,128)}), f32[128,896]{1,0:T(8,128)}) %reduce-scatter.2.cloned.1.call-update) | async-done | bytes 458768 | tf_op jit(solution)/shard_map/reduce_scatter | solution.py:90
  707.7 30.5 %all-reduce.2 = bf16[128,896]{1,0:T(8,128)(2,1)} all-reduce(f32[128,896]{1,0:T(8,128)} %reduce-scatter.2.cloned.1.call-done), channel_id=1, replica_groups=mesh['ctx'=32,'voc'=8] {'voc'}, use_global_device_ids=true, to_apply=%region_13.14 | all-reduce | flops 114688 | bytes 688128 | tf_op jit(solution)/shard_map/psum | solution.py:98
  (34 shorter events, 7.2 us)
Async XLA Ops:
  7.2 33.5 %copy-start = (bf16[64,128,128]{2,1,0:T(8,128)(2,1)S(1)}, bf16[64,128,128]{2,1,0:T(8,128)(2,1)}, u32[]{:S(2)}) copy-start(bf16[64,128,128]{2,1,0:T(8,128)(2,1)} %param.10) | copy-start | bytes 6291460
  7.2 33.3 %copy-start.4 = (s32[512]{0:T(512)S(1)}, s32[512]{0:T(512)}, u32[]{:S(2)}) copy-start(s32[512]{0:T(512)} %param.11) | copy-start | bytes 6148
  7.2 279.3 %all-gather.3.cloned.1.call-start = ((), (), s32[]{:S(2)}) async-start(), calls=%async_computation.3 | async-start | bytes 7569408 | tf_op jit(solution)/shard_map/all_gather | solution.py:68
  52.6 54.7 %all-to-all-start = ((bf16[8,16,128,128]{3,1,2,0:T(8,128)(2,1)}), bf16[8,16,128,128]{3,1,2,0:T(8,128)(2,1)}, u32[]{:S(2)}, u32[]{:S(2)}) async-start(bf16[8,16,128,128]{3,1,2,0:T(8,128)(2,1)} %copy.35), calls=%async_computation | async-start | bytes 8388608 | tf_op jit(solution)/shard_map/all_to_all | solution.py:49
  119.8 10.7 %copy-start.5 = (bf16[128]{0:T(256)(128)(2,1)S(1)}, bf16[128]{0:T(256)(128)(2,1)}, u32[]{:S(2)}) copy-start(bf16[128]{0:T(256)(128)(2,1)} %param.7) | copy-start | bytes 772
  119.8 128.3 %all-to-all-start.1 = ((bf16[128,128,128]{2,0,1:T(8,128)(2,1)}), bf16[128,128,128]{2,0,1:T(8,128)(2,1)}, u32[]{:S(2)}, u32[]{:S(2)}) async-start(bf16[128,128,128]{2,0,1:T(8,128)(2,1)} %copy.38), calls=%async_computation.1 | async-start | bytes 8388608 | tf_op jit(solution)/shard_map/all_to_all | solution.py:61
  130.5 577.2 %reduce-scatter.2.cloned.1.call-start = ((), (), s32[]{:S(2)}) async-start(), calls=%async_computation.4 | async-start | bytes 15138816 | tf_op jit(solution)/shard_map/reduce_scatter | solution.py:90
  268.8 1.4 copy-start.2
  277.4 9.0 %copy-start.6 = (bf16[896,512]{1,0:T(8,128)(2,1)S(1)}, bf16[896,512]{1,0:T(8,128)(2,1)}, u32[]{:S(2)}) copy-start(bf16[896,512]{1,0:T(8,128)(2,1)} %param.8) | copy-start | bytes 2752516
  464.4 2.0 copy-start.3
  474.2 264.0 %copy-start.1 = (bf16[64,128,128]{2,1,0:T(8,128)(2,1)S(1)}, bf16[64,128,128]{2,1,0:T(8,128)(2,1)}, u32[]{:S(2)}) copy-start(bf16[64,128,128]{2,1,0:T(8,128)(2,1)} %param.10) | copy-start | bytes 6291460
Sparse Core Ops, SparseCore 0:
  10.6 96.6 all-gather.2
  474.3 233.3 reduce-scatter.1
where the time goes:
time: 748 us; the launch traced here: 745 us
  blocking collectives  331 us (44%)
  waiting for transfers between devices  269 us (36%)
  local copies, waits for them, and re-layouts  50.1 us (7%)
  matrix products  41.3 us (6%)
  other arithmetic  22.9 us (3%)
  starting transfers between devices  16.5 us (2%)
  between operations  14.2 us (2%)
    reduce_scatter x1, waiting for transfers between devices, local(): lax.psum_scatter(lax.dot_general(grad_logits, head_weight, (((1,), (1,)),...  220 us
    all_gather x1, blocking collectives, local(): lax.all_gather(token_weight, 'ctx', axis=0, tiled=True)  118 us
    pmax x1, blocking collectives, local(): row_max = lax.pmax(local_top, ('ctx', 'voc'))  79.6 us
    psum x1, blocking collectives, local(): lax.psum((jnp.sum(jnp.exp(logits - row_max[:, None]), axis=1), mass_part,...  74.7 us
    all_to_all x1, waiting for transfers between devices, local(): lax.all_to_all(outgoing, 'voc', split_axis=0, concat_axis=0, tiled=True)  48.8 us
    psum x1, blocking collectives, local(): grad_hidden = lax.psum(summed, 'voc').astype(jnp.bfloat16)  30.5 us
    pmax x1, blocking collectives, local(): row_max = lax.pmax(local_top, 'voc')  15 us
  transfers between devices with their start and end apart: 4, of which 2 were waited for; matrix products, arithmetic and copies ran while one was open for 11% of the time, Pallas kernels for 0%

commit v1 on v0

v1 whole, which is shorter than its diff:
```python
import functools

import jax
import jax.numpy as jnp
from jax import lax
from jax.experimental import pallas as pl
from jax.experimental.pallas import tpu as pltpu
from jax.sharding import PartitionSpec as P

F32 = jnp.float32
BF16 = jnp.bfloat16
LANES = 128
VMEM_LIMIT = 56 * 1024 * 1024


def params():
    return pltpu.CompilerParams(vmem_limit_bytes=VMEM_LIMIT)


def pieces(value):
    high = value.astype(BF16).astype(F32)
    rest = value - high
    middle = rest.astype(BF16).astype(F32)
    return high, middle, rest - middle


def lanes_of(columns, rows):
    lane = lax.broadcasted_iota(jnp.int32, (rows, LANES), 1)
    tile = jnp.zeros((rows, LANES), F32)
    for index, column in enumerate(columns):
        tile = jnp.where(lane == index, column, tile)
    return tile


def teacher_kernel(logits_ref, coeff_ref, out_ref):
    rows = logits_ref.shape[0]
    groups, _, part, _ = out_ref.shape
    blocks = coeff_ref.shape[0]

    def top(b, carry):
        return jnp.maximum(carry, logits_ref[:, pl.ds(pl.multiple_of(b * LANES, LANES), LANES)])

    widest = lax.fori_loop(
        1, blocks, top, logits_ref[:, 0:LANES], unroll=4
    ).astype(F32)
    row_max = jnp.max(widest, axis=1, keepdims=True)

    def one(b, total):
        x = logits_ref[:, pl.ds(pl.multiple_of(b * LANES, LANES), LANES)].astype(F32)
        e = jnp.exp(x - row_max)
        mapped = jnp.dot(e.astype(BF16), coeff_ref[b], preferred_element_type=F32).astype(BF16)
        out_ref[:, b] = mapped.reshape(groups, part, LANES)
        return total + e

    total = lax.fori_loop(0, blocks, one, jnp.zeros((rows, LANES), F32), unroll=4)
    row_total = jnp.sum(total, axis=1, keepdims=True)
    tile = lanes_of((row_max,) + pieces(row_total), rows).astype(BF16)
    out_ref[:, blocks] = tile.reshape(groups, part, LANES)


def collect_kernel(slot_ref, in_ref, out_ref, mass_ref, sums, scales):
    voc_count, held, part, _ = in_ref.shape
    blocks = held - 1
    slots = out_ref.shape[0]
    tops, totals = [], []
    for v in range(voc_count):
        tile = in_ref[v, blocks].astype(F32)
        tops.append(tile[:, 0:1])
        totals.append(tile[:, 1:2] + tile[:, 2:3] + tile[:, 3:4])
    top = functools.reduce(jnp.maximum, tops)
    total = functools.reduce(
        jnp.add, [part_total * jnp.exp(part_top - top) for part_total, part_top in zip(totals, tops)]
    )
    for v in range(voc_count):
        scales[v] = jnp.broadcast_to(jnp.exp(tops[v] - top) / total, (part, LANES))

    def clear(s, carry):
        sums[s] = jnp.zeros((part, LANES), F32)
        return carry

    lax.fori_loop(0, slots, clear, 0, unroll=8)
    for v in range(voc_count):
        scale = scales[v]

        def add(b, carry):
            slot = slot_ref[v * blocks + b]
            sums[slot] = sums[slot] + scale * in_ref[v, b].astype(F32)
            return carry

        lax.fori_loop(0, blocks, add, 0, unroll=4)

    def store(s, mass):
        target = sums[s].astype(BF16)
        out_ref[s] = target
        return mass + target.astype(F32)

    mass = lax.fori_loop(0, slots, store, jnp.zeros((part, LANES), F32), unroll=8)
    mass_ref[...] = jnp.broadcast_to(jnp.sum(mass, axis=1, keepdims=True), (part, LANES))


def logits_kernel(hidden_ref, weight_ref, mass_ref, logits_ref, stats_ref, tops, totals):
    step = pl.program_id(0)
    rows, cols = logits_ref.shape[1:]

    @pl.when(step == 0)
    def _():
        tops[...] = jnp.full(tops.shape, -jnp.inf, F32)
        totals[...] = jnp.zeros(totals.shape, F32)

    logits = jnp.dot(hidden_ref[...], weight_ref[0], preferred_element_type=F32)
    logits_ref[0] = logits
    tiles = [logits[:, k : k + LANES] for k in range(0, cols, LANES)]
    old = tops[...]
    new = functools.reduce(jnp.maximum, tiles, old)
    total = totals[...] * jnp.exp(old - new)
    for tile in tiles:
        total = total + jnp.exp(tile - new)
    tops[...] = new
    totals[...] = total

    @pl.when(step == pl.num_programs(0) - 1)
    def _():
        lane_top, lane_total = tops[...], totals[...]
        top = jnp.max(lane_top, axis=1, keepdims=True)
        total = jnp.sum(lane_total * jnp.exp(lane_top - top), axis=1, keepdims=True)
        part = mass_ref.shape[0]
        flat = jnp.transpose(lanes_of((top, total), rows))
        mass = jnp.transpose(mass_ref[...])
        mass = jnp.concatenate([mass[0:1], jnp.zeros((1, rows - part), F32)], axis=1)
        packed = jnp.concatenate([flat[0:2], mass, jnp.zeros((1, rows), F32)], axis=0)
        stats_ref[...] = jnp.broadcast_to(packed[None], stats_ref.shape)


def grad_kernel(
    place_ref, stats_ref, logits_ref, target_ref, hidden_ref, hidden_t_ref, weight_ref,
    dweight_ref, dhidden_ref, base_ref, norm, mass, gain, cross, partial,
):
    step = pl.program_id(0)
    count, _, part, _ = target_ref.shape
    rows, cols = logits_ref.shape[1:]
    width = weight_ref.shape[1]

    @pl.when(step == 0)
    def _():
        tops = stats_ref[:, 0, :]
        top = jnp.max(tops, axis=0, keepdims=True)
        total = jnp.sum(stats_ref[:, 1, :] * jnp.exp(tops - top), axis=0, keepdims=True)
        norm_row = jnp.broadcast_to(top + jnp.log(total), (LANES, rows))
        norm[...] = jnp.transpose(norm_row)
        own = stats_ref[:, 2, 0:LANES]
        spread = jnp.broadcast_to(own[:, None, :], (count, part, LANES))
        diagonal = lax.broadcasted_iota(jnp.int32, (count, part, LANES), 1) == lax.broadcasted_iota(
            jnp.int32, (count, part, LANES), 2
        )
        column = jnp.sum(jnp.where(diagonal, spread, 0.0), axis=2, keepdims=True).reshape(rows, 1)
        mass[...] = jnp.broadcast_to(column, (rows, LANES))
        gain[...] = jnp.broadcast_to(
            hidden_ref[:, width : width + LANES].astype(F32)[:, 0:1], (rows, LANES)
        )
        cross[...] = jnp.zeros(cross.shape, F32)

    norm_tile, mass_tile, gain_tile = norm[...], mass[...], gain[...]
    crossed = cross[...]
    grads = []
    for q in range(cols // LANES):
        logit = logits_ref[0, :, q * LANES : (q + 1) * LANES]
        target = target_ref[:, q].reshape(rows, LANES).astype(F32)
        crossed = crossed + target * logit
        grads.append(
            (gain_tile * (mass_tile * jnp.exp(logit - norm_tile) - target)).astype(BF16)
        )
    cross[...] = crossed
    grad = jnp.concatenate(grads, axis=1)
    dweight_ref[0] = jnp.dot(hidden_t_ref[...], grad, preferred_element_type=F32).astype(BF16)
    product = lax.dot_general(
        grad, weight_ref[0], (((1,), (1,)), ((), ())), preferred_element_type=F32
    )

    @pl.when(step == 0)
    def _():
        partial[...] = product

    @pl.when(step > 0)
    def _():
        partial[...] = partial[...] + product

    @pl.when(step == pl.num_programs(0) - 1)
    def _():
        cross_sum = jnp.sum(cross[...], axis=1, keepdims=True)
        cross[...] = lanes_of(pieces(cross_sum), rows)
        for t in range(count):
            c = place_ref[t]
            dhidden_ref[c, :, 0:width] = partial[t * part : (t + 1) * part, :].astype(BF16)
            dhidden_ref[c, :, width : width + LANES] = cross[t * part : (t + 1) * part, :].astype(BF16)
        mass[...] = mass[...] * norm[...]
        start = pl.multiple_of(place_ref[count] * part, part)
        base_ref[...] = mass[pl.ds(start, part), :]


def finish_kernel(in_ref, base_ref, out_ref):
    count, part, wide = in_ref.shape
    width = wide - LANES
    total = jnp.zeros((part, wide), F32)
    for c in range(count):
        total = total + in_ref[c].astype(F32)
    out_ref[:, 0:width] = total[:, 0:width].astype(BF16)
    tail = total[:, width:wide]
    crossed = tail[:, 0:1] + tail[:, 1:2] + tail[:, 2:3]
    loss = base_ref[...][:, 0:1] - crossed
    out_ref[:, width:wide] = lanes_of(pieces(loss), part).astype(BF16)


def whole(shape):
    return pl.BlockSpec(shape, lambda *_: (0,) * len(shape))


def local(hidden, token_weight, head_weight, teacher_logits, block_coeff, block_map):
    ctx_count = lax.axis_size("ctx")
    voc_count = lax.axis_size("voc")
    voc_index = lax.axis_index("voc")
    ctx_index = lax.axis_index("ctx")
    rows_dev, width = hidden.shape
    half_rows = rows_dev // 2
    part = rows_dev // voc_count
    half_groups = voc_count // 2
    local_blocks = block_coeff.shape[0]
    cols = head_weight.shape[1]
    dev_blocks = cols // LANES
    owned_blocks = voc_count * dev_blocks
    slots = ctx_count * owned_blocks
    rows = ctx_count * part
    smem = pl.BlockSpec(memory_space=pltpu.SMEM)

    parity = voc_index // half_groups
    fold = jnp.where(ctx_index % 2 == parity, 0, 1)
    start = fold * half_rows + voc_index % half_groups * part
    mine = lax.dynamic_slice_in_dim(hidden, start, part, 0)
    mine_weight = lax.dynamic_slice_in_dim(token_weight, start, part, 0)
    mine = jnp.concatenate([mine, jnp.broadcast_to(mine_weight[:, None], (part, LANES))], axis=1)
    by_ctx = lax.all_to_all(
        jnp.broadcast_to(mine[None], (ctx_count, part, width + LANES)), "ctx", 0, 0, tiled=True
    )
    source = jnp.arange(ctx_count, dtype=jnp.int32)
    half_block = 2 * source + parity
    place = jnp.where(half_block < ctx_count, half_block, 2 * ctx_count - 1 - half_block)
    own_half = jnp.where(fold == 0, ctx_index, 2 * ctx_count - 1 - ctx_index)
    place = jnp.concatenate([place, (own_half // 2)[None]]).astype(jnp.int32)
    hidden_rows = by_ctx[place[:ctx_count]].reshape(rows, width + LANES)
    hidden_t = hidden_rows[:, :width].T

    outgoing = pl.pallas_call(
        teacher_kernel,
        out_shape=jax.ShapeDtypeStruct((voc_count, local_blocks + 1, part, LANES), BF16),
        compiler_params=params(),
        cost_estimate=pl.CostEstimate(
            flops=2 * rows_dev * local_blocks * LANES * LANES,
            bytes_accessed=6 * 1024 * 1024,
            transcendentals=rows_dev * local_blocks * LANES,
        ),
        name="teacher_map",
    )(teacher_logits, block_coeff)
    incoming = lax.all_to_all(outgoing, "voc", 0, 0, tiled=True)

    head_weight, incoming = lax.optimization_barrier((head_weight, incoming))
    weights = lax.all_gather(head_weight, "voc", axis=0, tiled=False)

    target, mass = pl.pallas_call(
        collect_kernel,
        out_shape=(
            jax.ShapeDtypeStruct((slots, part, LANES), BF16),
            jax.ShapeDtypeStruct((part, LANES), F32),
        ),
        in_specs=[smem, pl.BlockSpec(memory_space=pltpu.VMEM)],
        scratch_shapes=[
            pltpu.VMEM((slots, part, LANES), F32),
            pltpu.VMEM((voc_count, part, LANES), F32),
        ],
        compiler_params=params(),
        cost_estimate=pl.CostEstimate(
            flops=4 * slots * part * LANES, bytes_accessed=6 * 1024 * 1024, transcendentals=0
        ),
        name="collect_targets",
    )(block_map, incoming)
    target = target.reshape(ctx_count, owned_blocks, part, LANES)
    arrived = lax.all_to_all(target, "ctx", 0, 0, tiled=True)

    logits, stats = pl.pallas_call(
        logits_kernel,
        grid=(voc_count,),
        in_specs=[
            pl.BlockSpec((rows, width), lambda j: (0, 0)),
            pl.BlockSpec((1, width, cols), lambda j: (j, 0, 0)),
            whole((part, LANES)),
        ],
        out_specs=(
            pl.BlockSpec((1, rows, cols), lambda j: (j, 0, 0)),
            whole((ctx_count, 4, rows)),
        ),
        out_shape=(
            jax.ShapeDtypeStruct((voc_count, rows, cols), F32),
            jax.ShapeDtypeStruct((ctx_count, 4, rows), F32),
        ),
        scratch_shapes=[pltpu.VMEM((rows, LANES), F32)] * 2,
        compiler_params=params(),
        cost_estimate=pl.CostEstimate(
            flops=2 * rows * width * cols * voc_count,
            bytes_accessed=18 * 1024 * 1024,
            transcendentals=rows * cols * voc_count,
        ),
        name="student_logits",
    )(hidden_rows, weights, mass)
    all_stats = lax.all_to_all(stats, "ctx", 0, 0, tiled=True)

    dweight, dhidden, base = pl.pallas_call(
        grad_kernel,
        grid=(voc_count,),
        in_specs=[
            smem,
            whole((ctx_count, 4, rows)),
            pl.BlockSpec((1, rows, cols), lambda j: (j, 0, 0)),
            pl.BlockSpec((ctx_count, dev_blocks, part, LANES), lambda j: (0, j, 0, 0)),
            whole((rows, width + LANES)),
            whole((width, rows)),
            pl.BlockSpec((1, width, cols), lambda j: (j, 0, 0)),
        ],
        out_specs=(
            pl.BlockSpec((1, width, cols), lambda j: (j, 0, 0)),
            whole((ctx_count, part, width + LANES)),
            whole((part, LANES)),
        ),
        out_shape=(
            jax.ShapeDtypeStruct((voc_count, width, cols), BF16),
            jax.ShapeDtypeStruct((ctx_count, part, width + LANES), BF16),
            jax.ShapeDtypeStruct((part, LANES), F32),
        ),
        scratch_shapes=[pltpu.VMEM((rows, LANES), F32)] * 4 + [pltpu.VMEM((rows, width), F32)],
        compiler_params=params(),
        cost_estimate=pl.CostEstimate(
            flops=4 * rows * width * cols * voc_count,
            bytes_accessed=30 * 1024 * 1024,
            transcendentals=rows * cols * voc_count,
        ),
        name="grads",
    )(place, all_stats, logits, arrived, hidden_rows, hidden_t, weights)
    grad_weight = lax.psum_scatter(dweight, "voc", scatter_dimension=0, tiled=True)
    grad_weight = grad_weight.reshape(width, cols).astype(F32)
    returned = lax.all_to_all(dhidden, "ctx", 0, 0, tiled=True)
    done = pl.pallas_call(
        finish_kernel,
        out_shape=jax.ShapeDtypeStruct((part, width + LANES), BF16),
        compiler_params=params(),
        name="finish_rows",
    )(returned, base)
    all_done = lax.all_gather(done, "voc", axis=0, tiled=False)
    all_done = jnp.where(ctx_index % 2 == 0, all_done, jnp.roll(all_done, half_groups, axis=0))
    all_done = all_done.reshape(rows_dev, width + LANES)
    grad_hidden = all_done[:, :width]
    row_loss = jnp.sum(all_done[:, width : width + 3].astype(F32), axis=1)
    return (grad_hidden, grad_weight, row_loss)


def solution(mesh):
    return jax.shard_map(
        local,
        mesh=mesh,
        in_specs=(
            P("ctx", None),
            P("ctx"),
            P(None, ("ctx", "voc")),
            P("ctx", "voc"),
            P("voc", None, None),
            P(),
        ),
        out_specs=(P("ctx", None), P(None, ("ctx", "voc")), P("ctx")),
        check_vma=False,
    )
```

time: 748 us -> 289 us (0.39)
  blocking collectives: 331 us -> 53.4 us
  waiting for transfers between devices: 269 us -> 128 us
  Pallas kernels: 0 us -> 48.1 us
  local copies, waits for them, and re-layouts: 50.1 us -> 6.64 us
  matrix products: 41.3 us -> 0 us
  other arithmetic: 22.9 us -> 3.94 us
  starting transfers between devices: 16.5 us -> 33.9 us
    reduce_scatter x1, waiting for transfers between devices: 220 us -> 0.01 us  [local(): lax.psum_scatter(dweight, 'voc', scatter_dimension=0, tiled=True)]
    psum x3 -> x0, blocking collectives: 118 us -> none  [the longest x1 74.7 us: local(): lax.psum((jnp.sum(jnp.exp(logits - row_max[:, None]), axis=1), mass_part,...]
    all_gather x1, blocking collectives: 118 us -> 18.5 us  [local(): all_done = lax.all_gather(done, 'voc', axis=0, tiled=False)]
    pmax x2 -> x0, blocking collectives: 94.6 us -> none  [the longest x1 79.6 us: local(): row_max = lax.pmax(local_top, ('ctx', 'voc'))]
    all_to_all x2 -> x4, waiting for transfers between devices: 48.8 us -> 126 us  [the longest x1 77.2 us: local(): arrived = lax.all_to_all(target, 'ctx', 0, 0, tiled=True)]
    pallas_call x0 -> x5, Pallas kernels: none -> 48.1 us  [the longest x1 18.1 us: local(): pl.pallas_call(grad_kernel, grid=(voc_count,), in_specs=[smem, whole((ctx...]
    dot_general x6 -> x0, matrix products: 41.3 us -> none  [the longest x1 10.2 us: local(): lax.dot_general(all_rows, grad_logits, (((0,), (0,)), ((), ())), preferre...]
    all_to_all x0 -> x1, blocking collectives: none -> 35 us  [local(): incoming = lax.all_to_all(outgoing, 'voc', 0, 0, tiled=True)]
  transfers between devices with their start and end apart: 4 -> 6, of which waited for: 2 -> 5; matrix products, arithmetic and copies ran while one was open for 11% -> 2% of each run, Pallas kernels for 0% -> 8%
where the time goes in v1:
time: 289 us; the launch traced here: 288 us
  waiting for transfers between devices  128 us (44%)
  blocking collectives  53.4 us (18%)
  Pallas kernels  48.1 us (17%)
  starting transfers between devices  33.9 us (12%)
  between operations  14.2 us (5%)
  local copies, waits for them, and re-layouts  6.64 us (2%)
  other arithmetic  3.94 us (1%)
    all_to_all x1, waiting for transfers between devices, local(): arrived = lax.all_to_all(target, 'ctx', 0, 0, tiled=True)  77.2 us
    all_to_all x1, blocking collectives, local(): incoming = lax.all_to_all(outgoing, 'voc', 0, 0, tiled=True)  35 us
    all_to_all x1, waiting for transfers between devices, local(): returned = lax.all_to_all(dhidden, 'ctx', 0, 0, tiled=True)  24.5 us
    all_gather x1, blocking collectives, local(): all_done = lax.all_gather(done, 'voc', axis=0, tiled=False)  18.5 us
    pallas_call x1, Pallas kernels, local(): pl.pallas_call(grad_kernel, grid=(voc_count,), in_specs=[smem, whole((ctx...  18.1 us
    all_to_all x1, waiting for transfers between devices, local(): lax.all_to_all(jnp.broadcast_to(mine[None], (ctx_count, part, width + LAN...  16.4 us
    pallas_call x1, Pallas kernels, local(): pl.pallas_call(logits_kernel, grid=(voc_count,), in_specs=[pl.BlockSpec((...  12 us
    all_to_all x1, starting transfers between devices, local(): lax.all_to_all(jnp.broadcast_to(mine[None], (ctx_count, part, width + LAN...  9.55 us
  transfers between devices with their start and end apart: 6, of which 5 were waited for; matrix products, arithmetic and copies ran while one was open for 2% of the time, Pallas kernels for 8%

profile of v1, /device:TPU:1, one launch (start us, length us, event | category | flops | bytes accessed | tf_op | source)
XLA Modules:
  0.0 287.9 jit_solution(16906883326853110706)
XLA Ops:
  7.2 0.0 all-gather.4.cloned.1.call-start
  7.2 7.5 %teacher_map.1 = bf16[8,65,16,128]{3,2,1,0:T(8,128)(2,1)} custom-call(bf16[128,8192]{1,0:T(8,128)(2,1)} %logits_ref.1, bf16[64,128,128]{2,1,0:T(8,128)(2,1)} %coeff_ref.1), custom_call_target="tpu_custom_call" | custom-call | flops 268435456 | bytes 6291456 | tf_op jit(solution)/shard_map/teacher_map/pallas_call | solution.py:251
  14.7 35.0 %all_to_all.25.in_ref = bf16[8,65,16,128]{3,2,1,0:T(8,128)(2,1)} all-to-all(bf16[8,65,16,128]{3,2,1,0:T(8,128)(2,1)} %teacher_map.1), channel_id=1, replica_groups=mesh['ctx'=32,'voc'=8] {'voc'}, dimensions={0} | all-to-all | bytes 4259840 | tf_op jit(solution)/shard_map/all_to_all | solution.py:262
  49.7 0.0 all-gather.4.cloned.1.call-update
  49.7 0.1 dynamic_slice.7
  49.8 0.1 broadcast_in_dim.7
  49.9 1.1 broadcast_in_dim.8
  51.0 9.6 %all-to-all-start = ((bf16[32,16,1024]{2,1,0:T(8,128)(2,1)}), bf16[32,16,1024]{2,1,0:T(8,128)(2,1)S(1)}, u32[]{:S(2)}, u32[]{:S(2)}) async-start(bf16[32,16,1024]{2,1,0:T(8,128)(2,1)} %broadcast_in_dim.8), calls=%async_computation | async-start | bytes 2097152 | tf_op jit(solution)/shard_map/all_to_all | solution.py:240
  60.6 8.4 %collect_targets.1 = (bf16[1024,16,128]{2,1,0:T(8,128)(2,1)}, f32[16,128]{1,0:T(8,128)}) custom-call(s32[512]{0:T(512)} %slot_ref.1, bf16[8,65,16,128]{3,2,1,0:T(8,128)(2,1)} %all_to_all.25.in_ref), custom_call_target="tpu_custom_call" | custom-call | flops 8388608 | bytes 6291456 | tf_op jit(solution)/shard_map/collect_targets/pallas_call | solution.py:267
  69.0 16.4 %all-to-all-done = bf16[32,16,1024]{2,1,0:T(8,128)(2,1)S(1)} async-done(((bf16[32,16,1024]{2,1,0:T(8,128)(2,1)}), bf16[32,16,1024]{2,1,0:T(8,128)(2,1)S(1)}, u32[]{:S(2)}, u32[]{:S(2)}) %all-to-all-start) | async-done | bytes 1048608 | tf_op jit(solution)/shard_map/all_to_all | solution.py:240
  85.4 8.6 %all-to-all-start.3 = ((bf16[32,32,16,128]{3,2,1,0:T(8,128)(2,1)}), bf16[32,32,16,128]{3,2,1,0:T(8,128)(2,1)}, u32[]{:S(2)}, u32[]{:S(2)}) async-start(bf16[32,32,16,128]{3,2,1,0:T(8,128)(2,1)} %bitcast.14), calls=%async_computation.3 | async-start | bytes 8388608 | tf_op jit(solution)/shard_map/all_to_all | solution.py:285
  93.9 1.6 gather_fusion
  95.5 2.0 all-gather.4.cloned.1.call-done
  97.5 12.0 %student_logits.1 = (f32[8,512,512]{2,1,0:T(8,128)}, f32[32,4,512]{2,1,0:T(4,128)}) custom-call(bf16[512,1024]{1,0:T(8,128)(2,1)} %bitcast.15, bf16[8,896,512]{2,1,0:T(8,128)(2,1)} %bitcast.24, f32[16,128]{1,0:T(8,128)} %get-tuple-element.14.mass_ref), custom_call_target="tpu_custom_call" | custom-call | flops 3758096384 | bytes 18874368 | tf_op jit(solution)/shard_map/student_logits/pallas_call | solution.py:287
  109.5 77.2 %all-to-all-done.3.target_ref = bf16[32,32,16,128]{3,2,1,0:T(8,128)(2,1)} async-done(((bf16[32,32,16,128]{3,2,1,0:T(8,128)(2,1)}), bf16[32,32,16,128]{3,2,1,0:T(8,128)(2,1)}, u32[]{:S(2)}, u32[]{:S(2)}) %all-to-all-start.3) | async-done | bytes 4194336 | tf_op jit(solution)/shard_map/all_to_all | solution.py:285
  186.7 9.4 %all-to-all-start.2 = ((f32[32,4,512]{2,1,0:T(4,128)}), f32[32,4,512]{2,1,0:T(4,128)S(1)}, u32[]{:S(2)}, u32[]{:S(2)}) async-start(f32[32,4,512]{2,1,0:T(4,128)} %get-tuple-element.15), calls=%async_computation.2 | async-start | bytes 524288 | tf_op jit(solution)/shard_map/all_to_all | solution.py:312
  196.0 0.0 reduce-scatter.2.cloned.1.call-start
  196.1 0.6 pad_add_fusion.place_ref
  196.7 0.1 slice.26
  196.8 1.3 copy.12
  198.1 7.6 %all-to-all-done.2.stats_ref = f32[32,4,512]{2,1,0:T(4,128)S(1)} async-done(((f32[32,4,512]{2,1,0:T(4,128)}), f32[32,4,512]{2,1,0:T(4,128)S(1)}, u32[]{:S(2)}, u32[]{:S(2)}) %all-to-all-start.2) | async-done | bytes 262176 | tf_op jit(solution)/shard_map/all_to_all | solution.py:312
  205.7 0.7 copy-done.3
  206.4 18.1 %grads.1 = (bf16[8,896,512]{2,1,0:T(8,128)(2,1)}, bf16[32,16,1024]{2,1,0:T(8,128)(2,1)}, f32[16,128]{1,0:T(8,128)}) custom-call(s32[33]{0:T(128)} %pad_add_fusion.place_ref, f32[32,4,512]{2,1,0:T(4,128)} %copy-done.3, f32[8,512,512]{2,1,0:T(8,128)} %get-tuple-element.16.logits_ref, bf16[32,32,16,128]{3,2,1,0:T(8,128)(2,1)} %all-to-all-done.3.target_ref, ...), custom_call_target="tpu_custom_call" | custom-call | flops 7516192768 | bytes 31457280 | tf_op jit(solution)/shard_map/grads/pallas_call | solution.py:314
  224.5 0.0 reduce-scatter.2.cloned.1.call-update
  224.6 6.4 %all-to-all-start.4 = ((bf16[32,16,1024]{2,1,0:T(8,128)(2,1)}), bf16[32,16,1024]{2,1,0:T(8,128)(2,1)S(1)}, u32[]{:S(2)}, u32[]{:S(2)}) async-start(bf16[32,16,1024]{2,1,0:T(8,128)(2,1)} %get-tuple-element.18), calls=%async_computation.4 | async-start | bytes 2097152 | tf_op jit(solution)/shard_map/all_to_all | solution.py:347
  231.0 24.5 %all-to-all-done.4.in_ref = bf16[32,16,1024]{2,1,0:T(8,128)(2,1)S(1)} async-done(((bf16[32,16,1024]{2,1,0:T(8,128)(2,1)}), bf16[32,16,1024]{2,1,0:T(8,128)(2,1)S(1)}, u32[]{:S(2)}, u32[]{:S(2)}) %all-to-all-start.4) | async-done | bytes 1048608 | tf_op jit(solution)/shard_map/all_to_all | solution.py:347
  255.5 1.0 copy-done.1
  256.4 2.1 finish_rows.1
  258.5 18.5 %all-gather.1 = bf16[128,1024]{1,0:T(8,128)(2,1)S(1)} all-gather(bf16[16,1024]{1,0:T(8,128)(2,1)} %finish_rows.1), channel_id=3, replica_groups=mesh['ctx'=32,'voc'=8] {'voc'}, dimensions={0}, use_global_device_ids=true | all-gather | bytes 294912 | tf_op jit(solution)/shard_map/all_gather | solution.py:354
  277.1 0.7 slice.29
  277.8 0.6 convert_reduce_fusion
  278.4 2.7 bitcast_convert_fusion
  (16 shorter events, 0.1 us)
Async XLA Ops:
  7.2 42.7 %copy-start = (bf16[128,896]{1,0:T(8,128)(2,1)S(1)}, bf16[128,896]{1,0:T(8,128)(2,1)}, u32[]{:S(2)}) copy-start(bf16[128,896]{1,0:T(8,128)(2,1)} %param.6) | copy-start | bytes 688132
  7.2 90.3 %all-gather.4.cloned.1.call-start = ((), (), s32[]{:S(2)}) async-start(), calls=%async_computation.7 | async-start | bytes 8257536 | tf_op jit(solution)/shard_map/all_gather | solution.py:265
  14.7 35.1 %copy-start.4 = (bf16[128]{0:T(256)(128)(2,1)S(1)}, bf16[128]{0:T(256)(128)(2,1)}, u32[]{:S(2)}) copy-start(bf16[128]{0:T(256)(128)(2,1)} %param.7) | copy-start | bytes 772
  51.0 34.3 %all-to-all-start = ((bf16[32,16,1024]{2,1,0:T(8,128)(2,1)}), bf16[32,16,1024]{2,1,0:T(8,128)(2,1)S(1)}, u32[]{:S(2)}, u32[]{:S(2)}) async-start(bf16[32,16,1024]{2,1,0:T(8,128)(2,1)} %broadcast_in_dim.8), calls=%async_computation | async-start | bytes 2097152 | tf_op jit(solution)/shard_map/all_to_all | solution.py:240
  85.4 101.3 %all-to-all-start.3 = ((bf16[32,32,16,128]{3,2,1,0:T(8,128)(2,1)}), bf16[32,32,16,128]{3,2,1,0:T(8,128)(2,1)}, u32[]{:S(2)}, u32[]{:S(2)}) async-start(bf16[32,32,16,128]{3,2,1,0:T(8,128)(2,1)} %bitcast.14), calls=%async_computation.3 | async-start | bytes 8388608 | tf_op jit(solution)/shard_map/all_to_all | solution.py:285
  97.5 99.2 %copy-start.2 = (bf16[32,16,1024]{2,1,0:T(8,128)(2,1)S(1)}, bf16[32,16,1024]{2,1,0:T(8,128)(2,1)}, u32[]{:S(2)}) copy-start(bf16[32,16,1024]{2,1,0:T(8,128)(2,1)} %gather_fusion) | copy-start | bytes 3145732
  186.7 19.0 %all-to-all-start.2 = ((f32[32,4,512]{2,1,0:T(4,128)}), f32[32,4,512]{2,1,0:T(4,128)S(1)}, u32[]{:S(2)}, u32[]{:S(2)}) async-start(f32[32,4,512]{2,1,0:T(4,128)} %get-tuple-element.15), calls=%async_computation.2 | async-start | bytes 524288 | tf_op jit(solution)/shard_map/all_to_all | solution.py:312
  196.0 82.4 %reduce-scatter.2.cloned.1.call-start = ((), (), s32[]{:S(2)}) async-start(), calls=%async_computation.6 | async-start | bytes 8257536 | tf_op jit(solution)/shard_map/reduce_scatter | solution.py:345
  205.7 0.7 copy-start.3
  224.6 30.9 %all-to-all-start.4 = ((bf16[32,16,1024]{2,1,0:T(8,128)(2,1)}), bf16[32,16,1024]{2,1,0:T(8,128)(2,1)S(1)}, u32[]{:S(2)}, u32[]{:S(2)}) async-start(bf16[32,16,1024]{2,1,0:T(8,128)(2,1)} %get-tuple-element.18), calls=%async_computation.4 | async-start | bytes 2097152 | tf_op jit(solution)/shard_map/all_to_all | solution.py:347
  255.5 1.0 copy-start.1
Sparse Core Ops, SparseCore 0:
  49.8 47.6 all-gather.3
  224.7 47.0 reduce-scatter.1

commit v2 on v1

--- a/solution.py
+++ b/solution.py
@@ -58,10 +58,11 @@
     out_ref[:, blocks] = tile.reshape(groups, part, LANES)
 
 
-def collect_kernel(slot_ref, in_ref, out_ref, mass_ref, sums, scales):
+def collect_kernel(slot_ref, in_ref, out_ref, sums, scales):
     voc_count, held, part, _ = in_ref.shape
     blocks = held - 1
-    slots = out_ref.shape[0]
+    ctx_count, owned = out_ref.shape[0], out_ref.shape[1] - 1
+    slots = ctx_count * owned
     tops, totals = [], []
     for v in range(voc_count):
         tile = in_ref[v, blocks].astype(F32)
@@ -89,16 +90,20 @@
 
         lax.fori_loop(0, blocks, add, 0, unroll=4)
 
-    def store(s, mass):
-        target = sums[s].astype(BF16)
-        out_ref[s] = target
-        return mass + target.astype(F32)
-
-    mass = lax.fori_loop(0, slots, store, jnp.zeros((part, LANES), F32), unroll=8)
-    mass_ref[...] = jnp.broadcast_to(jnp.sum(mass, axis=1, keepdims=True), (part, LANES))
-
-
-def logits_kernel(hidden_ref, weight_ref, mass_ref, logits_ref, stats_ref, tops, totals):
+    def store(c, mass):
+        for k in range(owned):
+            target = sums[c * owned + k].astype(BF16)
+            out_ref[c, k] = target
+            mass = mass + target.astype(F32)
+        return mass
+
+    mass = lax.fori_loop(0, ctx_count, store, jnp.zeros((part, LANES), F32))
+    tile = lanes_of(pieces(jnp.sum(mass, axis=1, keepdims=True)), part).astype(BF16)
+    for c in range(ctx_count):
+        out_ref[c, owned] = tile
+
+
+def logits_kernel(hidden_ref, weight_ref, logits_ref, stats_ref, tops, totals):
     step = pl.program_id(0)
     rows, cols = logits_ref.shape[1:]
 
@@ -123,16 +128,11 @@
         lane_top, lane_total = tops[...], totals[...]
         top = jnp.max(lane_top, axis=1, keepdims=True)
         total = jnp.sum(lane_total * jnp.exp(lane_top - top), axis=1, keepdims=True)
-        part = mass_ref.shape[0]
-        flat = jnp.transpose(lanes_of((top, total), rows))
-        mass = jnp.transpose(mass_ref[...])
-        mass = jnp.concatenate([mass[0:1], jnp.zeros((1, rows - part), F32)], axis=1)
-        packed = jnp.concatenate([flat[0:2], mass, jnp.zeros((1, rows), F32)], axis=0)
-        stats_ref[...] = jnp.broadcast_to(packed[None], stats_ref.shape)
+        stats_ref[...] = jnp.transpose(lanes_of((top, total), rows))[0 : stats_ref.shape[0]]
 
 
 def grad_kernel(
-    place_ref, stats_ref, logits_ref, target_ref, hidden_ref, hidden_t_ref, weight_ref,
+    place_ref, stats_ref, mass_ref, logits_ref, target_ref, hidden_ref, hidden_t_ref, weight_ref,
     dweight_ref, dhidden_ref, base_ref, norm, mass, gain, cross, partial,
 ):
     step = pl.program_id(0)
@@ -142,18 +142,10 @@
 
     @pl.when(step == 0)
     def _():
-        tops = stats_ref[:, 0, :]
-        top = jnp.max(tops, axis=0, keepdims=True)
-        total = jnp.sum(stats_ref[:, 1, :] * jnp.exp(tops - top), axis=0, keepdims=True)
-        norm_row = jnp.broadcast_to(top + jnp.log(total), (LANES, rows))
-        norm[...] = jnp.transpose(norm_row)
-        own = stats_ref[:, 2, 0:LANES]
-        spread = jnp.broadcast_to(own[:, None, :], (count, part, LANES))
-        diagonal = lax.broadcasted_iota(jnp.int32, (count, part, LANES), 1) == lax.broadcasted_iota(
-            jnp.int32, (count, part, LANES), 2
-        )
-        column = jnp.sum(jnp.where(diagonal, spread, 0.0), axis=2, keepdims=True).reshape(rows, 1)
-        mass[...] = jnp.broadcast_to(column, (rows, LANES))
+        top, total = stats_ref[0:1], stats_ref[1:2]
+        norm[...] = jnp.transpose(jnp.broadcast_to(top + jnp.log(total), (LANES, rows)))
+        sent = mass_ref[...].reshape(rows, LANES).astype(F32)
+        mass[...] = jnp.broadcast_to(sent[:, 0:1] + sent[:, 1:2] + sent[:, 2:3], (rows, LANES))
         gain[...] = jnp.broadcast_to(
             hidden_ref[:, width : width + LANES].astype(F32)[:, 0:1], (rows, LANES)
         )
@@ -197,21 +189,56 @@
         base_ref[...] = mass[pl.ds(start, part), :]
 
 
-def finish_kernel(in_ref, base_ref, out_ref):
-    count, part, wide = in_ref.shape
-    width = wide - LANES
-    total = jnp.zeros((part, wide), F32)
-    for c in range(count):
-        total = total + in_ref[c].astype(F32)
-    out_ref[:, 0:width] = total[:, 0:width].astype(BF16)
-    tail = total[:, width:wide]
-    crossed = tail[:, 0:1] + tail[:, 1:2] + tail[:, 2:3]
-    loss = base_ref[...][:, 0:1] - crossed
-    out_ref[:, width:wide] = lanes_of(pieces(loss), part).astype(BF16)
+def fold(refs):
+    wide = refs[0].shape[-1]
+    total = refs[0][...].astype(F32)
+    for ref in refs[1:]:
+        total = total + ref[...].astype(F32)
+    tail = total[:, wide - LANES :]
+    return total[:, : wide - LANES], tail[:, 0:1] + tail[:, 1:2] + tail[:, 2:3]
+
+
+def fold_kernel(*refs):
+    out_ref = refs[-1]
+    rows, wide = out_ref.shape
+    total, crossed = fold(refs[:-1])
+    out_ref[:, 0 : wide - LANES] = total.astype(BF16)
+    out_ref[:, wide - LANES : wide] = lanes_of(pieces(crossed), rows).astype(BF16)
+
+
+def finish_kernel(*refs):
+    base_ref, out_ref = refs[-2:]
+    rows, wide = out_ref.shape
+    total, crossed = fold(refs[:-2])
+    out_ref[:, 0 : wide - LANES] = total.astype(BF16)
+    loss = base_ref[:, 0:1] - crossed
+    out_ref[:, wide - LANES : wide] = lanes_of(pieces(loss), rows).astype(BF16)
 
 
 def whole(shape):
     return pl.BlockSpec(shape, lambda *_: (0,) * len(shape))
+
+
+def shifted(value, ring, along_x, step):
+    count = lax.axis_size("ctx")
+    lines = count // ring
+    pairs = []
+    for x in range(lines):
+        for z in range(ring):
+            to = (x + step) % lines * ring + z if along_x else x * ring + (z + step) % ring
+            pairs.append((x * ring + z, to))
+    return lax.ppermute(value, "ctx", pairs)
+
+
+def spread(value, ring, along_x):
+    count = lax.axis_size("ctx") // ring if along_x else ring
+    return [value] + [shifted(value, ring, along_x, step) for step in range(1, count)]
+
+
+def merged(stats):
+    top = functools.reduce(jnp.maximum, [part[0:1] for part in stats])
+    total = functools.reduce(jnp.add, [part[1:2] * jnp.exp(part[0:1] - top) for part in stats])
+    return jnp.concatenate([top, total], axis=0)
 
 
 def local(hidden, token_weight, head_weight, teacher_logits, block_coeff, block_map):
@@ -232,20 +259,22 @@
     smem = pl.BlockSpec(memory_space=pltpu.SMEM)
 
     parity = voc_index // half_groups
-    fold = jnp.where(ctx_index % 2 == parity, 0, 1)
-    start = fold * half_rows + voc_index % half_groups * part
+    fold_side = jnp.where(ctx_index % 2 == parity, 0, 1)
+    start = fold_side * half_rows + voc_index % half_groups * part
     mine = lax.dynamic_slice_in_dim(hidden, start, part, 0)
     mine_weight = lax.dynamic_slice_in_dim(token_weight, start, part, 0)
     mine = jnp.concatenate([mine, jnp.broadcast_to(mine_weight[:, None], (part, LANES))], axis=1)
-    by_ctx = lax.all_to_all(
-        jnp.broadcast_to(mine[None], (ctx_count, part, width + LANES)), "ctx", 0, 0, tiled=True
-    )
+    ring = min(8, ctx_count)
+    near = jnp.stack(spread(mine, ring, False))
+    by_ctx = jnp.concatenate(spread(near, ring, True), axis=0)
     source = jnp.arange(ctx_count, dtype=jnp.int32)
     half_block = 2 * source + parity
     place = jnp.where(half_block < ctx_count, half_block, 2 * ctx_count - 1 - half_block)
-    own_half = jnp.where(fold == 0, ctx_index, 2 * ctx_count - 1 - ctx_index)
-    place = jnp.concatenate([place, (own_half // 2)[None]]).astype(jnp.int32)
-    hidden_rows = by_ctx[place[:ctx_count]].reshape(rows, width + LANES)
+    own_half = jnp.where(fold_side == 0, ctx_index, 2 * ctx_count - 1 - ctx_index)
+    behind = (ctx_index // ring - place // ring) % (ctx_count // ring) * ring + (ctx_index - place) % ring
+    ahead = (place // ring - ctx_index // ring) % (ctx_count // ring) * ring + (place - ctx_index) % ring
+    place = jnp.concatenate([ahead, (own_half // 2)[None]]).astype(jnp.int32)
+    hidden_rows = by_ctx[behind].reshape(rows, width + LANES)
     hidden_t = hidden_rows[:, :width].T
 
     outgoing = pl.pallas_call(
@@ -264,12 +293,9 @@
     head_weight, incoming = lax.optimization_barrier((head_weight, incoming))
     weights = lax.all_gather(head_weight, "voc", axis=0, tiled=False)
 
-    target, mass = pl.pallas_call(
+    target = pl.pallas_call(
         collect_kernel,
-        out_shape=(
-            jax.ShapeDtypeStruct((slots, part, LANES), BF16),
-            jax.ShapeDtypeStruct((part, LANES), F32),
-        ),
+        out_shape=jax.ShapeDtypeStruct((ctx_count, owned_blocks + 1, part, LANES), BF16),
         in_specs=[smem, pl.BlockSpec(memory_space=pltpu.VMEM)],
         scratch_shapes=[
             pltpu.VMEM((slots, part, LANES), F32),
@@ -281,7 +307,6 @@
         ),
         name="collect_targets",
     )(block_map, incoming)
-    target = target.reshape(ctx_count, owned_blocks, part, LANES)
     arrived = lax.all_to_all(target, "ctx", 0, 0, tiled=True)
 
     logits, stats = pl.pallas_call(
@@ -290,15 +315,14 @@
         in_specs=[
             pl.BlockSpec((rows, width), lambda j: (0, 0)),
             pl.BlockSpec((1, width, cols), lambda j: (j, 0, 0)),
-            whole((part, LANES)),
         ],
         out_specs=(
             pl.BlockSpec((1, rows, cols), lambda j: (j, 0, 0)),
-            whole((ctx_count, 4, rows)),
+            whole((8, rows)),
         ),
         out_shape=(
             jax.ShapeDtypeStruct((voc_count, rows, cols), F32),
-            jax.ShapeDtypeStruct((ctx_count, 4, rows), F32),
+            jax.ShapeDtypeStruct((8, rows), F32),
         ),
         scratch_shapes=[pltpu.VMEM((rows, LANES), F32)] * 2,
         compiler_params=params(),
@@ -308,15 +332,17 @@
             transcendentals=rows * cols * voc_count,
         ),
         name="student_logits",
-    )(hidden_rows, weights, mass)
-    all_stats = lax.all_to_all(stats, "ctx", 0, 0, tiled=True)
+    )(hidden_rows, weights)
+    stats = merged(spread(stats, ring, False))
+    stats = merged(spread(stats, ring, True))
 
     dweight, dhidden, base = pl.pallas_call(
         grad_kernel,
         grid=(voc_count,),
         in_specs=[
             smem,
-            whole((ctx_count, 4, rows)),
+            whole((2, rows)),
+            pl.BlockSpec((ctx_count, 1, part, LANES), lambda j: (0, owned_blocks, 0, 0)),
             pl.BlockSpec((1, rows, cols), lambda j: (j, 0, 0)),
             pl.BlockSpec((ctx_count, dev_blocks, part, LANES), lambda j: (0, j, 0, 0)),
             whole((rows, width + LANES)),
@@ -341,16 +367,27 @@
             transcendentals=rows * cols * voc_count,
         ),
         name="grads",
-    )(place, all_stats, logits, arrived, hidden_rows, hidden_t, weights)
+    )(place, stats, arrived, logits, arrived, hidden_rows, hidden_t, weights)
     grad_weight = lax.psum_scatter(dweight, "voc", scatter_dimension=0, tiled=True)
     grad_weight = grad_weight.reshape(width, cols).astype(F32)
-    returned = lax.all_to_all(dhidden, "ctx", 0, 0, tiled=True)
+    wide = width + LANES
+    pieces_x = dhidden.reshape(ctx_count // ring, ring * part, wide)
+    parts = [pieces_x[0]]
+    parts += [shifted(pieces_x[e], ring, True, e) for e in range(1, ctx_count // ring)]
+    folded = pl.pallas_call(
+        fold_kernel,
+        out_shape=jax.ShapeDtypeStruct((ring * part, wide), BF16),
+        compiler_params=params(),
+        name="fold_rows",
+    )(*parts)
+    pieces_z = folded.reshape(ring, part, wide)
+    parts = [pieces_z[0]] + [shifted(pieces_z[e], ring, False, e) for e in range(1, ring)]
     done = pl.pallas_call(
         finish_kernel,
-        out_shape=jax.ShapeDtypeStruct((part, width + LANES), BF16),
+        out_shape=jax.ShapeDtypeStruct((part, wide), BF16),
         compiler_params=params(),
         name="finish_rows",
-    )(returned, base)
+    )(*parts, base)
     all_done = lax.all_gather(done, "voc", axis=0, tiled=False)
     all_done = jnp.where(ctx_index % 2 == 0, all_done, jnp.roll(all_done, half_groups, axis=0))
     all_done = all_done.reshape(rows_dev, width + LANES)

time: 289 us -> 314 us (1.087)
  starting transfers between devices: 33.9 us -> 64.5 us
  waiting for transfers between devices: 128 us -> 114 us
  blocking collectives: 53.4 us -> 56.7 us
    ppermute x0 -> x30, waiting for transfers between devices: none -> 114 us  [shifted(): return lax.ppermute(value, 'ctx', pairs)]
    all_to_all x1, waiting for transfers between devices: 77.2 us -> 0.01 us  [local(): arrived = lax.all_to_all(target, 'ctx', 0, 0, tiled=True)]
    ppermute x0 -> x30, starting transfers between devices: none -> 54.7 us  [shifted(): return lax.ppermute(value, 'ctx', pairs)]
    all_to_all x3 -> x0, waiting for transfers between devices: 48.5 us -> none  [the longest x1 24.5 us: local(): returned = lax.all_to_all(dhidden, 'ctx', 0, 0, tiled=True)]
    all_to_all x3 -> x0, starting transfers between devices: 25.3 us -> none  [the longest x1 9.55 us: local(): lax.all_to_all(jnp.broadcast_to(mine[None], (ctx_count, part, width + LAN...]
    all_gather x1, blocking collectives: 18.5 us -> 21.9 us  [local(): all_done = lax.all_gather(done, 'voc', axis=0, tiled=False)]
    pallas_call x3 -> x4, Pallas kernels: 28.6 us -> 29.8 us  [the longest x1 18.1 us: local(): pl.pallas_call(grad_kernel, grid=(voc_count,), in_specs=[smem, whole((2,...]
  transfers between devices with their start and end apart: 6 -> 33, of which waited for: 5 -> 17; matrix products, arithmetic and copies ran while one was open for 2% -> 3% of each run, Pallas kernels for 8% -> 8%
where the time goes in v2:
time: 314 us; the launch traced here: 313 us
  waiting for transfers between devices  114 us (36%)
  starting transfers between devices  64.5 us (21%)
  blocking collectives  56.7 us (18%)
  Pallas kernels  49.2 us (16%)
  between operations  14.3 us (5%)
  local copies, waits for them, and re-layouts  8.73 us (3%)
  other arithmetic  5.47 us (2%)
    ppermute x30, waiting for transfers between devices, shifted(): return lax.ppermute(value, 'ctx', pairs)  114 us
    ppermute x30, starting transfers between devices, shifted(): return lax.ppermute(value, 'ctx', pairs)  54.7 us
    all_to_all x1, blocking collectives, local(): incoming = lax.all_to_all(outgoing, 'voc', 0, 0, tiled=True)  34.9 us
    all_gather x1, blocking collectives, local(): all_done = lax.all_gather(done, 'voc', axis=0, tiled=False)  21.9 us
    pallas_call x1, Pallas kernels, local(): pl.pallas_call(grad_kernel, grid=(voc_count,), in_specs=[smem, whole((2,...  18.1 us
    pallas_call x1, Pallas kernels, local(): pl.pallas_call(logits_kernel, grid=(voc_count,), in_specs=[pl.BlockSpec((...  11.8 us
    all_to_all x1, starting transfers between devices, local(): arrived = lax.all_to_all(target, 'ctx', 0, 0, tiled=True)  9.79 us
    pallas_call x1, Pallas kernels, local(): pl.pallas_call(collect_kernel, out_shape=jax.ShapeDtypeStruct((ctx_count,...  7.85 us
  transfers between devices with their start and end apart: 33, of which 17 were waited for; matrix products, arithmetic and copies ran while one was open for 3% of the time, Pallas kernels for 8%

profile of v2, /device:TPU:1, one launch (start us, length us, event | category | flops | bytes accessed | tf_op | source)
XLA Modules:
  0.0 312.9 jit_solution(4371956790455024741)
XLA Ops:
  7.2 7.5 %teacher_map.1 = bf16[8,65,16,128]{3,2,1,0:T(8,128)(2,1)} custom-call(bf16[128,8192]{1,0:T(8,128)(2,1)} %logits_ref.1, bf16[64,128,128]{2,1,0:T(8,128)(2,1)} %coeff_ref.1), custom_call_target="tpu_custom_call" | custom-call | flops 268435456 | bytes 6291456 | tf_op jit(solution)/shard_map/teacher_map/pallas_call | solution.py:280
  14.7 34.9 %all_to_all.10.in_ref = bf16[8,65,16,128]{3,2,1,0:T(8,128)(2,1)} all-to-all(bf16[8,65,16,128]{3,2,1,0:T(8,128)(2,1)} %teacher_map.1), channel_id=1, replica_groups=mesh['ctx'=32,'voc'=8] {'voc'}, dimensions={0} | all-to-all | bytes 4259840 | tf_op jit(solution)/shard_map/all_to_all | solution.py:291
  49.6 7.9 %collect_targets.1 = bf16[32,33,16,128]{3,2,1,0:T(8,128)(2,1)} custom-call(s32[512]{0:T(512)} %slot_ref.1, bf16[8,65,16,128]{3,2,1,0:T(8,128)(2,1)} %all_to_all.10.in_ref), custom_call_target="tpu_custom_call" | custom-call | flops 8388608 | bytes 6291456 | tf_op jit(solution)/shard_map/collect_targets/pallas_call | solution.py:296
  57.5 9.8 %all-to-all-start.1 = ((bf16[32,33,16,128]{3,2,1,0:T(8,128)(2,1)}), bf16[32,33,16,128]{3,2,1,0:T(8,128)(2,1)}, u32[]{:S(2)}, u32[]{:S(2)}) async-start(bf16[32,33,16,128]{3,2,1,0:T(8,128)(2,1)} %collect_targets.1), calls=%async_computation.1 | async-start | bytes 8650752 | tf_op jit(solution)/shard_map/all_to_all | solution.py:310
  67.5 3.3 %collective-permute-start.5 = (bf16[16,1024]{1,0:T(8,128)(2,1)S(1)}, bf16[16,1024]{1,0:T(8,128)(2,1)S(1)}, u32[]{:S(2)}, u32[]{:S(2)}) collective-permute-start(bf16[16,1024]{1,0:T(8,128)(2,1)S(1)} %pad_maximum_fusion), channel_id=1, source_target_pairs={{0,48},{8,56},{16,0},{24,8},{32,16},{40,24},{48,32},{56,40},{64,11... | collective-permute-start | bytes 98312 | tf_op jit(solution)/shard_map/ppermute | solution.py:230
  70.8 2.1 collective-permute-start.4
  72.9 2.4 collective-permute-start.3
  76.2 2.4 collective-permute-start
  78.6 85.7 %collective-permute-done = bf16[16,1024]{1,0:T(8,128)(2,1)S(1)} collective-permute-done((bf16[16,1024]{1,0:T(8,128)(2,1)S(1)}, bf16[16,1024]{1,0:T(8,128)(2,1)S(1)}, u32[]{:S(2)}, u32[]{:S(2)}) %collective-permute-start) | collective-permute-done | bytes 32800 | tf_op jit(solution)/shard_map/ppermute | solution.py:230
  164.3 2.1 collective-permute-start.1
  166.4 2.7 collective-permute-done.1
  169.2 4.4 %collective-permute-start.6 = (bf16[16,1024]{1,0:T(8,128)(2,1)S(1)}, bf16[16,1024]{1,0:T(8,128)(2,1)S(1)}, u32[]{:S(2)}, u32[]{:S(2)}) collective-permute-start(bf16[16,1024]{1,0:T(8,128)(2,1)S(1)} %pad_maximum_fusion), channel_id=1, source_target_pairs={{0,56},{8,0},{16,8},{24,16},{32,24},{40,32},{48,40},{56,48},{64,12... | collective-permute-start | bytes 98312 | tf_op jit(solution)/shard_map/ppermute | solution.py:230
  174.9 2.7 collective-permute-start.8
  177.6 2.0 collective-permute-start.9
  181.1 4.4 %collective-permute-done.8 = bf16[8,16,1024]{2,1,0:T(8,128)(2,1)S(1)} collective-permute-done((bf16[8,16,1024]{2,1,0:T(8,128)(2,1)S(1)}, bf16[8,16,1024]{2,1,0:T(8,128)(2,1)S(1)}, u32[]{:S(2)}, u32[]{:S(2)}) %collective-permute-start.8) | collective-permute-done | bytes 262176 | tf_op jit(solution)/shard_map/ppermute | solution.py:230
  188.2 11.8 %student_logits.1 = (f32[8,512,512]{2,1,0:T(8,128)}, f32[8,512]{1,0:T(8,128)}) custom-call(bf16[512,1024]{1,0:T(8,128)(2,1)} %bitcast.41, bf16[8,896,512]{2,1,0:T(8,128)(2,1)} %bitcast.54), custom_call_target="tpu_custom_call" | custom-call | flops 3758096384 | bytes 18874368 | tf_op jit(solution)/shard_map/student_logits/pallas_call | solution.py:312
  200.0 3.9 %collective-permute-start.16 = (f32[8,512]{1,0:T(8,128)}, f32[8,512]{1,0:T(8,128)S(1)}, u32[]{:S(2)}, u32[]{:S(2)}) collective-permute-start(f32[8,512]{1,0:T(8,128)} %get-tuple-element.11), channel_id=1, source_target_pairs={{0,56},{8,0},{16,8},{24,16},{32,24},{40,32},{48,40},{56,48},{64,12... | collective-permute-start | bytes 49160 | tf_op jit(solution)/shard_map/ppermute | solution.py:230
  203.9 2.6 collective-permute-start.15
  207.2 3.6 %collective-permute-start.13 = (f32[8,512]{1,0:T(8,128)}, f32[8,512]{1,0:T(8,128)S(1)}, u32[]{:S(2)}, u32[]{:S(2)}) collective-permute-start(f32[8,512]{1,0:T(8,128)} %get-tuple-element.11), channel_id=1, source_target_pairs={{0,32},{8,40},{16,48},{24,56},{32,0},{40,8},{48,16},{56,24},{64,96... | collective-permute-start | bytes 49160 | tf_op jit(solution)/shard_map/ppermute | solution.py:230
  210.8 3.2 %collective-permute-start.11 = (f32[8,512]{1,0:T(8,128)}, f32[8,512]{1,0:T(8,128)S(1)}, u32[]{:S(2)}, u32[]{:S(2)}) collective-permute-start(f32[8,512]{1,0:T(8,128)} %get-tuple-element.11), channel_id=1, source_target_pairs={{0,16},{8,24},{16,32},{24,40},{32,48},{40,56},{48,0},{56,8},{64,80... | collective-permute-start | bytes 49160 | tf_op jit(solution)/shard_map/ppermute | solution.py:230
  214.7 2.1 collective-permute-done.12
  219.5 3.0 collective-permute-start.19
  228.5 18.1 %grads.1 = (bf16[8,896,512]{2,1,0:T(8,128)(2,1)}, bf16[32,16,1024]{2,1,0:T(8,128)(2,1)}, f32[16,128]{1,0:T(8,128)}) custom-call(s32[33]{0:T(128)} %pad_add_fusion.place_ref, f32[2,512]{1,0:T(2,128)} %pad_maximum_fusion.2.stats_ref, bf16[32,33,16,128]{3,2,1,0:T(8,128)(2,1)} %all-to-all-done.1.mass_ref.target_ref, ...), custom_call_target="tpu_custom_call" | custom-call | flops 7516192768 | bytes 31457280 | tf_op jit(solution)/shard_map/grads/pallas_call | solution.py:339
  250.4 5.1 %collective-permute-done.21.refs_2_ = bf16[128,1024]{1,0:T(8,128)(2,1)S(1)} collective-permute-done((bf16[128,1024]{1,0:T(8,128)(2,1)S(1)}, bf16[128,1024]{1,0:T(8,128)(2,1)S(1)}, u32[]{:S(2)}, u32[]{:S(2)}) %collective-permute-start.21) | collective-permute-done | bytes 262176 | tf_op jit(solution)/shard_map/ppermute | solution.py:230
  258.9 2.2 fold_rows.1
  262.7 2.2 collective-permute-start.28
  264.9 2.2 collective-permute-start.27
  268.4 2.6 collective-permute-start.25
  271.0 2.5 collective-permute-start.24
  275.9 2.0 collective-permute-done.23.refs_1_
  280.1 21.9 %all-gather.1 = bf16[128,1024]{1,0:T(8,128)(2,1)S(1)} all-gather(bf16[16,1024]{1,0:T(8,128)(2,1)} %finish_rows.1), channel_id=3, replica_groups=mesh['ctx'=32,'voc'=8] {'voc'}, dimensions={0}, use_global_device_ids=true | all-gather | bytes 294912 | tf_op jit(solution)/shard_map/all_gather | solution.py:391
  303.4 2.7 bitcast_convert_fusion
  (105 shorter events, 32.5 us)
Async XLA Ops:
  7.2 181.0 %all-gather.4.cloned.1.call-start = ((), (), s32[]{:S(2)}) async-start(), calls=%async_computation.4 | async-start | bytes 8257536 | tf_op jit(solution)/shard_map/all_gather | solution.py:294
  57.5 171.0 %all-to-all-start.1 = ((bf16[32,33,16,128]{3,2,1,0:T(8,128)(2,1)}), bf16[32,33,16,128]{3,2,1,0:T(8,128)(2,1)}, u32[]{:S(2)}, u32[]{:S(2)}) async-start(bf16[32,33,16,128]{3,2,1,0:T(8,128)(2,1)} %collect_targets.1), calls=%async_computation.1 | async-start | bytes 8650752 | tf_op jit(solution)/shard_map/all_to_all | solution.py:310
  67.3 236.2 %reduce-scatter.2.cloned.1.call-start = ((), (), s32[]{:S(2)}) async-start(), calls=%async_computation.3 | async-start | bytes 8257536 | tf_op jit(solution)/shard_map/reduce_scatter | solution.py:371
  67.5 106.2 %collective-permute-start.5 = (bf16[16,1024]{1,0:T(8,128)(2,1)S(1)}, bf16[16,1024]{1,0:T(8,128)(2,1)S(1)}, u32[]{:S(2)}, u32[]{:S(2)}) collective-permute-start(bf16[16,1024]{1,0:T(8,128)(2,1)S(1)} %pad_maximum_fusion), channel_id=1, source_target_pairs={{0,48},{8,56},{16,0},{24,8},{32,16},{40,24},{48,32},{56,40},{64,11... | collective-permute-start | bytes 98312 | tf_op jit(solution)/shard_map/ppermute | solution.py:230
  70.8 102.8 %collective-permute-start.4 = (bf16[16,1024]{1,0:T(8,128)(2,1)S(1)}, bf16[16,1024]{1,0:T(8,128)(2,1)S(1)}, u32[]{:S(2)}, u32[]{:S(2)}) collective-permute-start(bf16[16,1024]{1,0:T(8,128)(2,1)S(1)} %pad_maximum_fusion), channel_id=1, source_target_pairs={{0,40},{8,48},{16,56},{24,0},{32,8},{40,16},{48,24},{56,32},{64,10... | collective-permute-start | bytes 98312 | tf_op jit(solution)/shard_map/ppermute | solution.py:230
  72.9 100.7 %collective-permute-start.3 = (bf16[16,1024]{1,0:T(8,128)(2,1)S(1)}, bf16[16,1024]{1,0:T(8,128)(2,1)S(1)}, u32[]{:S(2)}, u32[]{:S(2)}) collective-permute-start(bf16[16,1024]{1,0:T(8,128)(2,1)S(1)} %pad_maximum_fusion), channel_id=1, source_target_pairs={{0,32},{8,40},{16,48},{24,56},{32,0},{40,8},{48,16},{56,24},{64,96... | collective-permute-start | bytes 98312 | tf_op jit(solution)/shard_map/ppermute | solution.py:230
  75.3 98.3 %collective-permute-start.2 = (bf16[16,1024]{1,0:T(8,128)(2,1)S(1)}, bf16[16,1024]{1,0:T(8,128)(2,1)S(1)}, u32[]{:S(2)}, u32[]{:S(2)}) collective-permute-start(bf16[16,1024]{1,0:T(8,128)(2,1)S(1)} %pad_maximum_fusion), channel_id=1, source_target_pairs={{0,24},{8,32},{16,40},{24,48},{32,56},{40,0},{48,8},{56,16},{64,88... | collective-permute-start | bytes 98312 | tf_op jit(solution)/shard_map/ppermute | solution.py:230
  76.2 88.1 %collective-permute-start = (bf16[16,1024]{1,0:T(8,128)(2,1)S(1)}, bf16[16,1024]{1,0:T(8,128)(2,1)S(1)}, u32[]{:S(2)}, u32[]{:S(2)}) collective-permute-start(bf16[16,1024]{1,0:T(8,128)(2,1)S(1)} %pad_maximum_fusion), channel_id=1, source_target_pairs={{0,8},{8,16},{16,24},{24,32},{32,40},{40,48},{48,56},{56,0},{64,72... | collective-permute-start | bytes 98312 | tf_op jit(solution)/shard_map/ppermute | solution.py:230
  164.3 4.9 %collective-permute-start.1 = (bf16[16,1024]{1,0:T(8,128)(2,1)S(1)}, bf16[16,1024]{1,0:T(8,128)(2,1)S(1)}, u32[]{:S(2)}, u32[]{:S(2)}) collective-permute-start(bf16[16,1024]{1,0:T(8,128)(2,1)S(1)} %pad_maximum_fusion), channel_id=1, source_target_pairs={{0,16},{8,24},{16,32},{24,40},{32,48},{40,56},{48,0},{56,8},{64,80... | collective-permute-start | bytes 98312 | tf_op jit(solution)/shard_map/ppermute | solution.py:230
  169.2 5.5 %collective-permute-start.6 = (bf16[16,1024]{1,0:T(8,128)(2,1)S(1)}, bf16[16,1024]{1,0:T(8,128)(2,1)S(1)}, u32[]{:S(2)}, u32[]{:S(2)}) collective-permute-start(bf16[16,1024]{1,0:T(8,128)(2,1)S(1)} %pad_maximum_fusion), channel_id=1, source_target_pairs={{0,56},{8,0},{16,8},{24,16},{32,24},{40,32},{48,40},{56,48},{64,12... | collective-permute-start | bytes 98312 | tf_op jit(solution)/shard_map/ppermute | solution.py:230
  174.7 6.4 %collective-permute-start.7 = (bf16[8,16,1024]{2,1,0:T(8,128)(2,1)S(1)}, bf16[8,16,1024]{2,1,0:T(8,128)(2,1)S(1)}, u32[]{:S(2)}, u32[]{:S(2)}) collective-permute-start(bf16[8,16,1024]{2,1,0:T(8,128)(2,1)S(1)} %get-tuple-element.35), channel_id=1, source_target_pairs={{0,64},{8,72},{16,80},{24,88},{32,96},{40,104},{48,112},{56,120},{... | collective-permute-start | bytes 786440 | tf_op jit(solution)/shard_map/ppermute | solution.py:230
  174.9 10.6 %collective-permute-start.8 = (bf16[8,16,1024]{2,1,0:T(8,128)(2,1)S(1)}, bf16[8,16,1024]{2,1,0:T(8,128)(2,1)S(1)}, u32[]{:S(2)}, u32[]{:S(2)}) collective-permute-start(bf16[8,16,1024]{2,1,0:T(8,128)(2,1)S(1)} %get-tuple-element.35), channel_id=1, source_target_pairs={{0,128},{8,136},{16,144},{24,152},{32,160},{40,168},{48,176},{56,1... | collective-permute-start | bytes 786440 | tf_op jit(solution)/shard_map/ppermute | solution.py:230
  177.6 8.9 %collective-permute-start.9 = (bf16[8,16,1024]{2,1,0:T(8,128)(2,1)S(1)}, bf16[8,16,1024]{2,1,0:T(8,128)(2,1)S(1)}, u32[]{:S(2)}, u32[]{:S(2)}) collective-permute-start(bf16[8,16,1024]{2,1,0:T(8,128)(2,1)S(1)} %get-tuple-element.35), channel_id=1, source_target_pairs={{0,192},{8,200},{16,208},{24,216},{32,224},{40,232},{48,240},{56,2... | collective-permute-start | bytes 786440 | tf_op jit(solution)/shard_map/ppermute | solution.py:230
  200.0 10.7 %collective-permute-start.16 = (f32[8,512]{1,0:T(8,128)}, f32[8,512]{1,0:T(8,128)S(1)}, u32[]{:S(2)}, u32[]{:S(2)}) collective-permute-start(f32[8,512]{1,0:T(8,128)} %get-tuple-element.11), channel_id=1, source_target_pairs={{0,56},{8,0},{16,8},{24,16},{32,24},{40,32},{48,40},{56,48},{64,12... | collective-permute-start | bytes 49160 | tf_op jit(solution)/shard_map/ppermute | solution.py:230
  203.9 10.1 %collective-permute-start.15 = (f32[8,512]{1,0:T(8,128)}, f32[8,512]{1,0:T(8,128)S(1)}, u32[]{:S(2)}, u32[]{:S(2)}) collective-permute-start(f32[8,512]{1,0:T(8,128)} %get-tuple-element.11), channel_id=1, source_target_pairs={{0,48},{8,56},{16,0},{24,8},{32,16},{40,24},{48,32},{56,40},{64,11... | collective-permute-start | bytes 49160 | tf_op jit(solution)/shard_map/ppermute | solution.py:230
  206.6 8.1 %collective-permute-start.14 = (f32[8,512]{1,0:T(8,128)}, f32[8,512]{1,0:T(8,128)S(1)}, u32[]{:S(2)}, u32[]{:S(2)}) collective-permute-start(f32[8,512]{1,0:T(8,128)} %get-tuple-element.11), channel_id=1, source_target_pairs={{0,40},{8,48},{16,56},{24,0},{32,8},{40,16},{48,24},{56,32},{64,10... | collective-permute-start | bytes 49160 | tf_op jit(solution)/shard_map/ppermute | solution.py:230
  207.2 7.5 %collective-permute-start.13 = (f32[8,512]{1,0:T(8,128)}, f32[8,512]{1,0:T(8,128)S(1)}, u32[]{:S(2)}, u32[]{:S(2)}) collective-permute-start(f32[8,512]{1,0:T(8,128)} %get-tuple-element.11), channel_id=1, source_target_pairs={{0,32},{8,40},{16,48},{24,56},{32,0},{40,8},{48,16},{56,24},{64,96... | collective-permute-start | bytes 49160 | tf_op jit(solution)/shard_map/ppermute | solution.py:230
  210.8 6.0 %collective-permute-start.12 = (f32[8,512]{1,0:T(8,128)}, f32[8,512]{1,0:T(8,128)S(1)}, u32[]{:S(2)}, u32[]{:S(2)}) collective-permute-start(f32[8,512]{1,0:T(8,128)} %get-tuple-element.11), channel_id=1, source_target_pairs={{0,24},{8,32},{16,40},{24,48},{32,56},{40,0},{48,8},{56,16},{64,88... | collective-permute-start | bytes 49160 | tf_op jit(solution)/shard_map/ppermute | solution.py:230
  210.8 6.0 %collective-permute-start.11 = (f32[8,512]{1,0:T(8,128)}, f32[8,512]{1,0:T(8,128)S(1)}, u32[]{:S(2)}, u32[]{:S(2)}) collective-permute-start(f32[8,512]{1,0:T(8,128)} %get-tuple-element.11), channel_id=1, source_target_pairs={{0,16},{8,24},{16,32},{24,40},{32,48},{40,56},{48,0},{56,8},{64,80... | collective-permute-start | bytes 49160 | tf_op jit(solution)/shard_map/ppermute | solution.py:230
  214.0 4.6 %collective-permute-start.10 = (f32[8,512]{1,0:T(8,128)}, f32[8,512]{1,0:T(8,128)S(1)}, u32[]{:S(2)}, u32[]{:S(2)}) collective-permute-start(f32[8,512]{1,0:T(8,128)} %get-tuple-element.11), channel_id=1, source_target_pairs={{0,8},{8,16},{16,24},{24,32},{32,40},{40,48},{48,56},{56,0},{64,72... | collective-permute-start | bytes 49160 | tf_op jit(solution)/shard_map/ppermute | solution.py:230
  219.5 6.7 %collective-permute-start.19 = (f32[2,512]{1,0:T(2,128)S(1)}, f32[2,512]{1,0:T(2,128)S(1)}, u32[]{:S(2)}, u32[]{:S(2)}) collective-permute-start(f32[2,512]{1,0:T(2,128)S(1)} %pad_maximum_fusion.1), channel_id=1, source_target_pairs={{0,192},{8,200},{16,208},{24,216},{32,224},{40,232},{48,240},{56,2... | collective-permute-start | bytes 12296 | tf_op jit(solution)/shard_map/ppermute | solution.py:230
  222.5 4.0 %collective-permute-start.18 = (f32[2,512]{1,0:T(2,128)S(1)}, f32[2,512]{1,0:T(2,128)S(1)}, u32[]{:S(2)}, u32[]{:S(2)}) collective-permute-start(f32[2,512]{1,0:T(2,128)S(1)} %pad_maximum_fusion.1), channel_id=1, source_target_pairs={{0,128},{8,136},{16,144},{24,152},{32,160},{40,168},{48,176},{56,1... | collective-permute-start | bytes 12296 | tf_op jit(solution)/shard_map/ppermute | solution.py:230
  248.7 6.8 %collective-permute-start.21 = (bf16[128,1024]{1,0:T(8,128)(2,1)S(1)}, bf16[128,1024]{1,0:T(8,128)(2,1)S(1)}, u32[]{:S(2)}, u32[]{:S(2)}) collective-permute-start(bf16[128,1024]{1,0:T(8,128)(2,1)S(1)} %bitcast.53), channel_id=1, source_target_pairs={{0,128},{8,136},{16,144},{24,152},{32,160},{40,168},{48,176},{56,1... | collective-permute-start | bytes 786440 | tf_op jit(solution)/shard_map/ppermute | solution.py:230
  249.0 8.2 %collective-permute-start.22 = (bf16[128,1024]{1,0:T(8,128)(2,1)S(1)}, bf16[128,1024]{1,0:T(8,128)(2,1)S(1)}, u32[]{:S(2)}, u32[]{:S(2)}) collective-permute-start(bf16[128,1024]{1,0:T(8,128)(2,1)S(1)} %bitcast.52), channel_id=1, source_target_pairs={{0,192},{8,200},{16,208},{24,216},{32,224},{40,232},{48,240},{56,2... | collective-permute-start | bytes 786440 | tf_op jit(solution)/shard_map/ppermute | solution.py:230
  250.4 7.8 %collective-permute-start.20 = (bf16[128,1024]{1,0:T(8,128)(2,1)S(1)}, bf16[128,1024]{1,0:T(8,128)(2,1)S(1)}, u32[]{:S(2)}, u32[]{:S(2)}) collective-permute-start(bf16[128,1024]{1,0:T(8,128)(2,1)S(1)} %bitcast.51), channel_id=1, source_target_pairs={{0,64},{8,72},{16,80},{24,88},{32,96},{40,104},{48,112},{56,120},{... | collective-permute-start | bytes 786440 | tf_op jit(solution)/shard_map/ppermute | solution.py:230
  262.6 8.4 %collective-permute-start.29 = (bf16[16,1024]{1,0:T(8,128)(2,1)S(1)}, bf16[16,1024]{1,0:T(8,128)(2,1)S(1)}, u32[]{:S(2)}, u32[]{:S(2)}) collective-permute-start(bf16[16,1024]{1,0:T(8,128)(2,1)S(1)} %get-tuple-element.27), channel_id=1, source_target_pairs={{0,56},{8,0},{16,8},{24,16},{32,24},{40,32},{48,40},{56,48},{64,12... | collective-permute-start | bytes 98312 | tf_op jit(solution)/shard_map/ppermute | solution.py:230
  262.7 10.8 %collective-permute-start.28 = (bf16[16,1024]{1,0:T(8,128)(2,1)S(1)}, bf16[16,1024]{1,0:T(8,128)(2,1)S(1)}, u32[]{:S(2)}, u32[]{:S(2)}) collective-permute-start(bf16[16,1024]{1,0:T(8,128)(2,1)S(1)} %get-tuple-element.28), channel_id=1, source_target_pairs={{0,48},{8,56},{16,0},{24,8},{32,16},{40,24},{48,32},{56,40},{64,11... | collective-permute-start | bytes 98312 | tf_op jit(solution)/shard_map/ppermute | solution.py:230
  264.9 8.8 %collective-permute-start.27 = (bf16[16,1024]{1,0:T(8,128)(2,1)S(1)}, bf16[16,1024]{1,0:T(8,128)(2,1)S(1)}, u32[]{:S(2)}, u32[]{:S(2)}) collective-permute-start(bf16[16,1024]{1,0:T(8,128)(2,1)S(1)} %get-tuple-element.29), channel_id=1, source_target_pairs={{0,40},{8,48},{16,56},{24,0},{32,8},{40,16},{48,24},{56,32},{64,10... | collective-permute-start | bytes 98312 | tf_op jit(solution)/shard_map/ppermute | solution.py:230
  267.1 6.7 %collective-permute-start.26 = (bf16[16,1024]{1,0:T(8,128)(2,1)S(1)}, bf16[16,1024]{1,0:T(8,128)(2,1)S(1)}, u32[]{:S(2)}, u32[]{:S(2)}) collective-permute-start(bf16[16,1024]{1,0:T(8,128)(2,1)S(1)} %get-tuple-element.30), channel_id=1, source_target_pairs={{0,32},{8,40},{16,48},{24,56},{32,0},{40,8},{48,16},{56,24},{64,96... | collective-permute-start | bytes 98312 | tf_op jit(solution)/shard_map/ppermute | solution.py:230
  268.4 5.8 %collective-permute-start.25 = (bf16[16,1024]{1,0:T(8,128)(2,1)S(1)}, bf16[16,1024]{1,0:T(8,128)(2,1)S(1)}, u32[]{:S(2)}, u32[]{:S(2)}) collective-permute-start(bf16[16,1024]{1,0:T(8,128)(2,1)S(1)} %get-tuple-element.31), channel_id=1, source_target_pairs={{0,24},{8,32},{16,40},{24,48},{32,56},{40,0},{48,8},{56,16},{64,88... | collective-permute-start | bytes 98312 | tf_op jit(solution)/shard_map/ppermute | solution.py:230
  271.0 4.9 %collective-permute-start.24 = (bf16[16,1024]{1,0:T(8,128)(2,1)S(1)}, bf16[16,1024]{1,0:T(8,128)(2,1)S(1)}, u32[]{:S(2)}, u32[]{:S(2)}) collective-permute-start(bf16[16,1024]{1,0:T(8,128)(2,1)S(1)} %get-tuple-element.32), channel_id=1, source_target_pairs={{0,16},{8,24},{16,32},{24,40},{32,48},{40,56},{48,0},{56,8},{64,80... | collective-permute-start | bytes 98312 | tf_op jit(solution)/shard_map/ppermute | solution.py:230
  273.5 4.4 %collective-permute-start.23 = (bf16[16,1024]{1,0:T(8,128)(2,1)S(1)}, bf16[16,1024]{1,0:T(8,128)(2,1)S(1)}, u32[]{:S(2)}, u32[]{:S(2)}) collective-permute-start(bf16[16,1024]{1,0:T(8,128)(2,1)S(1)} %get-tuple-element.33), channel_id=1, source_target_pairs={{0,8},{8,16},{16,24},{24,32},{32,40},{40,48},{48,56},{56,0},{64,72... | collective-permute-start | bytes 98312 | tf_op jit(solution)/shard_map/ppermute | solution.py:230
  (15 other events, 142.1 us)
Sparse Core Ops, SparseCore 0:
  49.7 47.6 all-gather.3
  246.8 49.3 reduce-scatter.1

commit v3 on v1

--- a/solution.py
+++ b/solution.py
@@ -10,6 +10,7 @@
 F32 = jnp.float32
 BF16 = jnp.bfloat16
 LANES = 128
+COMPACT = 20
 VMEM_LIMIT = 56 * 1024 * 1024
 
 
@@ -132,7 +133,7 @@
 
 
 def grad_kernel(
-    place_ref, stats_ref, logits_ref, target_ref, hidden_ref, hidden_t_ref, weight_ref,
+    place_ref, slot_ref, stats_ref, logits_ref, target_ref, hidden_ref, hidden_t_ref, weight_ref,
     dweight_ref, dhidden_ref, base_ref, norm, mass, gain, cross, partial,
 ):
     step = pl.program_id(0)
@@ -164,7 +165,9 @@
     grads = []
     for q in range(cols // LANES):
         logit = logits_ref[0, :, q * LANES : (q + 1) * LANES]
-        target = target_ref[:, q].reshape(rows, LANES).astype(F32)
+        slot = slot_ref[step * (cols // LANES) + q]
+        held = target_ref[:, jnp.maximum(slot, 0)].reshape(rows, LANES).astype(F32)
+        target = jnp.where(slot >= 0, held, 0.0)
         crossed = crossed + target * logit
         grads.append(
             (gain_tile * (mass_tile * jnp.exp(logit - norm_tile) - target)).astype(BF16)
@@ -197,21 +200,148 @@
         base_ref[...] = mass[pl.ds(start, part), :]
 
 
-def finish_kernel(in_ref, base_ref, out_ref):
-    count, part, wide = in_ref.shape
-    width = wide - LANES
-    total = jnp.zeros((part, wide), F32)
-    for c in range(count):
-        total = total + in_ref[c].astype(F32)
-    out_ref[:, 0:width] = total[:, 0:width].astype(BF16)
-    tail = total[:, width:wide]
-    crossed = tail[:, 0:1] + tail[:, 1:2] + tail[:, 2:3]
-    loss = base_ref[...][:, 0:1] - crossed
-    out_ref[:, width:wide] = lanes_of(pieces(loss), part).astype(BF16)
+def fold(refs):
+    wide = refs[0].shape[-1]
+    total = refs[0][...].astype(F32)
+    for ref in refs[1:]:
+        total = total + ref[...].astype(F32)
+    tail = total[:, wide - LANES :]
+    return total[:, : wide - LANES], tail[:, 0:1] + tail[:, 1:2] + tail[:, 2:3]
+
+
+def fold_kernel(*refs):
+    out_ref = refs[-1]
+    rows, wide = out_ref.shape
+    total, crossed = fold(refs[:-1])
+    out_ref[:, 0 : wide - LANES] = total.astype(BF16)
+    out_ref[:, wide - LANES : wide] = lanes_of(pieces(crossed), rows).astype(BF16)
+
+
+def finish_kernel(*refs):
+    base_ref, out_ref = refs[-2:]
+    rows, wide = out_ref.shape
+    total, crossed = fold(refs[:-2])
+    out_ref[:, 0 : wide - LANES] = total.astype(BF16)
+    loss = base_ref[:, 0:1] - crossed
+    out_ref[:, wide - LANES : wide] = lanes_of(pieces(loss), rows).astype(BF16)
 
 
 def whole(shape):
     return pl.BlockSpec(shape, lambda *_: (0,) * len(shape))
+
+
+def shifted(value, ring, along_x, step):
+    count = lax.axis_size("ctx")
+    lines = count // ring
+    pairs = []
+    for x in range(lines):
+        for z in range(ring):
+            to = (x + step) % lines * ring + z if along_x else x * ring + (z + step) % ring
+            pairs.append((x * ring + z, to))
+    return lax.ppermute(value, "ctx", pairs)
+
+
+def spread(value, ring, along_x):
+    count = lax.axis_size("ctx") // ring if along_x else ring
+    return [value] + [shifted(value, ring, along_x, step) for step in range(1, count)]
+
+
+def exchange(
+    capacity, head_weight, incoming, compact_slot, whole_slot, own_slot, place, behind, by_ctx
+):
+    ctx_count = lax.axis_size("ctx")
+    voc_count, held, part, _ = incoming.shape
+    width, cols = head_weight.shape
+    dev_blocks = cols // LANES
+    owned_blocks = voc_count * dev_blocks
+    rows = ctx_count * part
+    slots = ctx_count * capacity
+    smem = pl.BlockSpec(memory_space=pltpu.SMEM)
+
+    weights = lax.all_gather(head_weight, "voc", axis=0, tiled=False)
+    slot = compact_slot if capacity == COMPACT else whole_slot
+    target, mass = pl.pallas_call(
+        collect_kernel,
+        out_shape=(
+            jax.ShapeDtypeStruct((slots, part, LANES), BF16),
+            jax.ShapeDtypeStruct((part, LANES), F32),
+        ),
+        in_specs=[smem, pl.BlockSpec(memory_space=pltpu.VMEM)],
+        scratch_shapes=[
+            pltpu.VMEM((slots, part, LANES), F32),
+            pltpu.VMEM((voc_count, part, LANES), F32),
+        ],
+        compiler_params=params(),
+        cost_estimate=pl.CostEstimate(
+            flops=4 * slots * part * LANES, bytes_accessed=6 * 1024 * 1024, transcendentals=0
+        ),
+        name="collect_targets",
+    )(slot, incoming)
+    target = target.reshape(ctx_count, capacity, part, LANES)
+    arrived = lax.all_to_all(target, "ctx", 0, 0, tiled=True)
+    hidden_rows = by_ctx[behind].reshape(rows, width + LANES)
+    hidden_t = hidden_rows[:, :width].T
+
+    logits, stats = pl.pallas_call(
+        logits_kernel,
+        grid=(voc_count,),
+        in_specs=[
+            pl.BlockSpec((rows, width), lambda j: (0, 0)),
+            pl.BlockSpec((1, width, cols), lambda j: (j, 0, 0)),
+            whole((part, LANES)),
+        ],
+        out_specs=(
+            pl.BlockSpec((1, rows, cols), lambda j: (j, 0, 0)),
+            whole((ctx_count, 4, rows)),
+        ),
+        out_shape=(
+            jax.ShapeDtypeStruct((voc_count, rows, cols), F32),
+            jax.ShapeDtypeStruct((ctx_count, 4, rows), F32),
+        ),
+        scratch_shapes=[pltpu.VMEM((rows, LANES), F32)] * 2,
+        compiler_params=params(),
+        cost_estimate=pl.CostEstimate(
+            flops=2 * rows * width * cols * voc_count,
+            bytes_accessed=18 * 1024 * 1024,
+            transcendentals=rows * cols * voc_count,
+        ),
+        name="student_logits",
+    )(hidden_rows, weights, mass)
+    all_stats = lax.all_to_all(stats, "ctx", 0, 0, tiled=True)
+
+    dweight, dhidden, base = pl.pallas_call(
+        grad_kernel,
+        grid=(voc_count,),
+        in_specs=[
+            smem,
+            smem,
+            whole((ctx_count, 4, rows)),
+            pl.BlockSpec((1, rows, cols), lambda j: (j, 0, 0)),
+            whole((ctx_count, capacity, part, LANES)),
+            whole((rows, width + LANES)),
+            whole((width, rows)),
+            pl.BlockSpec((1, width, cols), lambda j: (j, 0, 0)),
+        ],
+        out_specs=(
+            pl.BlockSpec((1, width, cols), lambda j: (j, 0, 0)),
+            whole((ctx_count, part, width + LANES)),
+            whole((part, LANES)),
+        ),
+        out_shape=(
+            jax.ShapeDtypeStruct((voc_count, width, cols), BF16),
+            jax.ShapeDtypeStruct((ctx_count, part, width + LANES), BF16),
+            jax.ShapeDtypeStruct((part, LANES), F32),
+        ),
+        scratch_shapes=[pltpu.VMEM((rows, LANES), F32)] * 4 + [pltpu.VMEM((rows, width), F32)],
+        compiler_params=params(),
+        cost_estimate=pl.CostEstimate(
+            flops=4 * rows * width * cols * voc_count,
+            bytes_accessed=30 * 1024 * 1024,
+            transcendentals=rows * cols * voc_count,
+        ),
+        name="grads",
+    )(place, own_slot, all_stats, logits, arrived, hidden_rows, hidden_t, weights)
+    return dweight, dhidden, base
 
 
 def local(hidden, token_weight, head_weight, teacher_logits, block_coeff, block_map):
@@ -229,25 +359,15 @@
     owned_blocks = voc_count * dev_blocks
     slots = ctx_count * owned_blocks
     rows = ctx_count * part
-    smem = pl.BlockSpec(memory_space=pltpu.SMEM)
+    wide = width + LANES
 
     parity = voc_index // half_groups
-    fold = jnp.where(ctx_index % 2 == parity, 0, 1)
-    start = fold * half_rows + voc_index % half_groups * part
+    fold_side = jnp.where(ctx_index % 2 == parity, 0, 1)
+    start = fold_side * half_rows + voc_index % half_groups * part
     mine = lax.dynamic_slice_in_dim(hidden, start, part, 0)
     mine_weight = lax.dynamic_slice_in_dim(token_weight, start, part, 0)
     mine = jnp.concatenate([mine, jnp.broadcast_to(mine_weight[:, None], (part, LANES))], axis=1)
-    by_ctx = lax.all_to_all(
-        jnp.broadcast_to(mine[None], (ctx_count, part, width + LANES)), "ctx", 0, 0, tiled=True
-    )
-    source = jnp.arange(ctx_count, dtype=jnp.int32)
-    half_block = 2 * source + parity
-    place = jnp.where(half_block < ctx_count, half_block, 2 * ctx_count - 1 - half_block)
-    own_half = jnp.where(fold == 0, ctx_index, 2 * ctx_count - 1 - ctx_index)
-    place = jnp.concatenate([place, (own_half // 2)[None]]).astype(jnp.int32)
-    hidden_rows = by_ctx[place[:ctx_count]].reshape(rows, width + LANES)
-    hidden_t = hidden_rows[:, :width].T
-
+    ring = min(8, ctx_count)
     outgoing = pl.pallas_call(
         teacher_kernel,
         out_shape=jax.ShapeDtypeStruct((voc_count, local_blocks + 1, part, LANES), BF16),
@@ -259,98 +379,57 @@
         ),
         name="teacher_map",
     )(teacher_logits, block_coeff)
+    near = jnp.stack(spread(mine, ring, False))
     incoming = lax.all_to_all(outgoing, "voc", 0, 0, tiled=True)
 
-    head_weight, incoming = lax.optimization_barrier((head_weight, incoming))
-    weights = lax.all_gather(head_weight, "voc", axis=0, tiled=False)
-
-    target, mass = pl.pallas_call(
-        collect_kernel,
-        out_shape=(
-            jax.ShapeDtypeStruct((slots, part, LANES), BF16),
-            jax.ShapeDtypeStruct((part, LANES), F32),
-        ),
-        in_specs=[smem, pl.BlockSpec(memory_space=pltpu.VMEM)],
-        scratch_shapes=[
-            pltpu.VMEM((slots, part, LANES), F32),
-            pltpu.VMEM((voc_count, part, LANES), F32),
-        ],
-        compiler_params=params(),
-        cost_estimate=pl.CostEstimate(
-            flops=4 * slots * part * LANES, bytes_accessed=6 * 1024 * 1024, transcendentals=0
-        ),
-        name="collect_targets",
-    )(block_map, incoming)
-    target = target.reshape(ctx_count, owned_blocks, part, LANES)
-    arrived = lax.all_to_all(target, "ctx", 0, 0, tiled=True)
-
-    logits, stats = pl.pallas_call(
-        logits_kernel,
-        grid=(voc_count,),
-        in_specs=[
-            pl.BlockSpec((rows, width), lambda j: (0, 0)),
-            pl.BlockSpec((1, width, cols), lambda j: (j, 0, 0)),
-            whole((part, LANES)),
-        ],
-        out_specs=(
-            pl.BlockSpec((1, rows, cols), lambda j: (j, 0, 0)),
-            whole((ctx_count, 4, rows)),
-        ),
-        out_shape=(
-            jax.ShapeDtypeStruct((voc_count, rows, cols), F32),
-            jax.ShapeDtypeStruct((ctx_count, 4, rows), F32),
-        ),
-        scratch_shapes=[pltpu.VMEM((rows, LANES), F32)] * 2,
-        compiler_params=params(),
-        cost_estimate=pl.CostEstimate(
-            flops=2 * rows * width * cols * voc_count,
-            bytes_accessed=18 * 1024 * 1024,
-            transcendentals=rows * cols * voc_count,
-        ),
-        name="student_logits",
-    )(hidden_rows, weights, mass)
-    all_stats = lax.all_to_all(stats, "ctx", 0, 0, tiled=True)
-
-    dweight, dhidden, base = pl.pallas_call(
-        grad_kernel,
-        grid=(voc_count,),
-        in_specs=[
-            smem,
-            whole((ctx_count, 4, rows)),
-            pl.BlockSpec((1, rows, cols), lambda j: (j, 0, 0)),
-            pl.BlockSpec((ctx_count, dev_blocks, part, LANES), lambda j: (0, j, 0, 0)),
-            whole((rows, width + LANES)),
-            whole((width, rows)),
-            pl.BlockSpec((1, width, cols), lambda j: (j, 0, 0)),
-        ],
-        out_specs=(
-            pl.BlockSpec((1, width, cols), lambda j: (j, 0, 0)),
-            whole((ctx_count, part, width + LANES)),
-            whole((part, LANES)),
-        ),
-        out_shape=(
-            jax.ShapeDtypeStruct((voc_count, width, cols), BF16),
-            jax.ShapeDtypeStruct((ctx_count, part, width + LANES), BF16),
-            jax.ShapeDtypeStruct((part, LANES), F32),
-        ),
-        scratch_shapes=[pltpu.VMEM((rows, LANES), F32)] * 4 + [pltpu.VMEM((rows, width), F32)],
-        compiler_params=params(),
-        cost_estimate=pl.CostEstimate(
-            flops=4 * rows * width * cols * voc_count,
-            bytes_accessed=30 * 1024 * 1024,
-            transcendentals=rows * cols * voc_count,
-        ),
-        name="grads",
-    )(place, all_stats, logits, arrived, hidden_rows, hidden_t, weights)
+    wanted = jnp.any(
+        block_map[:, None] == jnp.arange(slots, dtype=jnp.int32)[None, :], axis=0
+    ).astype(jnp.int32).reshape(ctx_count, owned_blocks)
+    number = jnp.cumsum(wanted, axis=1) - wanted
+    fits = jnp.max(jnp.sum(wanted, axis=1)) <= COMPACT
+    own_slot = jnp.where(wanted == 1, number, -1)
+    own_slot = lax.dynamic_index_in_dim(own_slot, ctx_index, 0, keepdims=False)
+    in_order = number.reshape(slots)[block_map]
+    compact_slot = block_map // owned_blocks * COMPACT + in_order
+    whole_slot = block_map // owned_blocks * owned_blocks + in_order
+
+    source = jnp.arange(ctx_count, dtype=jnp.int32)
+    half_block = 2 * source + parity
+    place = jnp.where(half_block < ctx_count, half_block, 2 * ctx_count - 1 - half_block)
+    own_half = jnp.where(fold_side == 0, ctx_index, 2 * ctx_count - 1 - ctx_index)
+    behind = (ctx_index // ring - place // ring) % (ctx_count // ring) * ring + (ctx_index - place) % ring
+    ahead = (place // ring - ctx_index // ring) % (ctx_count // ring) * ring + (place - ctx_index) % ring
+    place = jnp.concatenate([ahead, (own_half // 2)[None]]).astype(jnp.int32)
+    by_ctx = jnp.concatenate(spread(near, ring, True), axis=0)
+    operands = lax.optimization_barrier(
+        (incoming, compact_slot, whole_slot, own_slot, place, behind, by_ctx)
+    )
+    dweight, dhidden, base = lax.cond(
+        fits,
+        functools.partial(exchange, COMPACT),
+        functools.partial(exchange, owned_blocks),
+        head_weight,
+        *operands,
+    )
     grad_weight = lax.psum_scatter(dweight, "voc", scatter_dimension=0, tiled=True)
     grad_weight = grad_weight.reshape(width, cols).astype(F32)
-    returned = lax.all_to_all(dhidden, "ctx", 0, 0, tiled=True)
+    pieces_x = dhidden.reshape(ctx_count // ring, ring * part, wide)
+    parts = [pieces_x[0]]
+    parts += [shifted(pieces_x[e], ring, True, e) for e in range(1, ctx_count // ring)]
+    folded = pl.pallas_call(
+        fold_kernel,
+        out_shape=jax.ShapeDtypeStruct((ring * part, wide), BF16),
+        compiler_params=params(),
+        name="fold_rows",
+    )(*parts)
+    pieces_z = folded.reshape(ring, part, wide)
+    parts = [pieces_z[0]] + [shifted(pieces_z[e], ring, False, e) for e in range(1, ring)]
     done = pl.pallas_call(
         finish_kernel,
-        out_shape=jax.ShapeDtypeStruct((part, width + LANES), BF16),
+        out_shape=jax.ShapeDtypeStruct((part, wide), BF16),
         compiler_params=params(),
         name="finish_rows",
-    )(returned, base)
+    )(*parts, base)
     all_done = lax.all_gather(done, "voc", axis=0, tiled=False)
     all_done = jnp.where(ctx_index % 2 == 0, all_done, jnp.roll(all_done, half_groups, axis=0))
     all_done = all_done.reshape(rows_dev, width + LANES)

time: 289 us -> 245 us (0.85)
  waiting for transfers between devices: 128 us -> 80 us
  blocking collectives: 53.4 us -> 17.4 us
  starting transfers between devices: 33.9 us -> 58.9 us
  local copies, waits for them, and re-layouts: 6.64 us -> 18.7 us
    all_to_all x4 -> x3, waiting for transfers between devices: 126 us -> 19.5 us  [the longest x1 11.2 us: exchange(): arrived = lax.all_to_all(target, 'ctx', 0, 0, tiled=True)]
    ppermute x0 -> x20, starting transfers between devices: none -> 37.5 us  [shifted(): return lax.ppermute(value, 'ctx', pairs)]
    all_to_all x1 -> x0, blocking collectives: 35 us -> none  [local(): incoming = lax.all_to_all(outgoing, 'voc', 0, 0, tiled=True)]
    all_gather x1, waiting for transfers between devices: 1.99 us -> 35.1 us  [exchange(): weights = lax.all_gather(head_weight, 'voc', axis=0, tiled=False)]
    ppermute x0 -> x20, waiting for transfers between devices: none -> 24.1 us  [shifted(): return lax.ppermute(value, 'ctx', pairs)]
    all_to_all x4 -> x3, starting transfers between devices: 33.9 us -> 21.3 us  [the longest x1 7.46 us: exchange(): arrived = lax.all_to_all(target, 'ctx', 0, 0, tiled=True)]
    unnamed x11 -> x34, local copies, waits for them, and re-layouts: 3.01 us -> 7.12 us
    pallas_call x4 -> x5, Pallas kernels: 40.6 us -> 39.5 us  [the longest x1 17.9 us: exchange(): pl.pallas_call(grad_kernel, grid=(voc_count,), in_specs=[smem, smem, whol...]
  transfers between devices with their start and end apart: 6 -> 25, of which waited for: 5 -> 12; matrix products, arithmetic and copies ran while one was open for 2% -> 8% of each run, Pallas kernels for 8% -> 12%
where the time goes in v3:
time: 245 us; the launch traced here: 244 us
  waiting for transfers between devices  80 us (33%)
  starting transfers between devices  58.9 us (24%)
  Pallas kernels  46.9 us (19%)
  local copies, waits for them, and re-layouts  18.7 us (8%)
  blocking collectives  17.4 us (7%)
  between operations  16.3 us (7%)
  other arithmetic  5.41 us (2%)
    ppermute x20, starting transfers between devices, shifted(): return lax.ppermute(value, 'ctx', pairs)  37.5 us
    all_gather x1, waiting for transfers between devices, exchange(): weights = lax.all_gather(head_weight, 'voc', axis=0, tiled=False)  35.1 us
    ppermute x20, waiting for transfers between devices, shifted(): return lax.ppermute(value, 'ctx', pairs)  24.1 us
    pallas_call x1, Pallas kernels, exchange(): pl.pallas_call(grad_kernel, grid=(voc_count,), in_specs=[smem, smem, whol...  17.9 us
    all_gather x1, blocking collectives, local(): all_done = lax.all_gather(done, 'voc', axis=0, tiled=False)  17.4 us
    pallas_call x1, Pallas kernels, exchange(): pl.pallas_call(logits_kernel, grid=(voc_count,), in_specs=[pl.BlockSpec((...  11.9 us
    all_to_all x1, waiting for transfers between devices, exchange(): arrived = lax.all_to_all(target, 'ctx', 0, 0, tiled=True)  11.2 us
    all_to_all x1, waiting for transfers between devices, exchange(): all_stats = lax.all_to_all(stats, 'ctx', 0, 0, tiled=True)  8.23 us
  transfers between devices with their start and end apart: 25, of which 12 were waited for; matrix products, arithmetic and copies ran while one was open for 8% of the time, Pallas kernels for 12%

profile of v3, /device:TPU:1, one launch (start us, length us, event | category | flops | bytes accessed | tf_op | source)
XLA Modules:
  0.0 243.9 jit_solution(8941944846662964828)
XLA Ops:
  9.0 6.9 %collective-permute-start.5 = (bf16[16,1024]{1,0:T(8,128)(2,1)S(1)}, bf16[16,1024]{1,0:T(8,128)(2,1)S(1)}, u32[]{:S(2)}, u32[]{:S(2)}) collective-permute-start(bf16[16,1024]{1,0:T(8,128)(2,1)S(1)} %pad_maximum_fusion), channel_id=1, source_target_pairs={{0,48},{8,56},{16,0},{24,8},{32,16},{40,24},{48,32},{56,40},{64,11... | collective-permute-start | bytes 98312 | tf_op jit(solution)/shard_map/ppermute | solution.py:241
  16.6 4.2 %collective-permute-start.3 = (bf16[16,1024]{1,0:T(8,128)(2,1)S(1)}, bf16[16,1024]{1,0:T(8,128)(2,1)S(1)}, u32[]{:S(2)}, u32[]{:S(2)}) collective-permute-start(bf16[16,1024]{1,0:T(8,128)(2,1)S(1)} %pad_maximum_fusion), channel_id=1, source_target_pairs={{0,32},{8,40},{16,48},{24,56},{32,0},{40,8},{48,16},{56,24},{64,96... | collective-permute-start | bytes 98312 | tf_op jit(solution)/shard_map/ppermute | solution.py:241
  22.3 7.5 %teacher_map.1 = bf16[8,65,16,128]{3,2,1,0:T(8,128)(2,1)} custom-call(bf16[128,8192]{1,0:T(8,128)(2,1)} %logits_ref.1, bf16[64,128,128]{2,1,0:T(8,128)(2,1)} %coeff_ref.1), custom_call_target="tpu_custom_call" | custom-call | flops 268435456 | bytes 6291456 | tf_op jit(solution)/shard_map/teacher_map/pallas_call | solution.py:371
  29.7 6.7 %all-to-all-start.4 = ((bf16[8,65,16,128]{3,2,1,0:T(8,128)(2,1)}), bf16[8,65,16,128]{3,2,1,0:T(8,128)(2,1)S(1)}, u32[]{:S(2)}, u32[]{:S(2)}) async-start(bf16[8,65,16,128]{3,2,1,0:T(8,128)(2,1)} %teacher_map.1), calls=%async_computation.4 | async-start | bytes 4259840 | tf_op jit(solution)/shard_map/all_to_all | solution.py:383
  37.7 2.3 gather_fusion.2
  40.1 2.2 collective-permute-start.1
  42.9 2.9 %collective-permute-done.1 = bf16[16,1024]{1,0:T(8,128)(2,1)S(1)} collective-permute-done((bf16[16,1024]{1,0:T(8,128)(2,1)S(1)}, bf16[16,1024]{1,0:T(8,128)(2,1)S(1)}, u32[]{:S(2)}, u32[]{:S(2)}) %collective-permute-start.1) | collective-permute-done | bytes 32800 | tf_op jit(solution)/shard_map/ppermute | solution.py:241
  51.3 2.5 %collective-permute-start.8 = (bf16[8,16,1024]{2,1,0:T(8,128)(2,1)}, bf16[8,16,1024]{2,1,0:T(8,128)(2,1)}, u32[]{:S(2)}, u32[]{:S(2)}) collective-permute-start(bf16[8,16,1024]{2,1,0:T(8,128)(2,1)} %get-tuple-element.87), channel_id=1, source_target_pairs={{0,128},{8,136},{16,144},{24,152},{32,160},{40,168},{48,176},{56,1... | collective-permute-start | bytes 786440 | tf_op jit(solution)/shard_map/ppermute | solution.py:241
  56.5 1.9 collective-permute-done.7
  59.3 5.6 %collective-permute-done.8 = bf16[8,16,1024]{2,1,0:T(8,128)(2,1)} collective-permute-done((bf16[8,16,1024]{2,1,0:T(8,128)(2,1)}, bf16[8,16,1024]{2,1,0:T(8,128)(2,1)}, u32[]{:S(2)}, u32[]{:S(2)}) %collective-permute-start.8) | collective-permute-done | bytes 262176 | tf_op jit(solution)/shard_map/ppermute | solution.py:241
  66.9 109.5 %conditional.1 = ((bf16[8,896,512]{2,1,0:T(8,128)(2,1)}, bf16[32,16,1024]{2,1,0:T(8,128)(2,1)S(1)}, f32[16,128]{1,0:T(8,128)S(1)})) conditional(s32[]{:T(128)} %convert_element_type.24, (s32[32]{0:T(128)S(1)}, bf16[32,16,1024]{2,1,0:T(8,128)(2,1)S(1)}, bf16[896,512]{1,0:T(8,128)(2,1)}, s32[512]{0:T(512)S(1)}, bf16[8,65,16,128]{3,2,1,0:T(8,128)(2,1)S(1)}, ...), branch_computations={%region_4.5_spmd, %region_5.6_spmd} | conditional | flops 11282678784 | bytes 105779880 | solution.py:407
  67.9 5.7 %collect_targets.3 = (bf16[640,16,128]{2,1,0:T(8,128)(2,1)}, f32[16,128]{1,0:T(8,128)}) custom-call(s32[512]{0:T(512)S(1)} %get-tuple-element.44.slot_ref, bf16[8,65,16,128]{3,2,1,0:T(8,128)(2,1)S(1)} %get-tuple-element.45.in_ref), custom_call_target="tpu_custom_call" | custom-call | flops 5242880 | bytes 6291456 | tf_op jit(solution)/shard_map/cond/branch_1_fun/collect_targets/pallas_call | solution.py:263
  73.6 7.5 %all-to-all-start.3 = ((bf16[32,20,16,128]{3,2,1,0:T(8,128)(2,1)}), bf16[32,20,16,128]{3,2,1,0:T(8,128)(2,1)}, u32[]{:S(2)}, u32[]{:S(2)}) async-start(bf16[32,20,16,128]{3,2,1,0:T(8,128)(2,1)} %bitcast.53), calls=%async_computation.3 | async-start | bytes 5242880 | tf_op jit(solution)/shard_map/cond/branch_1_fun/all_to_all | solution.py:281
  81.1 1.6 gather_fusion.1
  82.7 35.1 %all-gather.8.cloned.1.call-done = bf16[7168,512]{1,0:T(8,128)(2,1)} async-done(((bf16[896,512]{1,0:T(8,128)(2,1)}), bf16[7168,512]{1,0:T(8,128)(2,1)}) %all-gather.8.cloned.1.call-update) | async-done | bytes 7340048 | tf_op jit(solution)/shard_map/cond/branch_1_fun/all_gather | solution.py:261
  117.8 11.9 %student_logits.3 = (f32[8,512,512]{2,1,0:T(8,128)}, f32[32,4,512]{2,1,0:T(4,128)}) custom-call(bf16[512,1024]{1,0:T(8,128)(2,1)} %bitcast.50, bf16[8,896,512]{2,1,0:T(8,128)(2,1)} %bitcast.67, f32[16,128]{1,0:T(8,128)} %get-tuple-element.46.mass_ref), custom_call_target="tpu_custom_call" | custom-call | flops 3758096384 | bytes 18874368 | tf_op jit(solution)/shard_map/cond/branch_1_fun/student_logits/pallas_call | solution.py:285
  129.7 11.2 %all-to-all-done.3.target_ref = bf16[32,20,16,128]{3,2,1,0:T(8,128)(2,1)} async-done(((bf16[32,20,16,128]{3,2,1,0:T(8,128)(2,1)}), bf16[32,20,16,128]{3,2,1,0:T(8,128)(2,1)}, u32[]{:S(2)}, u32[]{:S(2)}) %all-to-all-start.3) | async-done | bytes 2621472 | tf_op jit(solution)/shard_map/cond/branch_1_fun/all_to_all | solution.py:281
  141.0 7.2 %all-to-all-start.2 = ((f32[32,4,512]{2,1,0:T(4,128)}), f32[32,4,512]{2,1,0:T(4,128)S(1)}, u32[]{:S(2)}, u32[]{:S(2)}) async-start(f32[32,4,512]{2,1,0:T(4,128)} %get-tuple-element.47), calls=%async_computation.2 | async-start | bytes 524288 | tf_op jit(solution)/shard_map/cond/branch_1_fun/all_to_all | solution.py:310
  149.6 8.2 %all-to-all-done.2.stats_ref = f32[32,4,512]{2,1,0:T(4,128)S(1)} async-done(((f32[32,4,512]{2,1,0:T(4,128)}), f32[32,4,512]{2,1,0:T(4,128)S(1)}, u32[]{:S(2)}, u32[]{:S(2)}) %all-to-all-start.2) | async-done | bytes 262176 | tf_op jit(solution)/shard_map/cond/branch_1_fun/all_to_all | solution.py:310
  158.5 17.9 %grads.3 = (bf16[8,896,512]{2,1,0:T(8,128)(2,1)}, bf16[32,16,1024]{2,1,0:T(8,128)(2,1)S(1)}, f32[16,128]{1,0:T(8,128)S(1)}) custom-call(s32[33]{0:T(128)S(1)} %get-tuple-element.39.place_ref, s32[32]{0:T(128)S(1)} %get-tuple-element.40.slot_ref, f32[32,4,512]{2,1,0:T(4,128)} %copy-done.8, f32[8,512,512]{2,1,0:T(8,128)} %get-tuple-element.48.logits_ref, ...), custom_call_target="tpu_custom_call" | custom-call | flops 7516192768 | bytes 31457280 | tf_op jit(solution)/shard_map/cond/branch_1_fun/grads/pallas_call | solution.py:312
  180.7 3.8 %collective-permute-done.11.refs_2_ = bf16[128,1024]{1,0:T(8,128)(2,1)S(1)} collective-permute-done((bf16[128,1024]{1,0:T(8,128)(2,1)S(1)}, bf16[128,1024]{1,0:T(8,128)(2,1)S(1)}, u32[]{:S(2)}, u32[]{:S(2)}) %collective-permute-start.11) | collective-permute-done | bytes 262176 | tf_op jit(solution)/shard_map/ppermute | solution.py:241
  184.5 4.5 %collective-permute-done.12.refs_3_ = bf16[128,1024]{1,0:T(8,128)(2,1)S(1)} collective-permute-done((bf16[128,1024]{1,0:T(8,128)(2,1)S(1)}, bf16[128,1024]{1,0:T(8,128)(2,1)S(1)}, u32[]{:S(2)}, u32[]{:S(2)}) %collective-permute-start.12) | collective-permute-done | bytes 262176 | tf_op jit(solution)/shard_map/ppermute | solution.py:241
  189.8 2.3 fold_rows.1
  193.7 3.3 %collective-permute-start.19 = (bf16[16,1024]{1,0:T(8,128)(2,1)S(1)}, bf16[16,1024]{1,0:T(8,128)(2,1)S(1)}, u32[]{:S(2)}, u32[]{:S(2)}) collective-permute-start(bf16[16,1024]{1,0:T(8,128)(2,1)S(1)} %get-tuple-element.79), channel_id=1, source_target_pairs={{0,56},{8,0},{16,8},{24,16},{32,24},{40,32},{48,40},{56,48},{64,12... | collective-permute-start | bytes 98312 | tf_op jit(solution)/shard_map/ppermute | solution.py:241
  198.3 2.5 %collective-permute-start.17 = (bf16[16,1024]{1,0:T(8,128)(2,1)S(1)}, bf16[16,1024]{1,0:T(8,128)(2,1)S(1)}, u32[]{:S(2)}, u32[]{:S(2)}) collective-permute-start(bf16[16,1024]{1,0:T(8,128)(2,1)S(1)} %get-tuple-element.81), channel_id=1, source_target_pairs={{0,40},{8,48},{16,56},{24,0},{32,8},{40,16},{48,24},{56,32},{64,10... | collective-permute-start | bytes 98312 | tf_op jit(solution)/shard_map/ppermute | solution.py:241
  200.8 2.5 %collective-permute-start.16 = (bf16[16,1024]{1,0:T(8,128)(2,1)S(1)}, bf16[16,1024]{1,0:T(8,128)(2,1)S(1)}, u32[]{:S(2)}, u32[]{:S(2)}) collective-permute-start(bf16[16,1024]{1,0:T(8,128)(2,1)S(1)} %get-tuple-element.82), channel_id=1, source_target_pairs={{0,32},{8,40},{16,48},{24,56},{32,0},{40,8},{48,16},{56,24},{64,96... | collective-permute-start | bytes 98312 | tf_op jit(solution)/shard_map/ppermute | solution.py:241
  203.3 2.6 %collective-permute-start.15 = (bf16[16,1024]{1,0:T(8,128)(2,1)S(1)}, bf16[16,1024]{1,0:T(8,128)(2,1)S(1)}, u32[]{:S(2)}, u32[]{:S(2)}) collective-permute-start(bf16[16,1024]{1,0:T(8,128)(2,1)S(1)} %get-tuple-element.83), channel_id=1, source_target_pairs={{0,24},{8,32},{16,40},{24,48},{32,56},{40,0},{48,8},{56,16},{64,88... | collective-permute-start | bytes 98312 | tf_op jit(solution)/shard_map/ppermute | solution.py:241
  205.9 1.7 collective-permute-start.14
  210.9 1.8 collective-permute-done.13.refs_1_
  213.4 1.6 finish_rows.1
  215.0 17.4 %all-gather.2 = bf16[128,1024]{1,0:T(8,128)(2,1)S(1)} all-gather(bf16[16,1024]{1,0:T(8,128)(2,1)} %finish_rows.1), channel_id=4, replica_groups=mesh['ctx'=32,'voc'=8] {'voc'}, dimensions={0}, use_global_device_ids=true | all-gather | bytes 294912 | tf_op jit(solution)/shard_map/all_gather | solution.py:433
  233.8 2.7 %bitcast_convert_fusion = f32[896,512]{1,0:T(8,128)} fusion(bf16[1,896,512]{2,1,0:T(8,128)(2,1)} %reduce-scatter.2.cloned.1.call-done), kind=kLoop, calls=%fused_computation.9 | loop fusion | flops 458752 | bytes 2752512 | tf_op jit(solution)/shard_map/convert_element_type | solution.py:415
  (100 shorter events, 31.5 us)
Async XLA Ops:
  9.0 39.3 %collective-permute-start.5 = (bf16[16,1024]{1,0:T(8,128)(2,1)S(1)}, bf16[16,1024]{1,0:T(8,128)(2,1)S(1)}, u32[]{:S(2)}, u32[]{:S(2)}) collective-permute-start(bf16[16,1024]{1,0:T(8,128)(2,1)S(1)} %pad_maximum_fusion), channel_id=1, source_target_pairs={{0,48},{8,56},{16,0},{24,8},{32,16},{40,24},{48,32},{56,40},{64,11... | collective-permute-start | bytes 98312 | tf_op jit(solution)/shard_map/ppermute | solution.py:241
  15.9 31.8 %collective-permute-start.4 = (bf16[16,1024]{1,0:T(8,128)(2,1)S(1)}, bf16[16,1024]{1,0:T(8,128)(2,1)S(1)}, u32[]{:S(2)}, u32[]{:S(2)}) collective-permute-start(bf16[16,1024]{1,0:T(8,128)(2,1)S(1)} %pad_maximum_fusion), channel_id=1, source_target_pairs={{0,40},{8,48},{16,56},{24,0},{32,8},{40,16},{48,24},{56,32},{64,10... | collective-permute-start | bytes 98312 | tf_op jit(solution)/shard_map/ppermute | solution.py:241
  16.6 30.4 %collective-permute-start.3 = (bf16[16,1024]{1,0:T(8,128)(2,1)S(1)}, bf16[16,1024]{1,0:T(8,128)(2,1)S(1)}, u32[]{:S(2)}, u32[]{:S(2)}) collective-permute-start(bf16[16,1024]{1,0:T(8,128)(2,1)S(1)} %pad_maximum_fusion), channel_id=1, source_target_pairs={{0,32},{8,40},{16,48},{24,56},{32,0},{40,8},{48,16},{56,24},{64,96... | collective-permute-start | bytes 98312 | tf_op jit(solution)/shard_map/ppermute | solution.py:241
  20.8 25.6 %collective-permute-start.2 = (bf16[16,1024]{1,0:T(8,128)(2,1)S(1)}, bf16[16,1024]{1,0:T(8,128)(2,1)S(1)}, u32[]{:S(2)}, u32[]{:S(2)}) collective-permute-start(bf16[16,1024]{1,0:T(8,128)(2,1)S(1)} %pad_maximum_fusion), channel_id=1, source_target_pairs={{0,24},{8,32},{16,40},{24,48},{32,56},{40,0},{48,8},{56,16},{64,88... | collective-permute-start | bytes 98312 | tf_op jit(solution)/shard_map/ppermute | solution.py:241
  20.8 19.3 %collective-permute-start = (bf16[16,1024]{1,0:T(8,128)(2,1)S(1)}, bf16[16,1024]{1,0:T(8,128)(2,1)S(1)}, u32[]{:S(2)}, u32[]{:S(2)}) collective-permute-start(bf16[16,1024]{1,0:T(8,128)(2,1)S(1)} %pad_maximum_fusion), channel_id=1, source_target_pairs={{0,8},{8,16},{16,24},{24,32},{32,40},{40,48},{48,56},{56,0},{64,72... | collective-permute-start | bytes 98312 | tf_op jit(solution)/shard_map/ppermute | solution.py:241
  29.7 6.7 %copy-start.16 = (s32[512]{0:T(512)S(1)}, s32[512]{0:T(512)}, u32[]{:S(2)}) copy-start(s32[512]{0:T(512)} %param.13) | copy-start | bytes 6148
  29.7 37.2 %all-to-all-start.4 = ((bf16[8,65,16,128]{3,2,1,0:T(8,128)(2,1)}), bf16[8,65,16,128]{3,2,1,0:T(8,128)(2,1)S(1)}, u32[]{:S(2)}, u32[]{:S(2)}) async-start(bf16[8,65,16,128]{3,2,1,0:T(8,128)(2,1)} %teacher_map.1), calls=%async_computation.4 | async-start | bytes 4259840 | tf_op jit(solution)/shard_map/all_to_all | solution.py:383
  40.1 5.7 %collective-permute-start.1 = (bf16[16,1024]{1,0:T(8,128)(2,1)S(1)}, bf16[16,1024]{1,0:T(8,128)(2,1)S(1)}, u32[]{:S(2)}, u32[]{:S(2)}) collective-permute-start(bf16[16,1024]{1,0:T(8,128)(2,1)S(1)} %pad_maximum_fusion), channel_id=1, source_target_pairs={{0,16},{8,24},{16,32},{24,40},{32,48},{40,56},{48,0},{56,8},{64,80... | collective-permute-start | bytes 98312 | tf_op jit(solution)/shard_map/ppermute | solution.py:241
  45.8 3.6 %collective-permute-start.6 = (bf16[16,1024]{1,0:T(8,128)(2,1)S(1)}, bf16[16,1024]{1,0:T(8,128)(2,1)S(1)}, u32[]{:S(2)}, u32[]{:S(2)}) collective-permute-start(bf16[16,1024]{1,0:T(8,128)(2,1)S(1)} %pad_maximum_fusion), channel_id=1, source_target_pairs={{0,56},{8,0},{16,8},{24,16},{32,24},{40,32},{48,40},{56,48},{64,12... | collective-permute-start | bytes 98312 | tf_op jit(solution)/shard_map/ppermute | solution.py:241
  50.0 8.3 %collective-permute-start.7 = (bf16[8,16,1024]{2,1,0:T(8,128)(2,1)}, bf16[8,16,1024]{2,1,0:T(8,128)(2,1)}, u32[]{:S(2)}, u32[]{:S(2)}) collective-permute-start(bf16[8,16,1024]{2,1,0:T(8,128)(2,1)} %get-tuple-element.87), channel_id=1, source_target_pairs={{0,64},{8,72},{16,80},{24,88},{32,96},{40,104},{48,112},{56,120},{... | collective-permute-start | bytes 786440 | tf_op jit(solution)/shard_map/ppermute | solution.py:241
  51.3 13.7 %collective-permute-start.8 = (bf16[8,16,1024]{2,1,0:T(8,128)(2,1)}, bf16[8,16,1024]{2,1,0:T(8,128)(2,1)}, u32[]{:S(2)}, u32[]{:S(2)}) collective-permute-start(bf16[8,16,1024]{2,1,0:T(8,128)(2,1)} %get-tuple-element.87), channel_id=1, source_target_pairs={{0,128},{8,136},{16,144},{24,152},{32,160},{40,168},{48,176},{56,1... | collective-permute-start | bytes 786440 | tf_op jit(solution)/shard_map/ppermute | solution.py:241
  53.8 12.1 %collective-permute-start.9 = (bf16[8,16,1024]{2,1,0:T(8,128)(2,1)}, bf16[8,16,1024]{2,1,0:T(8,128)(2,1)}, u32[]{:S(2)}, u32[]{:S(2)}) collective-permute-start(bf16[8,16,1024]{2,1,0:T(8,128)(2,1)} %get-tuple-element.87), channel_id=1, source_target_pairs={{0,192},{8,200},{16,208},{24,216},{32,224},{40,232},{48,240},{56,2... | collective-permute-start | bytes 786440 | tf_op jit(solution)/shard_map/ppermute | solution.py:241
  67.1 50.7 %all-gather.8.cloned.1.call-start = ((), (), s32[]{:S(2)}) async-start(), calls=%async_computation.7 | async-start | bytes 8257536 | tf_op jit(solution)/shard_map/cond/branch_1_fun/all_gather | solution.py:261
  73.6 67.4 %all-to-all-start.3 = ((bf16[32,20,16,128]{3,2,1,0:T(8,128)(2,1)}), bf16[32,20,16,128]{3,2,1,0:T(8,128)(2,1)}, u32[]{:S(2)}, u32[]{:S(2)}) async-start(bf16[32,20,16,128]{3,2,1,0:T(8,128)(2,1)} %bitcast.53), calls=%async_computation.3 | async-start | bytes 5242880 | tf_op jit(solution)/shard_map/cond/branch_1_fun/all_to_all | solution.py:281
  117.8 30.4 %copy-start.3 = (bf16[32,16,1024]{2,1,0:T(8,128)(2,1)S(1)}, bf16[32,16,1024]{2,1,0:T(8,128)(2,1)}, u32[]{:S(2)}) copy-start(bf16[32,16,1024]{2,1,0:T(8,128)(2,1)} %gather_fusion.1) | copy-start | bytes 3145732 | tf_op jit(solution)/shard_map/cond
  141.0 16.9 %all-to-all-start.2 = ((f32[32,4,512]{2,1,0:T(4,128)}), f32[32,4,512]{2,1,0:T(4,128)S(1)}, u32[]{:S(2)}, u32[]{:S(2)}) async-start(f32[32,4,512]{2,1,0:T(4,128)} %get-tuple-element.47), calls=%async_computation.2 | async-start | bytes 524288 | tf_op jit(solution)/shard_map/cond/branch_1_fun/all_to_all | solution.py:310
  176.4 57.4 %reduce-scatter.2.cloned.1.call-start = ((), (), s32[]{:S(2)}) async-start(), calls=%async_computation.8 | async-start | bytes 8257536 | tf_op jit(solution)/shard_map/reduce_scatter | solution.py:414
  177.8 6.8 %collective-permute-start.11 = (bf16[128,1024]{1,0:T(8,128)(2,1)S(1)}, bf16[128,1024]{1,0:T(8,128)(2,1)S(1)}, u32[]{:S(2)}, u32[]{:S(2)}) collective-permute-start(bf16[128,1024]{1,0:T(8,128)(2,1)S(1)} %bitcast.64), channel_id=1, source_target_pairs={{0,128},{8,136},{16,144},{24,152},{32,160},{40,168},{48,176},{56,1... | collective-permute-start | bytes 786440 | tf_op jit(solution)/shard_map/ppermute | solution.py:241
  179.2 9.8 %collective-permute-start.12 = (bf16[128,1024]{1,0:T(8,128)(2,1)S(1)}, bf16[128,1024]{1,0:T(8,128)(2,1)S(1)}, u32[]{:S(2)}, u32[]{:S(2)}) collective-permute-start(bf16[128,1024]{1,0:T(8,128)(2,1)S(1)} %bitcast.63), channel_id=1, source_target_pairs={{0,192},{8,200},{16,208},{24,216},{32,224},{40,232},{48,240},{56,2... | collective-permute-start | bytes 786440 | tf_op jit(solution)/shard_map/ppermute | solution.py:241
  180.5 8.6 %collective-permute-start.10 = (bf16[128,1024]{1,0:T(8,128)(2,1)S(1)}, bf16[128,1024]{1,0:T(8,128)(2,1)S(1)}, u32[]{:S(2)}, u32[]{:S(2)}) collective-permute-start(bf16[128,1024]{1,0:T(8,128)(2,1)S(1)} %bitcast.62), channel_id=1, source_target_pairs={{0,64},{8,72},{16,80},{24,88},{32,96},{40,104},{48,112},{56,120},{... | collective-permute-start | bytes 786440 | tf_op jit(solution)/shard_map/ppermute | solution.py:241
  192.1 44.4 %copy-start.1 = (bf16[128,896]{1,0:T(8,128)(2,1)S(1)}, bf16[128,896]{1,0:T(8,128)(2,1)}, u32[]{:S(2)}) copy-start(bf16[128,896]{1,0:T(8,128)(2,1)} %param.8) | copy-start | bytes 688132
  193.7 12.3 %collective-permute-start.19 = (bf16[16,1024]{1,0:T(8,128)(2,1)S(1)}, bf16[16,1024]{1,0:T(8,128)(2,1)S(1)}, u32[]{:S(2)}, u32[]{:S(2)}) collective-permute-start(bf16[16,1024]{1,0:T(8,128)(2,1)S(1)} %get-tuple-element.79), channel_id=1, source_target_pairs={{0,56},{8,0},{16,8},{24,16},{32,24},{40,32},{48,40},{56,48},{64,12... | collective-permute-start | bytes 98312 | tf_op jit(solution)/shard_map/ppermute | solution.py:241
  197.0 10.6 %collective-permute-start.18 = (bf16[16,1024]{1,0:T(8,128)(2,1)S(1)}, bf16[16,1024]{1,0:T(8,128)(2,1)S(1)}, u32[]{:S(2)}, u32[]{:S(2)}) collective-permute-start(bf16[16,1024]{1,0:T(8,128)(2,1)S(1)} %get-tuple-element.80), channel_id=1, source_target_pairs={{0,48},{8,56},{16,0},{24,8},{32,16},{40,24},{48,32},{56,40},{64,11... | collective-permute-start | bytes 98312 | tf_op jit(solution)/shard_map/ppermute | solution.py:241
  198.3 9.6 %collective-permute-start.17 = (bf16[16,1024]{1,0:T(8,128)(2,1)S(1)}, bf16[16,1024]{1,0:T(8,128)(2,1)S(1)}, u32[]{:S(2)}, u32[]{:S(2)}) collective-permute-start(bf16[16,1024]{1,0:T(8,128)(2,1)S(1)} %get-tuple-element.81), channel_id=1, source_target_pairs={{0,40},{8,48},{16,56},{24,0},{32,8},{40,16},{48,24},{56,32},{64,10... | collective-permute-start | bytes 98312 | tf_op jit(solution)/shard_map/ppermute | solution.py:241
  200.8 7.1 %collective-permute-start.16 = (bf16[16,1024]{1,0:T(8,128)(2,1)S(1)}, bf16[16,1024]{1,0:T(8,128)(2,1)S(1)}, u32[]{:S(2)}, u32[]{:S(2)}) collective-permute-start(bf16[16,1024]{1,0:T(8,128)(2,1)S(1)} %get-tuple-element.82), channel_id=1, source_target_pairs={{0,32},{8,40},{16,48},{24,56},{32,0},{40,8},{48,16},{56,24},{64,96... | collective-permute-start | bytes 98312 | tf_op jit(solution)/shard_map/ppermute | solution.py:241
  203.3 6.1 %collective-permute-start.15 = (bf16[16,1024]{1,0:T(8,128)(2,1)S(1)}, bf16[16,1024]{1,0:T(8,128)(2,1)S(1)}, u32[]{:S(2)}, u32[]{:S(2)}) collective-permute-start(bf16[16,1024]{1,0:T(8,128)(2,1)S(1)} %get-tuple-element.83), channel_id=1, source_target_pairs={{0,24},{8,32},{16,40},{24,48},{32,56},{40,0},{48,8},{56,16},{64,88... | collective-permute-start | bytes 98312 | tf_op jit(solution)/shard_map/ppermute | solution.py:241
  205.9 6.9 %copy-start.9 = (bf16[16,1024]{1,0:T(8,128)(2,1)}, bf16[16,1024]{1,0:T(8,128)(2,1)S(1)}, u32[]{:S(2)}) copy-start(bf16[16,1024]{1,0:T(8,128)(2,1)S(1)} %collective-permute-done.19.refs_7_) | copy-start | bytes 98308
  205.9 5.0 %collective-permute-start.14 = (bf16[16,1024]{1,0:T(8,128)(2,1)S(1)}, bf16[16,1024]{1,0:T(8,128)(2,1)S(1)}, u32[]{:S(2)}, u32[]{:S(2)}) collective-permute-start(bf16[16,1024]{1,0:T(8,128)(2,1)S(1)} %get-tuple-element.84), channel_id=1, source_target_pairs={{0,16},{8,24},{16,32},{24,40},{32,48},{40,56},{48,0},{56,8},{64,80... | collective-permute-start | bytes 98312 | tf_op jit(solution)/shard_map/ppermute | solution.py:241
  207.6 5.2 %copy-start.10 = (bf16[16,1024]{1,0:T(8,128)(2,1)}, bf16[16,1024]{1,0:T(8,128)(2,1)S(1)}, u32[]{:S(2)}) copy-start(bf16[16,1024]{1,0:T(8,128)(2,1)S(1)} %collective-permute-done.18.refs_6_) | copy-start | bytes 98308
  207.6 5.1 %collective-permute-start.13 = (bf16[16,1024]{1,0:T(8,128)(2,1)S(1)}, bf16[16,1024]{1,0:T(8,128)(2,1)S(1)}, u32[]{:S(2)}, u32[]{:S(2)}) collective-permute-start(bf16[16,1024]{1,0:T(8,128)(2,1)S(1)} %get-tuple-element.85), channel_id=1, source_target_pairs={{0,8},{8,16},{16,24},{24,32},{32,40},{40,48},{48,56},{56,0},{64,72... | collective-permute-start | bytes 98312 | tf_op jit(solution)/shard_map/ppermute | solution.py:241
  207.9 4.9 %copy-start.11 = (bf16[16,1024]{1,0:T(8,128)(2,1)}, bf16[16,1024]{1,0:T(8,128)(2,1)S(1)}, u32[]{:S(2)}) copy-start(bf16[16,1024]{1,0:T(8,128)(2,1)S(1)} %collective-permute-done.17.refs_5_) | copy-start | bytes 98308
  207.9 4.9 %copy-start.12 = (bf16[16,1024]{1,0:T(8,128)(2,1)}, bf16[16,1024]{1,0:T(8,128)(2,1)S(1)}, u32[]{:S(2)}) copy-start(bf16[16,1024]{1,0:T(8,128)(2,1)S(1)} %collective-permute-done.16.refs_4_) | copy-start | bytes 98308
  (8 other events, 13.5 us)
Sparse Core Ops, SparseCore 0:
  69.8 47.9 all-gather.7
Sparse Core Ops, SparseCore 1:
  179.4 48.8 reduce-scatter.1

commit v4 on v3

--- a/solution.py
+++ b/solution.py
@@ -11,11 +11,11 @@
 BF16 = jnp.bfloat16
 LANES = 128
 COMPACT = 20
-VMEM_LIMIT = 56 * 1024 * 1024
-
-
-def params():
-    return pltpu.CompilerParams(vmem_limit_bytes=VMEM_LIMIT)
+MIB = 1024 * 1024
+
+
+def params(mib=8):
+    return pltpu.CompilerParams(vmem_limit_bytes=mib * MIB)
 
 
 def pieces(value):
@@ -200,6 +200,34 @@
         base_ref[...] = mass[pl.ds(start, part), :]
 
 
+def rows_kernel(turned_ref, in_ref, rows_ref, loss_ref):
+    count, part, wide = in_ref.shape
+    width = wide - LANES
+    for v in range(count):
+        got = in_ref[(v + turned_ref[0]) % count]
+        rows_ref[v * part : (v + 1) * part, :] = got[:, 0:width]
+        tail = got[:, width:wide].astype(F32)
+        loss_ref[v * part : (v + 1) * part, :] = jnp.broadcast_to(
+            tail[:, 0:1] + tail[:, 1:2] + tail[:, 2:3], (part, LANES)
+        )
+
+
+def stack_kernel(*refs):
+    out_ref = refs[-1]
+    part = refs[0].shape[0]
+    for k, ref in enumerate(refs[:-1]):
+        out_ref[k * part : (k + 1) * part, :] = ref[...]
+
+
+def arrange_kernel(behind_ref, *refs):
+    out_ref, held = refs[-2:]
+    near = refs[0].shape[0]
+    for k, ref in enumerate(refs[:-2]):
+        held[k * near : (k + 1) * near] = ref[...]
+    for t in range(out_ref.shape[0]):
+        out_ref[t] = held[behind_ref[t]]
+
+
 def fold(refs):
     wide = refs[0].shape[-1]
     total = refs[0][...].astype(F32)
@@ -247,7 +275,7 @@
 
 
 def exchange(
-    capacity, head_weight, incoming, compact_slot, whole_slot, own_slot, place, behind, by_ctx
+    capacity, ring, head_weight, incoming, compact_slot, whole_slot, own_slot, place, behind, *lines
 ):
     ctx_count = lax.axis_size("ctx")
     voc_count, held, part, _ = incoming.shape
@@ -256,6 +284,7 @@
     owned_blocks = voc_count * dev_blocks
     rows = ctx_count * part
     slots = ctx_count * capacity
+    wide = width + LANES
     smem = pl.BlockSpec(memory_space=pltpu.SMEM)
 
     weights = lax.all_gather(head_weight, "voc", axis=0, tiled=False)
@@ -271,7 +300,7 @@
             pltpu.VMEM((slots, part, LANES), F32),
             pltpu.VMEM((voc_count, part, LANES), F32),
         ],
-        compiler_params=params(),
+        compiler_params=params(20),
         cost_estimate=pl.CostEstimate(
             flops=4 * slots * part * LANES, bytes_accessed=6 * 1024 * 1024, transcendentals=0
         ),
@@ -279,7 +308,14 @@
     )(slot, incoming)
     target = target.reshape(ctx_count, capacity, part, LANES)
     arrived = lax.all_to_all(target, "ctx", 0, 0, tiled=True)
-    hidden_rows = by_ctx[behind].reshape(rows, width + LANES)
+    hidden_rows = pl.pallas_call(
+        arrange_kernel,
+        out_shape=jax.ShapeDtypeStruct((ctx_count, part, wide), BF16),
+        in_specs=[smem] + [pl.BlockSpec(memory_space=pltpu.VMEM)] * len(lines),
+        scratch_shapes=[pltpu.VMEM((ctx_count, part, wide), BF16)],
+        compiler_params=params(),
+        name="arrange_rows",
+    )(behind, *[line.reshape(ring, part, wide) for line in lines]).reshape(rows, wide)
     hidden_t = hidden_rows[:, :width].T
 
     logits, stats = pl.pallas_call(
@@ -299,7 +335,7 @@
             jax.ShapeDtypeStruct((ctx_count, 4, rows), F32),
         ),
         scratch_shapes=[pltpu.VMEM((rows, LANES), F32)] * 2,
-        compiler_params=params(),
+        compiler_params=params(16),
         cost_estimate=pl.CostEstimate(
             flops=2 * rows * width * cols * voc_count,
             bytes_accessed=18 * 1024 * 1024,
@@ -333,7 +369,7 @@
             jax.ShapeDtypeStruct((part, LANES), F32),
         ),
         scratch_shapes=[pltpu.VMEM((rows, LANES), F32)] * 4 + [pltpu.VMEM((rows, width), F32)],
-        compiler_params=params(),
+        compiler_params=params(28),
         cost_estimate=pl.CostEstimate(
             flops=4 * rows * width * cols * voc_count,
             bytes_accessed=30 * 1024 * 1024,
@@ -371,7 +407,7 @@
     outgoing = pl.pallas_call(
         teacher_kernel,
         out_shape=jax.ShapeDtypeStruct((voc_count, local_blocks + 1, part, LANES), BF16),
-        compiler_params=params(),
+        compiler_params=params(12),
         cost_estimate=pl.CostEstimate(
             flops=2 * rows_dev * local_blocks * LANES * LANES,
             bytes_accessed=6 * 1024 * 1024,
@@ -379,7 +415,13 @@
         ),
         name="teacher_map",
     )(teacher_logits, block_coeff)
-    near = jnp.stack(spread(mine, ring, False))
+    outgoing, mine = lax.optimization_barrier((outgoing, mine))
+    near = pl.pallas_call(
+        stack_kernel,
+        out_shape=jax.ShapeDtypeStruct((ring * part, wide), BF16),
+        compiler_params=params(),
+        name="stack_rows",
+    )(*spread(mine, ring, False))
     incoming = lax.all_to_all(outgoing, "voc", 0, 0, tiled=True)
 
     wanted = jnp.any(
@@ -400,14 +442,14 @@
     behind = (ctx_index // ring - place // ring) % (ctx_count // ring) * ring + (ctx_index - place) % ring
     ahead = (place // ring - ctx_index // ring) % (ctx_count // ring) * ring + (place - ctx_index) % ring
     place = jnp.concatenate([ahead, (own_half // 2)[None]]).astype(jnp.int32)
-    by_ctx = jnp.concatenate(spread(near, ring, True), axis=0)
+    lines = spread(near, ring, True)
     operands = lax.optimization_barrier(
-        (incoming, compact_slot, whole_slot, own_slot, place, behind, by_ctx)
+        (incoming, compact_slot, whole_slot, own_slot, place, behind, *lines)
     )
     dweight, dhidden, base = lax.cond(
         fits,
-        functools.partial(exchange, COMPACT),
-        functools.partial(exchange, owned_blocks),
+        functools.partial(exchange, COMPACT, ring),
+        functools.partial(exchange, owned_blocks, ring),
         head_weight,
         *operands,
     )
@@ -431,10 +473,21 @@
         name="finish_rows",
     )(*parts, base)
     all_done = lax.all_gather(done, "voc", axis=0, tiled=False)
-    all_done = jnp.where(ctx_index % 2 == 0, all_done, jnp.roll(all_done, half_groups, axis=0))
-    all_done = all_done.reshape(rows_dev, width + LANES)
-    grad_hidden = all_done[:, :width]
-    row_loss = jnp.sum(all_done[:, width : width + 3].astype(F32), axis=1)
+    turned = (ctx_index % 2 * half_groups).astype(jnp.int32)
+    grad_hidden, loss_tile = pl.pallas_call(
+        rows_kernel,
+        in_specs=[
+            pl.BlockSpec(memory_space=pltpu.SMEM),
+            pl.BlockSpec(memory_space=pltpu.VMEM),
+        ],
+        out_shape=(
+            jax.ShapeDtypeStruct((rows_dev, width), BF16),
+            jax.ShapeDtypeStruct((rows_dev, LANES), F32),
+        ),
+        compiler_params=params(),
+        name="own_rows",
+    )(turned[None], all_done)
+    row_loss = loss_tile[:, 0]
     return (grad_hidden, grad_weight, row_loss)
 
 

time: 245 us -> 233 us (0.951)
  Pallas kernels: 46.9 us -> 36.2 us
  starting transfers between devices: 58.9 us -> 54.5 us
  waiting for transfers between devices: 80 us -> 83.3 us
    cond x5 -> x9, local copies, waits for them, and re-layouts: 2.04 us -> 13.4 us
    pallas_call x1, Pallas kernels: 11.9 us -> 7.58 us  [exchange(): pl.pallas_call(logits_kernel, grid=(voc_count,), in_specs=[pl.BlockSpec((...]
    unnamed x34 -> x10, local copies, waits for them, and re-layouts: 7.12 us -> 3.3 us
  transfers between devices with their start and end apart: 25 -> 25, of which waited for: 12 -> 15; matrix products, arithmetic and copies ran while one was open for 8% -> 2% of each run, Pallas kernels for 12% -> 7%
where the time goes in v4:
time: 233 us; the launch traced here: 232 us
  waiting for transfers between devices  83.3 us (36%)
  starting transfers between devices  54.5 us (23%)
  Pallas kernels  36.2 us (16%)
  local copies, waits for them, and re-layouts  20.8 us (9%)
  blocking collectives  17.3 us (7%)
  between operations  16.3 us (7%)
  other arithmetic  4.1 us (2%)
    all_gather x1, waiting for transfers between devices, exchange(): weights = lax.all_gather(head_weight, 'voc', axis=0, tiled=False)  36.1 us
    ppermute x20, starting transfers between devices, shifted(): return lax.ppermute(value, 'ctx', pairs)  35.5 us
    ppermute x20, waiting for transfers between devices, shifted(): return lax.ppermute(value, 'ctx', pairs)  26.4 us
    all_gather x1, blocking collectives, local(): all_done = lax.all_gather(done, 'voc', axis=0, tiled=False)  17.3 us
    pallas_call x1, Pallas kernels, exchange(): pl.pallas_call(grad_kernel, grid=(voc_count,), in_specs=[smem, smem, whol...  15.8 us
    cond x9, local copies, waits for them, and re-layouts  13.4 us
    all_to_all x1, waiting for transfers between devices, exchange(): arrived = lax.all_to_all(target, 'ctx', 0, 0, tiled=True)  9.32 us
    all_to_all x1, waiting for transfers between devices, exchange(): all_stats = lax.all_to_all(stats, 'ctx', 0, 0, tiled=True)  9.05 us
  transfers between devices with their start and end apart: 25, of which 15 were waited for; matrix products, arithmetic and copies ran while one was open for 2% of the time, Pallas kernels for 7%

profile of v4, /device:TPU:1, one launch (start us, length us, event | category | flops | bytes accessed | tf_op | source)
XLA Modules:
  0.0 232.5 jit_solution(5909289515620295592)
XLA Ops:
  12.2 5.2 %teacher_map.1 = bf16[8,65,16,128]{3,2,1,0:T(8,128)(2,1)} custom-call(bf16[128,8192]{1,0:T(8,128)(2,1)S(1)} %copy-done.3, bf16[64,128,128]{2,1,0:T(8,128)(2,1)S(1)} %copy-done.4), custom_call_target="tpu_custom_call" | custom-call | flops 268435456 | bytes 6291456 | tf_op jit(solution)/shard_map/teacher_map/pallas_call | solution.py:407
  17.4 6.9 %all-to-all-start.4 = ((bf16[8,65,16,128]{3,2,1,0:T(8,128)(2,1)}), bf16[8,65,16,128]{3,2,1,0:T(8,128)(2,1)S(1)}, u32[]{:S(2)}, u32[]{:S(2)}) async-start(bf16[8,65,16,128]{3,2,1,0:T(8,128)(2,1)} %teacher_map.1), calls=%async_computation.4 | async-start | bytes 4259840 | tf_op jit(solution)/shard_map/all_to_all | solution.py:425
  24.3 4.8 %collective-permute-start.6 = (bf16[16,1024]{1,0:T(8,128)(2,1)S(1)}, bf16[16,1024]{1,0:T(8,128)(2,1)S(1)}, u32[]{:S(2)}, u32[]{:S(2)}) collective-permute-start(bf16[16,1024]{1,0:T(8,128)(2,1)S(1)} %pad_maximum_fusion.refs_0_), channel_id=1, source_target_pairs={{0,56},{8,0},{16,8},{24,16},{32,24},{40,32},{48,40},{56,48},{64,12... | collective-permute-start | bytes 98312 | tf_op jit(solution)/shard_map/ppermute | solution.py:269
  30.7 4.5 %collective-permute-start.3 = (bf16[16,1024]{1,0:T(8,128)(2,1)S(1)}, bf16[16,1024]{1,0:T(8,128)(2,1)S(1)}, u32[]{:S(2)}, u32[]{:S(2)}) collective-permute-start(bf16[16,1024]{1,0:T(8,128)(2,1)S(1)} %pad_maximum_fusion.refs_0_), channel_id=1, source_target_pairs={{0,32},{8,40},{16,48},{24,56},{32,0},{40,8},{48,16},{56,24},{64,96... | collective-permute-start | bytes 98312 | tf_op jit(solution)/shard_map/ppermute | solution.py:269
  36.0 2.2 collective-permute-start.1
  42.7 2.6 %collective-permute-start.9 = (bf16[128,1024]{1,0:T(8,128)(2,1)S(1)}, bf16[128,1024]{1,0:T(8,128)(2,1)S(1)}, u32[]{:S(2)}, u32[]{:S(2)}) collective-permute-start(bf16[128,1024]{1,0:T(8,128)(2,1)S(1)} %stack_rows.1), channel_id=1, source_target_pairs={{0,192},{8,200},{16,208},{24,216},{32,224},{40,232},{48,240},{56,2... | collective-permute-start | bytes 786440 | tf_op jit(solution)/shard_map/ppermute | solution.py:269
  47.8 2.3 gather_fusion
  52.0 8.2 %collective-permute-done.7 = bf16[128,1024]{1,0:T(8,128)(2,1)S(1)} collective-permute-done((bf16[128,1024]{1,0:T(8,128)(2,1)S(1)}, bf16[128,1024]{1,0:T(8,128)(2,1)S(1)}, u32[]{:S(2)}, u32[]{:S(2)}) %collective-permute-start.7) | collective-permute-done | bytes 262176 | tf_op jit(solution)/shard_map/ppermute | solution.py:269
  60.2 110.6 %conditional.1 = ((bf16[8,896,512]{2,1,0:T(8,128)(2,1)}, bf16[32,16,1024]{2,1,0:T(8,128)(2,1)S(1)}, f32[16,128]{1,0:T(8,128)S(1)})) conditional(s32[]{:T(128)} %convert_element_type.21, (bf16[128,1024]{1,0:T(8,128)(2,1)S(1)}, bf16[128,1024]{1,0:T(8,128)(2,1)S(1)}, bf16[128,1024]{1,0:T(8,128)(2,1)S(1)}, bf16[128,1024]{1,0:T(8,128)(2,1)S(1)}, ...), branch_computations={%region_4.5_spmd, %region_5.6_spmd} | conditional | flops 11282677760 | bytes 241041664 | solution.py:449
  61.0 5.7 %collect_targets.3 = (bf16[640,16,128]{2,1,0:T(8,128)(2,1)}, f32[16,128]{1,0:T(8,128)S(1)}) custom-call(s32[512]{0:T(512)S(1)} %get-tuple-element.62.slot_ref, bf16[8,65,16,128]{3,2,1,0:T(8,128)(2,1)S(1)} %get-tuple-element.63.in_ref), custom_call_target="tpu_custom_call" | custom-call | flops 5242880 | bytes 6291456 | tf_op jit(solution)/shard_map/cond/branch_1_fun/collect_targets/pallas_call | solution.py:292
  66.7 5.2 %all-to-all-start.3 = ((bf16[32,20,16,128]{3,2,1,0:T(8,128)(2,1)}), bf16[32,20,16,128]{3,2,1,0:T(8,128)(2,1)}, u32[]{:S(2)}, u32[]{:S(2)}) async-start(bf16[32,20,16,128]{3,2,1,0:T(8,128)(2,1)} %bitcast.14), calls=%async_computation.3 | async-start | bytes 5242880 | tf_op jit(solution)/shard_map/cond/branch_1_fun/all_to_all | solution.py:310
  72.6 36.1 %all-gather.8.cloned.1.call-done = bf16[7168,512]{1,0:T(8,128)(2,1)} async-done(((bf16[896,512]{1,0:T(8,128)(2,1)}), bf16[7168,512]{1,0:T(8,128)(2,1)}) %all-gather.8.cloned.1.call-update) | async-done | bytes 7340048 | tf_op jit(solution)/shard_map/cond/branch_1_fun/all_gather | solution.py:290
  108.7 3.1 %copy-done.7 = bf16[7168,512]{1,0:T(8,128)(2,1)S(1)} copy-done((bf16[7168,512]{1,0:T(8,128)(2,1)S(1)}, bf16[7168,512]{1,0:T(8,128)(2,1)}, u32[]{:S(2)}) %copy-start.7) | copy-done | bytes 7340056 | tf_op jit(solution)/shard_map/cond
  111.8 7.6 %student_logits.3 = (f32[8,512,512]{2,1,0:T(8,128)S(1)}, f32[32,4,512]{2,1,0:T(4,128)}) custom-call(bf16[512,1024]{1,0:T(8,128)(2,1)S(1)} %bitcast.32, bf16[8,896,512]{2,1,0:T(8,128)(2,1)S(1)} %bitcast.41, f32[16,128]{1,0:T(8,128)S(1)} %get-tuple-element.64.mass_ref), custom_call_target="tpu_custom_call" | custom-call | flops 3758096384 | bytes 18874368 | tf_op jit(solution)/shard_map/cond/branch_1_fun/student_logits/pallas_call | solution.py:321
  119.4 3.3 %copy-done.11 = f32[8,512,512]{2,1,0:T(8,128)} copy-done((f32[8,512,512]{2,1,0:T(8,128)}, f32[8,512,512]{2,1,0:T(8,128)S(1)}, u32[]{:S(2)}) %copy-start.11) | copy-done | bytes 8388632 | tf_op jit(solution)/shard_map/cond
  122.7 9.3 %all-to-all-done.3.target_ref = bf16[32,20,16,128]{3,2,1,0:T(8,128)(2,1)} async-done(((bf16[32,20,16,128]{3,2,1,0:T(8,128)(2,1)}), bf16[32,20,16,128]{3,2,1,0:T(8,128)(2,1)}, u32[]{:S(2)}, u32[]{:S(2)}) %all-to-all-start.3) | async-done | bytes 2621472 | tf_op jit(solution)/shard_map/cond/branch_1_fun/all_to_all | solution.py:310
  132.0 6.9 %all-to-all-start.2 = ((f32[32,4,512]{2,1,0:T(4,128)}), f32[32,4,512]{2,1,0:T(4,128)S(1)}, u32[]{:S(2)}, u32[]{:S(2)}) async-start(f32[32,4,512]{2,1,0:T(4,128)} %get-tuple-element.65), calls=%async_computation.2 | async-start | bytes 524288 | tf_op jit(solution)/shard_map/cond/branch_1_fun/all_to_all | solution.py:346
  139.6 9.0 %all-to-all-done.2.stats_ref = f32[32,4,512]{2,1,0:T(4,128)S(1)} async-done(((f32[32,4,512]{2,1,0:T(4,128)}), f32[32,4,512]{2,1,0:T(4,128)S(1)}, u32[]{:S(2)}, u32[]{:S(2)}) %all-to-all-start.2) | async-done | bytes 262176 | tf_op jit(solution)/shard_map/cond/branch_1_fun/all_to_all | solution.py:346
  148.6 3.1 %copy-done.8 = bf16[7168,512]{1,0:T(8,128)(2,1)S(1)} copy-done((bf16[7168,512]{1,0:T(8,128)(2,1)S(1)}, bf16[7168,512]{1,0:T(8,128)(2,1)}, u32[]{:S(2)}) %copy-start.8) | copy-done | bytes 7340056 | tf_op jit(solution)/shard_map/cond
  151.7 3.4 %copy-done.12 = f32[8,512,512]{2,1,0:T(8,128)S(1)} copy-done((f32[8,512,512]{2,1,0:T(8,128)S(1)}, f32[8,512,512]{2,1,0:T(8,128)}, u32[]{:S(2)}) %copy-start.12) | copy-done | bytes 8388632 | tf_op jit(solution)/shard_map/cond
  155.1 15.8 %grads.3 = (bf16[8,896,512]{2,1,0:T(8,128)(2,1)}, bf16[32,16,1024]{2,1,0:T(8,128)(2,1)S(1)}, f32[16,128]{1,0:T(8,128)S(1)}) custom-call(s32[33]{0:T(128)S(1)} %get-tuple-element.54.place_ref, s32[32]{0:T(128)S(1)} %get-tuple-element.55.slot_ref, f32[32,4,512]{2,1,0:T(4,128)S(1)} %all-to-all-done.2.stats_ref, f32[8,512,512]{2,1,0:T(8,128)S(1)} %copy-done.12, ...), custom_call_target="tpu_custom_call" | custom-call | flops 7516192768 | bytes 31457280 | tf_op jit(solution)/shard_map/cond/branch_1_fun/grads/pallas_call | solution.py:348
  171.5 2.0 collective-permute-start.11
  175.0 3.3 %collective-permute-done.11.refs_2_ = bf16[128,1024]{1,0:T(8,128)(2,1)S(1)} collective-permute-done((bf16[128,1024]{1,0:T(8,128)(2,1)S(1)}, bf16[128,1024]{1,0:T(8,128)(2,1)S(1)}, u32[]{:S(2)}, u32[]{:S(2)}) %collective-permute-start.11) | collective-permute-done | bytes 262176 | tf_op jit(solution)/shard_map/ppermute | solution.py:269
  178.3 5.4 %collective-permute-done.12.refs_3_ = bf16[128,1024]{1,0:T(8,128)(2,1)S(1)} collective-permute-done((bf16[128,1024]{1,0:T(8,128)(2,1)S(1)}, bf16[128,1024]{1,0:T(8,128)(2,1)S(1)}, u32[]{:S(2)}, u32[]{:S(2)}) %collective-permute-start.12) | collective-permute-done | bytes 262176 | tf_op jit(solution)/shard_map/ppermute | solution.py:269
  184.1 2.8 %collective-permute-start.19 = (bf16[16,1024]{1,0:T(8,128)(2,1)S(1)}, bf16[16,1024]{1,0:T(8,128)(2,1)S(1)}, u32[]{:S(2)}, u32[]{:S(2)}) collective-permute-start(bf16[16,1024]{1,0:T(8,128)(2,1)S(1)} %get-tuple-element.109), channel_id=1, source_target_pairs={{0,56},{8,0},{16,8},{24,16},{32,24},{40,32},{48,40},{56,48},{64,12... | collective-permute-start | bytes 98312 | tf_op jit(solution)/shard_map/ppermute | solution.py:269
  187.7 2.9 %collective-permute-start.17 = (bf16[16,1024]{1,0:T(8,128)(2,1)S(1)}, bf16[16,1024]{1,0:T(8,128)(2,1)S(1)}, u32[]{:S(2)}, u32[]{:S(2)}) collective-permute-start(bf16[16,1024]{1,0:T(8,128)(2,1)S(1)} %get-tuple-element.111), channel_id=1, source_target_pairs={{0,40},{8,48},{16,56},{24,0},{32,8},{40,16},{48,24},{56,32},{64,10... | collective-permute-start | bytes 98312 | tf_op jit(solution)/shard_map/ppermute | solution.py:269
  190.7 2.3 %collective-permute-start.16 = (bf16[16,1024]{1,0:T(8,128)(2,1)S(1)}, bf16[16,1024]{1,0:T(8,128)(2,1)S(1)}, u32[]{:S(2)}, u32[]{:S(2)}) collective-permute-start(bf16[16,1024]{1,0:T(8,128)(2,1)S(1)} %get-tuple-element.112), channel_id=1, source_target_pairs={{0,32},{8,40},{16,48},{24,56},{32,0},{40,8},{48,16},{56,24},{64,96... | collective-permute-start | bytes 98312 | tf_op jit(solution)/shard_map/ppermute | solution.py:269
  193.0 2.5 %collective-permute-start.15 = (bf16[16,1024]{1,0:T(8,128)(2,1)S(1)}, bf16[16,1024]{1,0:T(8,128)(2,1)S(1)}, u32[]{:S(2)}, u32[]{:S(2)}) collective-permute-start(bf16[16,1024]{1,0:T(8,128)(2,1)S(1)} %get-tuple-element.113), channel_id=1, source_target_pairs={{0,24},{8,32},{16,40},{24,48},{32,56},{40,0},{48,8},{56,16},{64,88... | collective-permute-start | bytes 98312 | tf_op jit(solution)/shard_map/ppermute | solution.py:269
  195.5 1.9 collective-permute-start.14
  200.5 2.0 collective-permute-done.13.refs_1_
  202.6 17.3 %all-gather.2 = bf16[128,1024]{1,0:T(8,128)(2,1)S(1)} all-gather(bf16[16,1024]{1,0:T(8,128)(2,1)S(1)} %finish_rows.1), channel_id=4, replica_groups=mesh['ctx'=32,'voc'=8] {'voc'}, dimensions={0}, use_global_device_ids=true | all-gather | bytes 294912 | tf_op jit(solution)/shard_map/all_gather | solution.py:475
  222.4 2.7 %bitcast_convert_fusion = f32[896,512]{1,0:T(8,128)} fusion(bf16[1,896,512]{2,1,0:T(8,128)(2,1)} %reduce-scatter.2.cloned.1.call-done), kind=kLoop, calls=%fused_computation.3 | loop fusion | flops 458752 | bytes 2752512 | tf_op jit(solution)/shard_map/convert_element_type | solution.py:457
  (73 shorter events, 25.9 us)
Async XLA Ops:
  9.0 1.6 copy-start.3
  17.4 17.8 %copy-start.13 = (s32[512]{0:T(512)S(1)}, s32[512]{0:T(512)}, u32[]{:S(2)}) copy-start(s32[512]{0:T(512)} %param.13) | copy-start | bytes 6148
  17.4 42.8 %all-to-all-start.4 = ((bf16[8,65,16,128]{3,2,1,0:T(8,128)(2,1)}), bf16[8,65,16,128]{3,2,1,0:T(8,128)(2,1)S(1)}, u32[]{:S(2)}, u32[]{:S(2)}) async-start(bf16[8,65,16,128]{3,2,1,0:T(8,128)(2,1)} %teacher_map.1), calls=%async_computation.4 | async-start | bytes 4259840 | tf_op jit(solution)/shard_map/all_to_all | solution.py:425
  24.3 11.7 %collective-permute-start.6 = (bf16[16,1024]{1,0:T(8,128)(2,1)S(1)}, bf16[16,1024]{1,0:T(8,128)(2,1)S(1)}, u32[]{:S(2)}, u32[]{:S(2)}) collective-permute-start(bf16[16,1024]{1,0:T(8,128)(2,1)S(1)} %pad_maximum_fusion.refs_0_), channel_id=1, source_target_pairs={{0,56},{8,0},{16,8},{24,16},{32,24},{40,32},{48,40},{56,48},{64,12... | collective-permute-start | bytes 98312 | tf_op jit(solution)/shard_map/ppermute | solution.py:269
  29.1 9.0 %collective-permute-start.5 = (bf16[16,1024]{1,0:T(8,128)(2,1)S(1)}, bf16[16,1024]{1,0:T(8,128)(2,1)S(1)}, u32[]{:S(2)}, u32[]{:S(2)}) collective-permute-start(bf16[16,1024]{1,0:T(8,128)(2,1)S(1)} %pad_maximum_fusion.refs_0_), channel_id=1, source_target_pairs={{0,48},{8,56},{16,0},{24,8},{32,16},{40,24},{48,32},{56,40},{64,11... | collective-permute-start | bytes 98312 | tf_op jit(solution)/shard_map/ppermute | solution.py:269
  30.3 9.3 %collective-permute-start.4 = (bf16[16,1024]{1,0:T(8,128)(2,1)S(1)}, bf16[16,1024]{1,0:T(8,128)(2,1)S(1)}, u32[]{:S(2)}, u32[]{:S(2)}) collective-permute-start(bf16[16,1024]{1,0:T(8,128)(2,1)S(1)} %pad_maximum_fusion.refs_0_), channel_id=1, source_target_pairs={{0,40},{8,48},{16,56},{24,0},{32,8},{40,16},{48,24},{56,32},{64,10... | collective-permute-start | bytes 98312 | tf_op jit(solution)/shard_map/ppermute | solution.py:269
  30.7 8.9 %collective-permute-start.3 = (bf16[16,1024]{1,0:T(8,128)(2,1)S(1)}, bf16[16,1024]{1,0:T(8,128)(2,1)S(1)}, u32[]{:S(2)}, u32[]{:S(2)}) collective-permute-start(bf16[16,1024]{1,0:T(8,128)(2,1)S(1)} %pad_maximum_fusion.refs_0_), channel_id=1, source_target_pairs={{0,32},{8,40},{16,48},{24,56},{32,0},{40,8},{48,16},{56,24},{64,96... | collective-permute-start | bytes 98312 | tf_op jit(solution)/shard_map/ppermute | solution.py:269
  35.2 5.8 %collective-permute-start.2 = (bf16[16,1024]{1,0:T(8,128)(2,1)S(1)}, bf16[16,1024]{1,0:T(8,128)(2,1)S(1)}, u32[]{:S(2)}, u32[]{:S(2)}) collective-permute-start(bf16[16,1024]{1,0:T(8,128)(2,1)S(1)} %pad_maximum_fusion.refs_0_), channel_id=1, source_target_pairs={{0,24},{8,32},{16,40},{24,48},{32,56},{40,0},{48,8},{56,16},{64,88... | collective-permute-start | bytes 98312 | tf_op jit(solution)/shard_map/ppermute | solution.py:269
  36.0 5.4 %collective-permute-start.1 = (bf16[16,1024]{1,0:T(8,128)(2,1)S(1)}, bf16[16,1024]{1,0:T(8,128)(2,1)S(1)}, u32[]{:S(2)}, u32[]{:S(2)}) collective-permute-start(bf16[16,1024]{1,0:T(8,128)(2,1)S(1)} %pad_maximum_fusion.refs_0_), channel_id=1, source_target_pairs={{0,16},{8,24},{16,32},{24,40},{32,48},{40,56},{48,0},{56,8},{64,80... | collective-permute-start | bytes 98312 | tf_op jit(solution)/shard_map/ppermute | solution.py:269
  38.2 4.5 %collective-permute-start = (bf16[16,1024]{1,0:T(8,128)(2,1)S(1)}, bf16[16,1024]{1,0:T(8,128)(2,1)S(1)}, u32[]{:S(2)}, u32[]{:S(2)}) collective-permute-start(bf16[16,1024]{1,0:T(8,128)(2,1)S(1)} %pad_maximum_fusion.refs_0_), channel_id=1, source_target_pairs={{0,8},{8,16},{16,24},{24,32},{32,40},{40,48},{48,56},{56,0},{64,72... | collective-permute-start | bytes 98312 | tf_op jit(solution)/shard_map/ppermute | solution.py:269
  42.7 7.8 %collective-permute-start.9 = (bf16[128,1024]{1,0:T(8,128)(2,1)S(1)}, bf16[128,1024]{1,0:T(8,128)(2,1)S(1)}, u32[]{:S(2)}, u32[]{:S(2)}) collective-permute-start(bf16[128,1024]{1,0:T(8,128)(2,1)S(1)} %stack_rows.1), channel_id=1, source_target_pairs={{0,192},{8,200},{16,208},{24,216},{32,224},{40,232},{48,240},{56,2... | collective-permute-start | bytes 786440 | tf_op jit(solution)/shard_map/ppermute | solution.py:269
  45.2 6.8 %collective-permute-start.8 = (bf16[128,1024]{1,0:T(8,128)(2,1)S(1)}, bf16[128,1024]{1,0:T(8,128)(2,1)S(1)}, u32[]{:S(2)}, u32[]{:S(2)}) collective-permute-start(bf16[128,1024]{1,0:T(8,128)(2,1)S(1)} %stack_rows.1), channel_id=1, source_target_pairs={{0,128},{8,136},{16,144},{24,152},{32,160},{40,168},{48,176},{56,1... | collective-permute-start | bytes 786440 | tf_op jit(solution)/shard_map/ppermute | solution.py:269
  45.7 14.5 %collective-permute-start.7 = (bf16[128,1024]{1,0:T(8,128)(2,1)S(1)}, bf16[128,1024]{1,0:T(8,128)(2,1)S(1)}, u32[]{:S(2)}, u32[]{:S(2)}) collective-permute-start(bf16[128,1024]{1,0:T(8,128)(2,1)S(1)} %stack_rows.1), channel_id=1, source_target_pairs={{0,64},{8,72},{16,80},{24,88},{32,96},{40,104},{48,112},{56,120},{... | collective-permute-start | bytes 786440 | tf_op jit(solution)/shard_map/ppermute | solution.py:269
  60.2 48.5 %all-gather.8.cloned.1.call-start = ((), (), s32[]{:S(2)}) async-start(), calls=%async_computation.7 | async-start | bytes 8257536 | tf_op jit(solution)/shard_map/cond/branch_1_fun/all_gather | solution.py:290
  66.7 65.3 %all-to-all-start.3 = ((bf16[32,20,16,128]{3,2,1,0:T(8,128)(2,1)}), bf16[32,20,16,128]{3,2,1,0:T(8,128)(2,1)}, u32[]{:S(2)}, u32[]{:S(2)}) async-start(bf16[32,20,16,128]{3,2,1,0:T(8,128)(2,1)} %bitcast.14), calls=%async_computation.3 | async-start | bytes 5242880 | tf_op jit(solution)/shard_map/cond/branch_1_fun/all_to_all | solution.py:310
  108.7 3.1 %copy-start.7 = (bf16[7168,512]{1,0:T(8,128)(2,1)S(1)}, bf16[7168,512]{1,0:T(8,128)(2,1)}, u32[]{:S(2)}) copy-start(bf16[7168,512]{1,0:T(8,128)(2,1)} %all-gather.8.cloned.1.call-done) | copy-start | bytes 22020100 | tf_op jit(solution)/shard_map/cond
  119.4 3.3 %copy-start.11 = (f32[8,512,512]{2,1,0:T(8,128)}, f32[8,512,512]{2,1,0:T(8,128)S(1)}, u32[]{:S(2)}) copy-start(f32[8,512,512]{2,1,0:T(8,128)S(1)} %get-tuple-element.66.logits_ref) | copy-start | bytes 25165828 | tf_op jit(solution)/shard_map/cond
  132.0 16.6 %all-to-all-start.2 = ((f32[32,4,512]{2,1,0:T(4,128)}), f32[32,4,512]{2,1,0:T(4,128)S(1)}, u32[]{:S(2)}, u32[]{:S(2)}) async-start(f32[32,4,512]{2,1,0:T(4,128)} %get-tuple-element.65), calls=%async_computation.2 | async-start | bytes 524288 | tf_op jit(solution)/shard_map/cond/branch_1_fun/all_to_all | solution.py:346
  148.6 3.1 %copy-start.8 = (bf16[7168,512]{1,0:T(8,128)(2,1)S(1)}, bf16[7168,512]{1,0:T(8,128)(2,1)}, u32[]{:S(2)}) copy-start(bf16[7168,512]{1,0:T(8,128)(2,1)} %all-gather.8.cloned.1.call-done) | copy-start | bytes 22020100 | tf_op jit(solution)/shard_map/cond
  151.7 3.4 %copy-start.12 = (f32[8,512,512]{2,1,0:T(8,128)S(1)}, f32[8,512,512]{2,1,0:T(8,128)}, u32[]{:S(2)}) copy-start(f32[8,512,512]{2,1,0:T(8,128)} %copy-done.11) | copy-start | bytes 25165828 | tf_op jit(solution)/shard_map/cond
  170.8 51.5 %reduce-scatter.2.cloned.1.call-start = ((), (), s32[]{:S(2)}) async-start(), calls=%async_computation.8 | async-start | bytes 8257536 | tf_op jit(solution)/shard_map/reduce_scatter | solution.py:456
  171.5 6.8 %collective-permute-start.11 = (bf16[128,1024]{1,0:T(8,128)(2,1)S(1)}, bf16[128,1024]{1,0:T(8,128)(2,1)S(1)}, u32[]{:S(2)}, u32[]{:S(2)}) collective-permute-start(bf16[128,1024]{1,0:T(8,128)(2,1)S(1)} %bitcast.53), channel_id=1, source_target_pairs={{0,128},{8,136},{16,144},{24,152},{32,160},{40,168},{48,176},{56,1... | collective-permute-start | bytes 786440 | tf_op jit(solution)/shard_map/ppermute | solution.py:269
  173.5 10.2 %collective-permute-start.12 = (bf16[128,1024]{1,0:T(8,128)(2,1)S(1)}, bf16[128,1024]{1,0:T(8,128)(2,1)S(1)}, u32[]{:S(2)}, u32[]{:S(2)}) collective-permute-start(bf16[128,1024]{1,0:T(8,128)(2,1)S(1)} %bitcast.52), channel_id=1, source_target_pairs={{0,192},{8,200},{16,208},{24,216},{32,224},{40,232},{48,240},{56,2... | collective-permute-start | bytes 786440 | tf_op jit(solution)/shard_map/ppermute | solution.py:269
  174.5 9.3 %collective-permute-start.10 = (bf16[128,1024]{1,0:T(8,128)(2,1)S(1)}, bf16[128,1024]{1,0:T(8,128)(2,1)S(1)}, u32[]{:S(2)}, u32[]{:S(2)}) collective-permute-start(bf16[128,1024]{1,0:T(8,128)(2,1)S(1)} %bitcast.51), channel_id=1, source_target_pairs={{0,64},{8,72},{16,80},{24,88},{32,96},{40,104},{48,112},{56,120},{... | collective-permute-start | bytes 786440 | tf_op jit(solution)/shard_map/ppermute | solution.py:269
  183.7 41.3 %copy-start.1 = (bf16[128,896]{1,0:T(8,128)(2,1)S(1)}, bf16[128,896]{1,0:T(8,128)(2,1)}, u32[]{:S(2)}) copy-start(bf16[128,896]{1,0:T(8,128)(2,1)} %param.8) | copy-start | bytes 688132
  184.1 11.4 %collective-permute-start.19 = (bf16[16,1024]{1,0:T(8,128)(2,1)S(1)}, bf16[16,1024]{1,0:T(8,128)(2,1)S(1)}, u32[]{:S(2)}, u32[]{:S(2)}) collective-permute-start(bf16[16,1024]{1,0:T(8,128)(2,1)S(1)} %get-tuple-element.109), channel_id=1, source_target_pairs={{0,56},{8,0},{16,8},{24,16},{32,24},{40,32},{48,40},{56,48},{64,12... | collective-permute-start | bytes 98312 | tf_op jit(solution)/shard_map/ppermute | solution.py:269
  186.9 10.6 %collective-permute-start.18 = (bf16[16,1024]{1,0:T(8,128)(2,1)S(1)}, bf16[16,1024]{1,0:T(8,128)(2,1)S(1)}, u32[]{:S(2)}, u32[]{:S(2)}) collective-permute-start(bf16[16,1024]{1,0:T(8,128)(2,1)S(1)} %get-tuple-element.110), channel_id=1, source_target_pairs={{0,48},{8,56},{16,0},{24,8},{32,16},{40,24},{48,32},{56,40},{64,11... | collective-permute-start | bytes 98312 | tf_op jit(solution)/shard_map/ppermute | solution.py:269
  187.7 10.1 %collective-permute-start.17 = (bf16[16,1024]{1,0:T(8,128)(2,1)S(1)}, bf16[16,1024]{1,0:T(8,128)(2,1)S(1)}, u32[]{:S(2)}, u32[]{:S(2)}) collective-permute-start(bf16[16,1024]{1,0:T(8,128)(2,1)S(1)} %get-tuple-element.111), channel_id=1, source_target_pairs={{0,40},{8,48},{16,56},{24,0},{32,8},{40,16},{48,24},{56,32},{64,10... | collective-permute-start | bytes 98312 | tf_op jit(solution)/shard_map/ppermute | solution.py:269
  190.7 7.2 %collective-permute-start.16 = (bf16[16,1024]{1,0:T(8,128)(2,1)S(1)}, bf16[16,1024]{1,0:T(8,128)(2,1)S(1)}, u32[]{:S(2)}, u32[]{:S(2)}) collective-permute-start(bf16[16,1024]{1,0:T(8,128)(2,1)S(1)} %get-tuple-element.112), channel_id=1, source_target_pairs={{0,32},{8,40},{16,48},{24,56},{32,0},{40,8},{48,16},{56,24},{64,96... | collective-permute-start | bytes 98312 | tf_op jit(solution)/shard_map/ppermute | solution.py:269
  193.0 6.0 %collective-permute-start.15 = (bf16[16,1024]{1,0:T(8,128)(2,1)S(1)}, bf16[16,1024]{1,0:T(8,128)(2,1)S(1)}, u32[]{:S(2)}, u32[]{:S(2)}) collective-permute-start(bf16[16,1024]{1,0:T(8,128)(2,1)S(1)} %get-tuple-element.113), channel_id=1, source_target_pairs={{0,24},{8,32},{16,40},{24,48},{32,56},{40,0},{48,8},{56,16},{64,88... | collective-permute-start | bytes 98312 | tf_op jit(solution)/shard_map/ppermute | solution.py:269
  195.5 5.0 %collective-permute-start.14 = (bf16[16,1024]{1,0:T(8,128)(2,1)S(1)}, bf16[16,1024]{1,0:T(8,128)(2,1)S(1)}, u32[]{:S(2)}, u32[]{:S(2)}) collective-permute-start(bf16[16,1024]{1,0:T(8,128)(2,1)S(1)} %get-tuple-element.114), channel_id=1, source_target_pairs={{0,16},{8,24},{16,32},{24,40},{32,48},{40,56},{48,0},{56,8},{64,80... | collective-permute-start | bytes 98312 | tf_op jit(solution)/shard_map/ppermute | solution.py:269
  197.4 5.0 %collective-permute-start.13 = (bf16[16,1024]{1,0:T(8,128)(2,1)S(1)}, bf16[16,1024]{1,0:T(8,128)(2,1)S(1)}, u32[]{:S(2)}, u32[]{:S(2)}) collective-permute-start(bf16[16,1024]{1,0:T(8,128)(2,1)S(1)} %get-tuple-element.115), channel_id=1, source_target_pairs={{0,8},{8,16},{16,24},{24,32},{32,40},{40,48},{48,56},{56,0},{64,72... | collective-permute-start | bytes 98312 | tf_op jit(solution)/shard_map/ppermute | solution.py:269
  (2 other events, 2.5 us)
Sparse Core Ops, SparseCore 0:
  62.9 45.7 all-gather.7
Sparse Core Ops, SparseCore 1:
  173.8 48.5 reduce-scatter.1

commit v5 on v4

--- a/solution.py
+++ b/solution.py
@@ -369,7 +369,7 @@
             jax.ShapeDtypeStruct((part, LANES), F32),
         ),
         scratch_shapes=[pltpu.VMEM((rows, LANES), F32)] * 4 + [pltpu.VMEM((rows, width), F32)],
-        compiler_params=params(28),
+        compiler_params=params(56),
         cost_estimate=pl.CostEstimate(
             flops=4 * rows * width * cols * voc_count,
             bytes_accessed=30 * 1024 * 1024,
@@ -407,7 +407,7 @@
     outgoing = pl.pallas_call(
         teacher_kernel,
         out_shape=jax.ShapeDtypeStruct((voc_count, local_blocks + 1, part, LANES), BF16),
-        compiler_params=params(12),
+        compiler_params=params(56),
         cost_estimate=pl.CostEstimate(
             flops=2 * rows_dev * local_blocks * LANES * LANES,
             bytes_accessed=6 * 1024 * 1024,

time: 233 us -> 229 us (0.983)
  local copies, waits for them, and re-layouts: 20.8 us -> 12.6 us
  Pallas kernels: 36.2 us -> 40.5 us
    cond x9, local copies, waits for them, and re-layouts: 13.4 us -> 8.42 us
    unnamed x10 -> x6, local copies, waits for them, and re-layouts: 3.3 us -> 0.12 us
  transfers between devices with their start and end apart: 25 -> 25, of which waited for: 15 -> 15; matrix products, arithmetic and copies ran while one was open for 2% -> 3% of each run, Pallas kernels for 7% -> 7%
where the time goes in v5:
time: 229 us; the launch traced here: 228 us
  waiting for transfers between devices  82.8 us (36%)
  starting transfers between devices  54.4 us (24%)
  Pallas kernels  40.5 us (18%)
  blocking collectives  17.1 us (7%)
  between operations  16.3 us (7%)
  local copies, waits for them, and re-layouts  12.6 us (6%)
  other arithmetic  4.1 us (2%)
    all_gather x1, waiting for transfers between devices, exchange(): weights = lax.all_gather(head_weight, 'voc', axis=0, tiled=False)  36.1 us
    ppermute x20, starting transfers between devices, shifted(): return lax.ppermute(value, 'ctx', pairs)  35.4 us
    ppermute x20, waiting for transfers between devices, shifted(): return lax.ppermute(value, 'ctx', pairs)  26.8 us
    pallas_call x1, Pallas kernels, exchange(): pl.pallas_call(grad_kernel, grid=(voc_count,), in_specs=[smem, smem, whol...  17.9 us
    all_gather x1, blocking collectives, local(): all_done = lax.all_gather(done, 'voc', axis=0, tiled=False)  17.1 us
    all_to_all x1, waiting for transfers between devices, exchange(): arrived = lax.all_to_all(target, 'ctx', 0, 0, tiled=True)  9.33 us
    cond x9, local copies, waits for them, and re-layouts  8.42 us
    all_to_all x1, waiting for transfers between devices, exchange(): all_stats = lax.all_to_all(stats, 'ctx', 0, 0, tiled=True)  8.23 us
  transfers between devices with their start and end apart: 25, of which 15 were waited for; matrix products, arithmetic and copies ran while one was open for 3% of the time, Pallas kernels for 7%

profile of v5, /device:TPU:1, one launch (start us, length us, event | category | flops | bytes accessed | tf_op | source)
XLA Modules:
  0.0 227.8 jit_solution(2039310896867065421)
XLA Ops:
  9.0 7.4 %teacher_map.1 = bf16[8,65,16,128]{3,2,1,0:T(8,128)(2,1)} custom-call(bf16[128,8192]{1,0:T(8,128)(2,1)} %logits_ref.1, bf16[64,128,128]{2,1,0:T(8,128)(2,1)} %coeff_ref.1), custom_call_target="tpu_custom_call" | custom-call | flops 268435456 | bytes 6291456 | tf_op jit(solution)/shard_map/teacher_map/pallas_call | solution.py:407
  16.5 6.9 %all-to-all-start.4 = ((bf16[8,65,16,128]{3,2,1,0:T(8,128)(2,1)}), bf16[8,65,16,128]{3,2,1,0:T(8,128)(2,1)S(1)}, u32[]{:S(2)}, u32[]{:S(2)}) async-start(bf16[8,65,16,128]{3,2,1,0:T(8,128)(2,1)} %teacher_map.1), calls=%async_computation.4 | async-start | bytes 4259840 | tf_op jit(solution)/shard_map/all_to_all | solution.py:425
  23.3 4.8 %collective-permute-start.6 = (bf16[16,1024]{1,0:T(8,128)(2,1)S(1)}, bf16[16,1024]{1,0:T(8,128)(2,1)S(1)}, u32[]{:S(2)}, u32[]{:S(2)}) collective-permute-start(bf16[16,1024]{1,0:T(8,128)(2,1)S(1)} %pad_maximum_fusion.refs_0_), channel_id=1, source_target_pairs={{0,56},{8,0},{16,8},{24,16},{32,24},{40,32},{48,40},{56,48},{64,12... | collective-permute-start | bytes 98312 | tf_op jit(solution)/shard_map/ppermute | solution.py:269
  29.8 4.5 %collective-permute-start.3 = (bf16[16,1024]{1,0:T(8,128)(2,1)S(1)}, bf16[16,1024]{1,0:T(8,128)(2,1)S(1)}, u32[]{:S(2)}, u32[]{:S(2)}) collective-permute-start(bf16[16,1024]{1,0:T(8,128)(2,1)S(1)} %pad_maximum_fusion.refs_0_), channel_id=1, source_target_pairs={{0,32},{8,40},{16,48},{24,56},{32,0},{40,8},{48,16},{56,24},{64,96... | collective-permute-start | bytes 98312 | tf_op jit(solution)/shard_map/ppermute | solution.py:269
  35.0 2.2 collective-permute-start.1
  41.7 2.6 %collective-permute-start.9 = (bf16[128,1024]{1,0:T(8,128)(2,1)S(1)}, bf16[128,1024]{1,0:T(8,128)(2,1)S(1)}, u32[]{:S(2)}, u32[]{:S(2)}) collective-permute-start(bf16[128,1024]{1,0:T(8,128)(2,1)S(1)} %stack_rows.1), channel_id=1, source_target_pairs={{0,192},{8,200},{16,208},{24,216},{32,224},{40,232},{48,240},{56,2... | collective-permute-start | bytes 786440 | tf_op jit(solution)/shard_map/ppermute | solution.py:269
  46.8 2.3 %gather_fusion = s32[512]{0:T(512)S(1)} fusion(s32[1024]{0:T(1024)S(1)} %get-tuple-element.122, s32[1024]{0:T(1024)S(1)} %get-tuple-element.121), kind=kCustom, calls=%fused_computation | custom fusion | bytes 6144 | tf_op jit(solution)/shard_map/gather | solution.py:434
  49.4 1.6 collective-permute-done.8
  51.1 8.2 %collective-permute-done.7 = bf16[128,1024]{1,0:T(8,128)(2,1)S(1)} collective-permute-done((bf16[128,1024]{1,0:T(8,128)(2,1)S(1)}, bf16[128,1024]{1,0:T(8,128)(2,1)S(1)}, u32[]{:S(2)}, u32[]{:S(2)}) %collective-permute-start.7) | collective-permute-done | bytes 262176 | tf_op jit(solution)/shard_map/ppermute | solution.py:269
  59.2 106.9 %conditional.1 = ((bf16[8,896,512]{2,1,0:T(8,128)(2,1)}, bf16[32,16,1024]{2,1,0:T(8,128)(2,1)S(1)}, f32[16,128]{1,0:T(8,128)S(1)})) conditional(s32[]{:T(128)} %convert_element_type.21, (bf16[128,1024]{1,0:T(8,128)(2,1)S(1)}, bf16[128,1024]{1,0:T(8,128)(2,1)S(1)}, bf16[128,1024]{1,0:T(8,128)(2,1)S(1)}, bf16[128,1024]{1,0:T(8,128)(2,1)S(1)}, ...), branch_computations={%region_4.5_spmd, %region_5.6_spmd} | conditional | flops 11282677760 | bytes 183369984 | solution.py:449
  60.0 5.7 %collect_targets.3 = (bf16[640,16,128]{2,1,0:T(8,128)(2,1)}, f32[16,128]{1,0:T(8,128)S(1)}) custom-call(s32[512]{0:T(512)S(1)} %get-tuple-element.62.slot_ref, bf16[8,65,16,128]{3,2,1,0:T(8,128)(2,1)S(1)} %get-tuple-element.63.in_ref), custom_call_target="tpu_custom_call" | custom-call | flops 5242880 | bytes 6291456 | tf_op jit(solution)/shard_map/cond/branch_1_fun/collect_targets/pallas_call | solution.py:292
  65.7 5.2 %all-to-all-start.3 = ((bf16[32,20,16,128]{3,2,1,0:T(8,128)(2,1)}), bf16[32,20,16,128]{3,2,1,0:T(8,128)(2,1)}, u32[]{:S(2)}, u32[]{:S(2)}) async-start(bf16[32,20,16,128]{3,2,1,0:T(8,128)(2,1)} %bitcast.14), calls=%async_computation.3 | async-start | bytes 5242880 | tf_op jit(solution)/shard_map/cond/branch_1_fun/all_to_all | solution.py:310
  71.6 36.1 %all-gather.8.cloned.1.call-done = bf16[7168,512]{1,0:T(8,128)(2,1)} async-done(((bf16[896,512]{1,0:T(8,128)(2,1)}), bf16[7168,512]{1,0:T(8,128)(2,1)}) %all-gather.8.cloned.1.call-update) | async-done | bytes 7340048 | tf_op jit(solution)/shard_map/cond/branch_1_fun/all_gather | solution.py:290
  107.8 3.1 %copy-done.6 = bf16[7168,512]{1,0:T(8,128)(2,1)S(1)} copy-done((bf16[7168,512]{1,0:T(8,128)(2,1)S(1)}, bf16[7168,512]{1,0:T(8,128)(2,1)}, u32[]{:S(2)}) %copy-start.6) | copy-done | bytes 7340056 | tf_op jit(solution)/shard_map/cond
  110.8 7.6 %student_logits.3 = (f32[8,512,512]{2,1,0:T(8,128)S(1)}, f32[32,4,512]{2,1,0:T(4,128)}) custom-call(bf16[512,1024]{1,0:T(8,128)(2,1)S(1)} %bitcast.32, bf16[8,896,512]{2,1,0:T(8,128)(2,1)S(1)} %bitcast.40, f32[16,128]{1,0:T(8,128)S(1)} %get-tuple-element.64.mass_ref), custom_call_target="tpu_custom_call" | custom-call | flops 3758096384 | bytes 18874368 | tf_op jit(solution)/shard_map/cond/branch_1_fun/student_logits/pallas_call | solution.py:321
  118.4 3.3 %copy-done.8 = f32[8,512,512]{2,1,0:T(8,128)} copy-done((f32[8,512,512]{2,1,0:T(8,128)}, f32[8,512,512]{2,1,0:T(8,128)S(1)}, u32[]{:S(2)}) %copy-start.8) | copy-done | bytes 8388632 | tf_op jit(solution)/shard_map/cond
  121.7 9.3 %all-to-all-done.3.target_ref = bf16[32,20,16,128]{3,2,1,0:T(8,128)(2,1)} async-done(((bf16[32,20,16,128]{3,2,1,0:T(8,128)(2,1)}), bf16[32,20,16,128]{3,2,1,0:T(8,128)(2,1)}, u32[]{:S(2)}, u32[]{:S(2)}) %all-to-all-start.3) | async-done | bytes 2621472 | tf_op jit(solution)/shard_map/cond/branch_1_fun/all_to_all | solution.py:310
  131.0 6.9 %all-to-all-start.2 = ((f32[32,4,512]{2,1,0:T(4,128)}), f32[32,4,512]{2,1,0:T(4,128)S(1)}, u32[]{:S(2)}, u32[]{:S(2)}) async-start(f32[32,4,512]{2,1,0:T(4,128)} %get-tuple-element.65), calls=%async_computation.2 | async-start | bytes 524288 | tf_op jit(solution)/shard_map/cond/branch_1_fun/all_to_all | solution.py:346
  139.4 8.2 %all-to-all-done.2.stats_ref = f32[32,4,512]{2,1,0:T(4,128)S(1)} async-done(((f32[32,4,512]{2,1,0:T(4,128)}), f32[32,4,512]{2,1,0:T(4,128)S(1)}, u32[]{:S(2)}, u32[]{:S(2)}) %all-to-all-start.2) | async-done | bytes 262176 | tf_op jit(solution)/shard_map/cond/branch_1_fun/all_to_all | solution.py:346
  148.3 17.9 %grads.3 = (bf16[8,896,512]{2,1,0:T(8,128)(2,1)}, bf16[32,16,1024]{2,1,0:T(8,128)(2,1)S(1)}, f32[16,128]{1,0:T(8,128)S(1)}) custom-call(s32[33]{0:T(128)S(1)} %get-tuple-element.54.place_ref, s32[32]{0:T(128)S(1)} %get-tuple-element.55.slot_ref, f32[32,4,512]{2,1,0:T(4,128)} %copy-done.10, f32[8,512,512]{2,1,0:T(8,128)} %copy-done.8, ...), custom_call_target="tpu_custom_call" | custom-call | flops 7516192768 | bytes 31457280 | tf_op jit(solution)/shard_map/cond/branch_1_fun/grads/pallas_call | solution.py:348
  166.8 2.0 collective-permute-start.11
  170.3 3.4 %collective-permute-done.11.refs_2_ = bf16[128,1024]{1,0:T(8,128)(2,1)S(1)} collective-permute-done((bf16[128,1024]{1,0:T(8,128)(2,1)S(1)}, bf16[128,1024]{1,0:T(8,128)(2,1)S(1)}, u32[]{:S(2)}, u32[]{:S(2)}) %collective-permute-start.11) | collective-permute-done | bytes 262176 | tf_op jit(solution)/shard_map/ppermute | solution.py:269
  173.6 5.4 %collective-permute-done.12.refs_3_ = bf16[128,1024]{1,0:T(8,128)(2,1)S(1)} collective-permute-done((bf16[128,1024]{1,0:T(8,128)(2,1)S(1)}, bf16[128,1024]{1,0:T(8,128)(2,1)S(1)}, u32[]{:S(2)}, u32[]{:S(2)}) %collective-permute-start.12) | collective-permute-done | bytes 262176 | tf_op jit(solution)/shard_map/ppermute | solution.py:269
  179.5 2.7 %collective-permute-start.19 = (bf16[16,1024]{1,0:T(8,128)(2,1)S(1)}, bf16[16,1024]{1,0:T(8,128)(2,1)S(1)}, u32[]{:S(2)}, u32[]{:S(2)}) collective-permute-start(bf16[16,1024]{1,0:T(8,128)(2,1)S(1)} %get-tuple-element.109), channel_id=1, source_target_pairs={{0,56},{8,0},{16,8},{24,16},{32,24},{40,32},{48,40},{56,48},{64,12... | collective-permute-start | bytes 98312 | tf_op jit(solution)/shard_map/ppermute | solution.py:269
  183.1 2.9 %collective-permute-start.17 = (bf16[16,1024]{1,0:T(8,128)(2,1)S(1)}, bf16[16,1024]{1,0:T(8,128)(2,1)S(1)}, u32[]{:S(2)}, u32[]{:S(2)}) collective-permute-start(bf16[16,1024]{1,0:T(8,128)(2,1)S(1)} %get-tuple-element.111), channel_id=1, source_target_pairs={{0,40},{8,48},{16,56},{24,0},{32,8},{40,16},{48,24},{56,32},{64,10... | collective-permute-start | bytes 98312 | tf_op jit(solution)/shard_map/ppermute | solution.py:269
  186.0 2.3 collective-permute-start.16
  188.3 2.4 %collective-permute-start.15 = (bf16[16,1024]{1,0:T(8,128)(2,1)S(1)}, bf16[16,1024]{1,0:T(8,128)(2,1)S(1)}, u32[]{:S(2)}, u32[]{:S(2)}) collective-permute-start(bf16[16,1024]{1,0:T(8,128)(2,1)S(1)} %get-tuple-element.113), channel_id=1, source_target_pairs={{0,24},{8,32},{16,40},{24,48},{32,56},{40,0},{48,8},{56,16},{64,88... | collective-permute-start | bytes 98312 | tf_op jit(solution)/shard_map/ppermute | solution.py:269
  190.8 2.0 collective-permute-start.14
  194.3 1.5 collective-permute-done.14.refs_2_
  195.8 2.2 collective-permute-done.13.refs_1_
  198.2 17.1 %all-gather.2 = bf16[128,1024]{1,0:T(8,128)(2,1)S(1)} all-gather(bf16[16,1024]{1,0:T(8,128)(2,1)S(1)} %finish_rows.1), channel_id=4, replica_groups=mesh['ctx'=32,'voc'=8] {'voc'}, dimensions={0}, use_global_device_ids=true | all-gather | bytes 294912 | tf_op jit(solution)/shard_map/all_gather | solution.py:475
  217.7 2.7 %bitcast_convert_fusion = f32[896,512]{1,0:T(8,128)} fusion(bf16[1,896,512]{2,1,0:T(8,128)(2,1)} %reduce-scatter.2.cloned.1.call-done), kind=kLoop, calls=%fused_computation.3 | loop fusion | flops 458752 | bytes 2752512 | tf_op jit(solution)/shard_map/convert_element_type | solution.py:457
  (69 shorter events, 21.0 us)
Async XLA Ops:
  8.0 0.9 copy-start
  16.5 17.8 %copy-start.11 = (s32[512]{0:T(512)S(1)}, s32[512]{0:T(512)}, u32[]{:S(2)}) copy-start(s32[512]{0:T(512)} %param.13) | copy-start | bytes 6148
  16.5 42.8 %all-to-all-start.4 = ((bf16[8,65,16,128]{3,2,1,0:T(8,128)(2,1)}), bf16[8,65,16,128]{3,2,1,0:T(8,128)(2,1)S(1)}, u32[]{:S(2)}, u32[]{:S(2)}) async-start(bf16[8,65,16,128]{3,2,1,0:T(8,128)(2,1)} %teacher_map.1), calls=%async_computation.4 | async-start | bytes 4259840 | tf_op jit(solution)/shard_map/all_to_all | solution.py:425
  23.3 11.7 %collective-permute-start.6 = (bf16[16,1024]{1,0:T(8,128)(2,1)S(1)}, bf16[16,1024]{1,0:T(8,128)(2,1)S(1)}, u32[]{:S(2)}, u32[]{:S(2)}) collective-permute-start(bf16[16,1024]{1,0:T(8,128)(2,1)S(1)} %pad_maximum_fusion.refs_0_), channel_id=1, source_target_pairs={{0,56},{8,0},{16,8},{24,16},{32,24},{40,32},{48,40},{56,48},{64,12... | collective-permute-start | bytes 98312 | tf_op jit(solution)/shard_map/ppermute | solution.py:269
  28.1 9.0 %collective-permute-start.5 = (bf16[16,1024]{1,0:T(8,128)(2,1)S(1)}, bf16[16,1024]{1,0:T(8,128)(2,1)S(1)}, u32[]{:S(2)}, u32[]{:S(2)}) collective-permute-start(bf16[16,1024]{1,0:T(8,128)(2,1)S(1)} %pad_maximum_fusion.refs_0_), channel_id=1, source_target_pairs={{0,48},{8,56},{16,0},{24,8},{32,16},{40,24},{48,32},{56,40},{64,11... | collective-permute-start | bytes 98312 | tf_op jit(solution)/shard_map/ppermute | solution.py:269
  29.3 9.3 %collective-permute-start.4 = (bf16[16,1024]{1,0:T(8,128)(2,1)S(1)}, bf16[16,1024]{1,0:T(8,128)(2,1)S(1)}, u32[]{:S(2)}, u32[]{:S(2)}) collective-permute-start(bf16[16,1024]{1,0:T(8,128)(2,1)S(1)} %pad_maximum_fusion.refs_0_), channel_id=1, source_target_pairs={{0,40},{8,48},{16,56},{24,0},{32,8},{40,16},{48,24},{56,32},{64,10... | collective-permute-start | bytes 98312 | tf_op jit(solution)/shard_map/ppermute | solution.py:269
  29.8 8.9 %collective-permute-start.3 = (bf16[16,1024]{1,0:T(8,128)(2,1)S(1)}, bf16[16,1024]{1,0:T(8,128)(2,1)S(1)}, u32[]{:S(2)}, u32[]{:S(2)}) collective-permute-start(bf16[16,1024]{1,0:T(8,128)(2,1)S(1)} %pad_maximum_fusion.refs_0_), channel_id=1, source_target_pairs={{0,32},{8,40},{16,48},{24,56},{32,0},{40,8},{48,16},{56,24},{64,96... | collective-permute-start | bytes 98312 | tf_op jit(solution)/shard_map/ppermute | solution.py:269
  34.2 5.8 %collective-permute-start.2 = (bf16[16,1024]{1,0:T(8,128)(2,1)S(1)}, bf16[16,1024]{1,0:T(8,128)(2,1)S(1)}, u32[]{:S(2)}, u32[]{:S(2)}) collective-permute-start(bf16[16,1024]{1,0:T(8,128)(2,1)S(1)} %pad_maximum_fusion.refs_0_), channel_id=1, source_target_pairs={{0,24},{8,32},{16,40},{24,48},{32,56},{40,0},{48,8},{56,16},{64,88... | collective-permute-start | bytes 98312 | tf_op jit(solution)/shard_map/ppermute | solution.py:269
  35.0 5.4 %collective-permute-start.1 = (bf16[16,1024]{1,0:T(8,128)(2,1)S(1)}, bf16[16,1024]{1,0:T(8,128)(2,1)S(1)}, u32[]{:S(2)}, u32[]{:S(2)}) collective-permute-start(bf16[16,1024]{1,0:T(8,128)(2,1)S(1)} %pad_maximum_fusion.refs_0_), channel_id=1, source_target_pairs={{0,16},{8,24},{16,32},{24,40},{32,48},{40,56},{48,0},{56,8},{64,80... | collective-permute-start | bytes 98312 | tf_op jit(solution)/shard_map/ppermute | solution.py:269
  37.2 4.5 %collective-permute-start = (bf16[16,1024]{1,0:T(8,128)(2,1)S(1)}, bf16[16,1024]{1,0:T(8,128)(2,1)S(1)}, u32[]{:S(2)}, u32[]{:S(2)}) collective-permute-start(bf16[16,1024]{1,0:T(8,128)(2,1)S(1)} %pad_maximum_fusion.refs_0_), channel_id=1, source_target_pairs={{0,8},{8,16},{16,24},{24,32},{32,40},{40,48},{48,56},{56,0},{64,72... | collective-permute-start | bytes 98312 | tf_op jit(solution)/shard_map/ppermute | solution.py:269
  41.7 7.8 %collective-permute-start.9 = (bf16[128,1024]{1,0:T(8,128)(2,1)S(1)}, bf16[128,1024]{1,0:T(8,128)(2,1)S(1)}, u32[]{:S(2)}, u32[]{:S(2)}) collective-permute-start(bf16[128,1024]{1,0:T(8,128)(2,1)S(1)} %stack_rows.1), channel_id=1, source_target_pairs={{0,192},{8,200},{16,208},{24,216},{32,224},{40,232},{48,240},{56,2... | collective-permute-start | bytes 786440 | tf_op jit(solution)/shard_map/ppermute | solution.py:269
  44.2 6.8 %collective-permute-start.8 = (bf16[128,1024]{1,0:T(8,128)(2,1)S(1)}, bf16[128,1024]{1,0:T(8,128)(2,1)S(1)}, u32[]{:S(2)}, u32[]{:S(2)}) collective-permute-start(bf16[128,1024]{1,0:T(8,128)(2,1)S(1)} %stack_rows.1), channel_id=1, source_target_pairs={{0,128},{8,136},{16,144},{24,152},{32,160},{40,168},{48,176},{56,1... | collective-permute-start | bytes 786440 | tf_op jit(solution)/shard_map/ppermute | solution.py:269
  44.8 14.5 %collective-permute-start.7 = (bf16[128,1024]{1,0:T(8,128)(2,1)S(1)}, bf16[128,1024]{1,0:T(8,128)(2,1)S(1)}, u32[]{:S(2)}, u32[]{:S(2)}) collective-permute-start(bf16[128,1024]{1,0:T(8,128)(2,1)S(1)} %stack_rows.1), channel_id=1, source_target_pairs={{0,64},{8,72},{16,80},{24,88},{32,96},{40,104},{48,112},{56,120},{... | collective-permute-start | bytes 786440 | tf_op jit(solution)/shard_map/ppermute | solution.py:269
  59.2 48.5 %all-gather.8.cloned.1.call-start = ((), (), s32[]{:S(2)}) async-start(), calls=%async_computation.7 | async-start | bytes 8257536 | tf_op jit(solution)/shard_map/cond/branch_1_fun/all_gather | solution.py:290
  65.7 65.3 %all-to-all-start.3 = ((bf16[32,20,16,128]{3,2,1,0:T(8,128)(2,1)}), bf16[32,20,16,128]{3,2,1,0:T(8,128)(2,1)}, u32[]{:S(2)}, u32[]{:S(2)}) async-start(bf16[32,20,16,128]{3,2,1,0:T(8,128)(2,1)} %bitcast.14), calls=%async_computation.3 | async-start | bytes 5242880 | tf_op jit(solution)/shard_map/cond/branch_1_fun/all_to_all | solution.py:310
  71.6 66.3 %copy-start.4 = (bf16[32,16,1024]{2,1,0:T(8,128)(2,1)}, bf16[32,16,1024]{2,1,0:T(8,128)(2,1)S(1)}, u32[]{:S(2)}) copy-start(bf16[32,16,1024]{2,1,0:T(8,128)(2,1)S(1)} %arrange_rows.3) | copy-start | bytes 3145732 | tf_op jit(solution)/shard_map/cond
  107.7 3.1 %copy-start.6 = (bf16[7168,512]{1,0:T(8,128)(2,1)S(1)}, bf16[7168,512]{1,0:T(8,128)(2,1)}, u32[]{:S(2)}) copy-start(bf16[7168,512]{1,0:T(8,128)(2,1)} %all-gather.8.cloned.1.call-done) | copy-start | bytes 22020100 | tf_op jit(solution)/shard_map/cond
  118.4 3.3 %copy-start.8 = (f32[8,512,512]{2,1,0:T(8,128)}, f32[8,512,512]{2,1,0:T(8,128)S(1)}, u32[]{:S(2)}) copy-start(f32[8,512,512]{2,1,0:T(8,128)S(1)} %get-tuple-element.66.logits_ref) | copy-start | bytes 25165828 | tf_op jit(solution)/shard_map/cond
  131.0 16.6 %all-to-all-start.2 = ((f32[32,4,512]{2,1,0:T(4,128)}), f32[32,4,512]{2,1,0:T(4,128)S(1)}, u32[]{:S(2)}, u32[]{:S(2)}) async-start(f32[32,4,512]{2,1,0:T(4,128)} %get-tuple-element.65), calls=%async_computation.2 | async-start | bytes 524288 | tf_op jit(solution)/shard_map/cond/branch_1_fun/all_to_all | solution.py:346
  147.6 0.7 copy-start.10
  166.2 51.5 %reduce-scatter.2.cloned.1.call-start = ((), (), s32[]{:S(2)}) async-start(), calls=%async_computation.8 | async-start | bytes 8257536 | tf_op jit(solution)/shard_map/reduce_scatter | solution.py:456
  166.8 6.8 %collective-permute-start.11 = (bf16[128,1024]{1,0:T(8,128)(2,1)S(1)}, bf16[128,1024]{1,0:T(8,128)(2,1)S(1)}, u32[]{:S(2)}, u32[]{:S(2)}) collective-permute-start(bf16[128,1024]{1,0:T(8,128)(2,1)S(1)} %bitcast.53), channel_id=1, source_target_pairs={{0,128},{8,136},{16,144},{24,152},{32,160},{40,168},{48,176},{56,1... | collective-permute-start | bytes 786440 | tf_op jit(solution)/shard_map/ppermute | solution.py:269
  168.8 10.3 %collective-permute-start.12 = (bf16[128,1024]{1,0:T(8,128)(2,1)S(1)}, bf16[128,1024]{1,0:T(8,128)(2,1)S(1)}, u32[]{:S(2)}, u32[]{:S(2)}) collective-permute-start(bf16[128,1024]{1,0:T(8,128)(2,1)S(1)} %bitcast.52), channel_id=1, source_target_pairs={{0,192},{8,200},{16,208},{24,216},{32,224},{40,232},{48,240},{56,2... | collective-permute-start | bytes 786440 | tf_op jit(solution)/shard_map/ppermute | solution.py:269
  169.8 9.3 %collective-permute-start.10 = (bf16[128,1024]{1,0:T(8,128)(2,1)S(1)}, bf16[128,1024]{1,0:T(8,128)(2,1)S(1)}, u32[]{:S(2)}, u32[]{:S(2)}) collective-permute-start(bf16[128,1024]{1,0:T(8,128)(2,1)S(1)} %bitcast.51), channel_id=1, source_target_pairs={{0,64},{8,72},{16,80},{24,88},{32,96},{40,104},{48,112},{56,120},{... | collective-permute-start | bytes 786440 | tf_op jit(solution)/shard_map/ppermute | solution.py:269
  179.1 41.3 %copy-start.1 = (bf16[128,896]{1,0:T(8,128)(2,1)S(1)}, bf16[128,896]{1,0:T(8,128)(2,1)}, u32[]{:S(2)}) copy-start(bf16[128,896]{1,0:T(8,128)(2,1)} %param.8) | copy-start | bytes 688132
  179.5 11.3 %collective-permute-start.19 = (bf16[16,1024]{1,0:T(8,128)(2,1)S(1)}, bf16[16,1024]{1,0:T(8,128)(2,1)S(1)}, u32[]{:S(2)}, u32[]{:S(2)}) collective-permute-start(bf16[16,1024]{1,0:T(8,128)(2,1)S(1)} %get-tuple-element.109), channel_id=1, source_target_pairs={{0,56},{8,0},{16,8},{24,16},{32,24},{40,32},{48,40},{56,48},{64,12... | collective-permute-start | bytes 98312 | tf_op jit(solution)/shard_map/ppermute | solution.py:269
  182.2 10.6 %collective-permute-start.18 = (bf16[16,1024]{1,0:T(8,128)(2,1)S(1)}, bf16[16,1024]{1,0:T(8,128)(2,1)S(1)}, u32[]{:S(2)}, u32[]{:S(2)}) collective-permute-start(bf16[16,1024]{1,0:T(8,128)(2,1)S(1)} %get-tuple-element.110), channel_id=1, source_target_pairs={{0,48},{8,56},{16,0},{24,8},{32,16},{40,24},{48,32},{56,40},{64,11... | collective-permute-start | bytes 98312 | tf_op jit(solution)/shard_map/ppermute | solution.py:269
  183.1 10.1 %collective-permute-start.17 = (bf16[16,1024]{1,0:T(8,128)(2,1)S(1)}, bf16[16,1024]{1,0:T(8,128)(2,1)S(1)}, u32[]{:S(2)}, u32[]{:S(2)}) collective-permute-start(bf16[16,1024]{1,0:T(8,128)(2,1)S(1)} %get-tuple-element.111), channel_id=1, source_target_pairs={{0,40},{8,48},{16,56},{24,0},{32,8},{40,16},{48,24},{56,32},{64,10... | collective-permute-start | bytes 98312 | tf_op jit(solution)/shard_map/ppermute | solution.py:269
  186.0 7.1 %collective-permute-start.16 = (bf16[16,1024]{1,0:T(8,128)(2,1)S(1)}, bf16[16,1024]{1,0:T(8,128)(2,1)S(1)}, u32[]{:S(2)}, u32[]{:S(2)}) collective-permute-start(bf16[16,1024]{1,0:T(8,128)(2,1)S(1)} %get-tuple-element.112), channel_id=1, source_target_pairs={{0,32},{8,40},{16,48},{24,56},{32,0},{40,8},{48,16},{56,24},{64,96... | collective-permute-start | bytes 98312 | tf_op jit(solution)/shard_map/ppermute | solution.py:269
  188.3 6.0 %collective-permute-start.15 = (bf16[16,1024]{1,0:T(8,128)(2,1)S(1)}, bf16[16,1024]{1,0:T(8,128)(2,1)S(1)}, u32[]{:S(2)}, u32[]{:S(2)}) collective-permute-start(bf16[16,1024]{1,0:T(8,128)(2,1)S(1)} %get-tuple-element.113), channel_id=1, source_target_pairs={{0,24},{8,32},{16,40},{24,48},{32,56},{40,0},{48,8},{56,16},{64,88... | collective-permute-start | bytes 98312 | tf_op jit(solution)/shard_map/ppermute | solution.py:269
  190.8 5.0 %collective-permute-start.14 = (bf16[16,1024]{1,0:T(8,128)(2,1)S(1)}, bf16[16,1024]{1,0:T(8,128)(2,1)S(1)}, u32[]{:S(2)}, u32[]{:S(2)}) collective-permute-start(bf16[16,1024]{1,0:T(8,128)(2,1)S(1)} %get-tuple-element.114), channel_id=1, source_target_pairs={{0,16},{8,24},{16,32},{24,40},{32,48},{40,56},{48,0},{56,8},{64,80... | collective-permute-start | bytes 98312 | tf_op jit(solution)/shard_map/ppermute | solution.py:269
  192.8 5.2 %collective-permute-start.13 = (bf16[16,1024]{1,0:T(8,128)(2,1)S(1)}, bf16[16,1024]{1,0:T(8,128)(2,1)S(1)}, u32[]{:S(2)}, u32[]{:S(2)}) collective-permute-start(bf16[16,1024]{1,0:T(8,128)(2,1)S(1)} %get-tuple-element.115), channel_id=1, source_target_pairs={{0,8},{8,16},{16,24},{24,32},{32,40},{40,48},{48,56},{56,0},{64,72... | collective-permute-start | bytes 98312 | tf_op jit(solution)/shard_map/ppermute | solution.py:269
Sparse Core Ops, SparseCore 0:
  61.9 45.7 all-gather.7
Sparse Core Ops, SparseCore 1:
  169.2 48.5 reduce-scatter.1

commit v6 on v5

--- a/solution.py
+++ b/solution.py
@@ -129,12 +129,12 @@
         mass = jnp.transpose(mass_ref[...])
         mass = jnp.concatenate([mass[0:1], jnp.zeros((1, rows - part), F32)], axis=1)
         packed = jnp.concatenate([flat[0:2], mass, jnp.zeros((1, rows), F32)], axis=0)
-        stats_ref[...] = jnp.broadcast_to(packed[None], stats_ref.shape)
+        stats_ref[...] = jnp.concatenate([packed, jnp.zeros((4, rows), F32)], axis=0)
 
 
 def grad_kernel(
-    place_ref, slot_ref, stats_ref, logits_ref, target_ref, hidden_ref, hidden_t_ref, weight_ref,
-    dweight_ref, dhidden_ref, base_ref, norm, mass, gain, cross, partial,
+    place_ref, slot_ref, from_ref, stats_refs, logits_ref, target_ref, hidden_ref, hidden_t_ref, weight_ref,
+    dweight_ref, dhidden_ref, base_ref, norm, mass, gain, cross, partial, by_place, in_order,
 ):
     step = pl.program_id(0)
     count, _, part, _ = target_ref.shape
@@ -143,12 +143,18 @@
 
     @pl.when(step == 0)
     def _():
-        tops = stats_ref[:, 0, :]
-        top = jnp.max(tops, axis=0, keepdims=True)
-        total = jnp.sum(stats_ref[:, 1, :] * jnp.exp(tops - top), axis=0, keepdims=True)
-        norm_row = jnp.broadcast_to(top + jnp.log(total), (LANES, rows))
-        norm[...] = jnp.transpose(norm_row)
-        own = stats_ref[:, 2, 0:LANES]
+        top = functools.reduce(jnp.maximum, [ref[0:1] for ref in stats_refs])
+        total = functools.reduce(
+            jnp.add, [ref[1:2] * jnp.exp(ref[0:1] - top) for ref in stats_refs]
+        )
+        norm[...] = jnp.transpose(jnp.broadcast_to(top + jnp.log(total), (LANES, rows)))
+        ring = stats_refs[0].shape[0] - 8
+        for e, ref in enumerate(stats_refs):
+            for k in range(ring):
+                by_place[e * ring + k] = ref[8 + k : 9 + k, 0:LANES]
+        for t in range(count):
+            in_order[t] = by_place[from_ref[t]]
+        own = in_order[...][:, 0, :]
         spread = jnp.broadcast_to(own[:, None, :], (count, part, LANES))
         diagonal = lax.broadcasted_iota(jnp.int32, (count, part, LANES), 1) == lax.broadcasted_iota(
             jnp.int32, (count, part, LANES), 2
@@ -200,6 +206,22 @@
         base_ref[...] = mass[pl.ds(start, part), :]
 
 
+def grads_of(lines):
+    def kernel(place_ref, slot_ref, from_ref, *refs):
+        grad_kernel(place_ref, slot_ref, from_ref, refs[:lines], *refs[lines:])
+
+    return kernel
+
+
+def merge_kernel(*refs):
+    out_ref = refs[-1]
+    top = functools.reduce(jnp.maximum, [ref[0:1] for ref in refs[:-1]])
+    total = functools.reduce(jnp.add, [ref[1:2] * jnp.exp(ref[0:1] - top) for ref in refs[:-1]])
+    out_ref[0:8] = jnp.concatenate([top, total, jnp.zeros((6, top.shape[1]), F32)], axis=0)
+    for k, ref in enumerate(refs[:-1]):
+        out_ref[8 + k : 9 + k] = ref[2:3]
+
+
 def rows_kernel(turned_ref, in_ref, rows_ref, loss_ref):
     count, part, wide = in_ref.shape
     width = wide - LANES
@@ -275,7 +297,7 @@
 
 
 def exchange(
-    capacity, ring, head_weight, incoming, compact_slot, whole_slot, own_slot, place, behind, *lines
+    capacity, ring, head_weight, incoming, compact_slot, whole_slot, own_slot, place, behind, from_where, *lines
 ):
     ctx_count = lax.axis_size("ctx")
     voc_count, held, part, _ = incoming.shape
@@ -328,11 +350,11 @@
         ],
         out_specs=(
             pl.BlockSpec((1, rows, cols), lambda j: (j, 0, 0)),
-            whole((ctx_count, 4, rows)),
+            whole((8, rows)),
         ),
         out_shape=(
             jax.ShapeDtypeStruct((voc_count, rows, cols), F32),
-            jax.ShapeDtypeStruct((ctx_count, 4, rows), F32),
+            jax.ShapeDtypeStruct((8, rows), F32),
         ),
         scratch_shapes=[pltpu.VMEM((rows, LANES), F32)] * 2,
         compiler_params=params(16),
@@ -343,15 +365,35 @@
         ),
         name="student_logits",
     )(hidden_rows, weights, mass)
-    all_stats = lax.all_to_all(stats, "ctx", 0, 0, tiled=True)
+    def merge(parts):
+        return pl.pallas_call(
+            merge_kernel,
+            out_shape=jax.ShapeDtypeStruct((8 + ring, rows), F32),
+            compiler_params=params(),
+            name="merge_stats",
+        )(*parts)
+
+    if capacity == COMPACT:
+        all_stats = spread(merge(spread(stats, ring, False)), ring, True)
+    else:
+        arrived, stats = lax.optimization_barrier((arrived, stats))
+        everywhere = jnp.broadcast_to(stats[None], (ctx_count, 8, rows))
+        got = lax.all_to_all(everywhere, "ctx", 0, 0, tiled=True)
+        all_stats = [
+            merge([got[e + k] for k in range(ring)]) for e in range(0, ctx_count, ring)
+        ]
+        from_where = jnp.arange(ctx_count, dtype=jnp.int32)
 
     dweight, dhidden, base = pl.pallas_call(
-        grad_kernel,
+        grads_of(len(all_stats)),
         grid=(voc_count,),
         in_specs=[
             smem,
             smem,
-            whole((ctx_count, 4, rows)),
+            smem,
+        ]
+        + [whole((8 + ring, rows))] * len(all_stats)
+        + [
             pl.BlockSpec((1, rows, cols), lambda j: (j, 0, 0)),
             whole((ctx_count, capacity, part, LANES)),
             whole((rows, width + LANES)),
@@ -368,7 +410,9 @@
             jax.ShapeDtypeStruct((ctx_count, part, width + LANES), BF16),
             jax.ShapeDtypeStruct((part, LANES), F32),
         ),
-        scratch_shapes=[pltpu.VMEM((rows, LANES), F32)] * 4 + [pltpu.VMEM((rows, width), F32)],
+        scratch_shapes=[pltpu.VMEM((rows, LANES), F32)] * 4
+        + [pltpu.VMEM((rows, width), F32)]
+        + [pltpu.VMEM((ctx_count, 1, LANES), F32)] * 2,
         compiler_params=params(56),
         cost_estimate=pl.CostEstimate(
             flops=4 * rows * width * cols * voc_count,
@@ -376,7 +420,7 @@
             transcendentals=rows * cols * voc_count,
         ),
         name="grads",
-    )(place, own_slot, all_stats, logits, arrived, hidden_rows, hidden_t, weights)
+    )(place, own_slot, from_where, *all_stats, logits, arrived, hidden_rows, hidden_t, weights)
     return dweight, dhidden, base
 
 
@@ -440,11 +484,14 @@
     place = jnp.where(half_block < ctx_count, half_block, 2 * ctx_count - 1 - half_block)
     own_half = jnp.where(fold_side == 0, ctx_index, 2 * ctx_count - 1 - ctx_index)
     behind = (ctx_index // ring - place // ring) % (ctx_count // ring) * ring + (ctx_index - place) % ring
+    from_where = (ctx_index // ring - source // ring) % (ctx_count // ring) * ring + (
+        ctx_index - source
+    ) % ring
     ahead = (place // ring - ctx_index // ring) % (ctx_count // ring) * ring + (place - ctx_index) % ring
     place = jnp.concatenate([ahead, (own_half // 2)[None]]).astype(jnp.int32)
     lines = spread(near, ring, True)
     operands = lax.optimization_barrier(
-        (incoming, compact_slot, whole_slot, own_slot, place, behind, *lines)
+        (incoming, compact_slot, whole_slot, own_slot, place, behind, from_where, *lines)
     )
     dweight, dhidden, base = lax.cond(
         fits,

time: 229 us -> 227 us (level)
  waiting for transfers between devices: 82.8 us -> 71 us
  starting transfers between devices: 54.4 us -> 63.2 us
  blocking collectives: 17.1 us -> 19.5 us
    ppermute x20 -> x30, starting transfers between devices: 35.4 us -> 51.2 us  [shifted(): return lax.ppermute(value, 'ctx', pairs)]
    all_to_all x1, waiting for transfers between devices: 9.33 us -> 0.01 us  [exchange(): arrived = lax.all_to_all(target, 'ctx', 0, 0, tiled=True)]
    all_to_all x1 -> x0, waiting for transfers between devices: 8.23 us -> none  [exchange(): all_stats = lax.all_to_all(stats, 'ctx', 0, 0, tiled=True)]
    all_to_all x1 -> x0, starting transfers between devices: 6.92 us -> none  [exchange(): all_stats = lax.all_to_all(stats, 'ctx', 0, 0, tiled=True)]
    reduce_scatter x1, waiting for transfers between devices: 1.04 us -> 4.25 us  [local(): lax.psum_scatter(dweight, 'voc', scatter_dimension=0, tiled=True)]
    ppermute x20 -> x30, waiting for transfers between devices: 26.8 us -> 29.4 us  [shifted(): return lax.ppermute(value, 'ctx', pairs)]
    all_gather x1, blocking collectives: 17.1 us -> 19.5 us  [local(): all_done = lax.all_gather(done, 'voc', axis=0, tiled=False)]
    cond x9 -> x15, local copies, waits for them, and re-layouts: 8.42 us -> 8.34 us
  transfers between devices with their start and end apart: 25 -> 34, of which waited for: 15 -> 17; matrix products, arithmetic and copies ran while one was open for 3% -> 3% of each run, Pallas kernels for 7% -> 6%
where the time goes in v6:
time: 227 us
  waiting for transfers between devices  71 us (31%)
  starting transfers between devices  63.2 us (28%)
  Pallas kernels  39.8 us (18%)
  blocking collectives  19.5 us (9%)
  between operations  16.3 us (7%)
  local copies, waits for them, and re-layouts  12.5 us (6%)
  other arithmetic  4.11 us (2%)
    ppermute x30, starting transfers between devices, shifted(): return lax.ppermute(value, 'ctx', pairs)  51.2 us
    all_gather x1, waiting for transfers between devices, exchange(): weights = lax.all_gather(head_weight, 'voc', axis=0, tiled=False)  36.1 us
    ppermute x30, waiting for transfers between devices, shifted(): return lax.ppermute(value, 'ctx', pairs)  29.4 us
    all_gather x1, blocking collectives, local(): all_done = lax.all_gather(done, 'voc', axis=0, tiled=False)  19.5 us
    pallas_call x1, Pallas kernels, exchange(): pl.pallas_call(grads_of(len(all_stats)), grid=(voc_count,), in_specs=[sme...  17.8 us
    cond x15, local copies, waits for them, and re-layouts  8.34 us
    pallas_call x1, Pallas kernels, local(): pl.pallas_call(teacher_kernel, out_shape=jax.ShapeDtypeStruct((voc_count,...  7.44 us
    all_to_all x1, starting transfers between devices, local(): incoming = lax.all_to_all(outgoing, 'voc', 0, 0, tiled=True)  6.88 us
  transfers between devices with their start and end apart: 34, of which 17 were waited for; matrix products, arithmetic and copies ran while one was open for 3% of the time, Pallas kernels for 6%

profile of v6, /device:TPU:1, one launch (start us, length us, event | category | flops | bytes accessed | tf_op | source)
XLA Modules:
  0.0 226.5 jit_solution(9043169938686378869)
XLA Ops:
  9.0 7.4 %teacher_map.1 = bf16[8,65,16,128]{3,2,1,0:T(8,128)(2,1)} custom-call(bf16[128,8192]{1,0:T(8,128)(2,1)} %logits_ref.1, bf16[64,128,128]{2,1,0:T(8,128)(2,1)} %coeff_ref.1), custom_call_target="tpu_custom_call" | custom-call | flops 268435456 | bytes 6291456 | tf_op jit(solution)/shard_map/teacher_map/pallas_call | solution.py:451
  16.5 6.9 %all-to-all-start.3 = ((bf16[8,65,16,128]{3,2,1,0:T(8,128)(2,1)}), bf16[8,65,16,128]{3,2,1,0:T(8,128)(2,1)S(1)}, u32[]{:S(2)}, u32[]{:S(2)}) async-start(bf16[8,65,16,128]{3,2,1,0:T(8,128)(2,1)} %teacher_map.1), calls=%async_computation.3 | async-start | bytes 4259840 | tf_op jit(solution)/shard_map/all_to_all | solution.py:469
  23.4 4.8 %collective-permute-start.16 = (bf16[16,1024]{1,0:T(8,128)(2,1)S(1)}, bf16[16,1024]{1,0:T(8,128)(2,1)S(1)}, u32[]{:S(2)}, u32[]{:S(2)}) collective-permute-start(bf16[16,1024]{1,0:T(8,128)(2,1)S(1)} %pad_maximum_fusion.refs_0_), channel_id=1, source_target_pairs={{0,56},{8,0},{16,8},{24,16},{32,24},{40,32},{48,40},{56,48},{64,12... | collective-permute-start | bytes 98312 | tf_op jit(solution)/shard_map/ppermute | solution.py:291
  29.8 4.5 %collective-permute-start.13 = (bf16[16,1024]{1,0:T(8,128)(2,1)S(1)}, bf16[16,1024]{1,0:T(8,128)(2,1)S(1)}, u32[]{:S(2)}, u32[]{:S(2)}) collective-permute-start(bf16[16,1024]{1,0:T(8,128)(2,1)S(1)} %pad_maximum_fusion.refs_0_), channel_id=1, source_target_pairs={{0,32},{8,40},{16,48},{24,56},{32,0},{40,8},{48,16},{56,24},{64,96... | collective-permute-start | bytes 98312 | tf_op jit(solution)/shard_map/ppermute | solution.py:291
  35.1 2.2 collective-permute-start.11
  41.7 2.6 %collective-permute-start.19 = (bf16[128,1024]{1,0:T(8,128)(2,1)S(1)}, bf16[128,1024]{1,0:T(8,128)(2,1)S(1)}, u32[]{:S(2)}, u32[]{:S(2)}) collective-permute-start(bf16[128,1024]{1,0:T(8,128)(2,1)S(1)} %stack_rows.1), channel_id=1, source_target_pairs={{0,192},{8,200},{16,208},{24,216},{32,224},{40,232},{48,240},{56,2... | collective-permute-start | bytes 786440 | tf_op jit(solution)/shard_map/ppermute | solution.py:291
  46.9 2.3 %gather_fusion = s32[512]{0:T(512)S(1)} fusion(s32[1024]{0:T(1024)S(1)} %get-tuple-element.161, s32[1024]{0:T(1024)S(1)} %get-tuple-element.160), kind=kCustom, calls=%fused_computation | custom fusion | bytes 6144 | tf_op jit(solution)/shard_map/gather | solution.py:478
  49.5 1.6 collective-permute-done.18
  51.1 8.3 %collective-permute-done.17 = bf16[128,1024]{1,0:T(8,128)(2,1)S(1)} collective-permute-done((bf16[128,1024]{1,0:T(8,128)(2,1)S(1)}, bf16[128,1024]{1,0:T(8,128)(2,1)S(1)}, u32[]{:S(2)}, u32[]{:S(2)}) %collective-permute-start.17) | collective-permute-done | bytes 262176 | tf_op jit(solution)/shard_map/ppermute | solution.py:291
  59.4 103.9 %conditional.1 = ((bf16[8,896,512]{2,1,0:T(8,128)(2,1)}, bf16[32,16,1024]{2,1,0:T(8,128)(2,1)S(1)}, f32[16,128]{1,0:T(8,128)S(1)})) conditional(s32[]{:T(128)} %convert_element_type.21, (s32[512]{0:T(512)S(1)}, bf16[8,65,16,128]{3,2,1,0:T(8,128)(2,1)S(1)}, bf16[128,1024]{1,0:T(8,128)(2,1)S(1)}, bf16[128,1024]{1,0:T(8,128)(2,1)S(1)}, ...), branch_computations={%region_4.5_spmd, %region_5.6_spmd} | conditional | flops 11282677760 | bytes 185221600 | solution.py:496
  60.1 5.7 %collect_targets.3 = (bf16[640,16,128]{2,1,0:T(8,128)(2,1)}, f32[16,128]{1,0:T(8,128)S(1)}) custom-call(s32[512]{0:T(512)S(1)} %get-tuple-element.67.slot_ref, bf16[8,65,16,128]{3,2,1,0:T(8,128)(2,1)S(1)} %get-tuple-element.68.in_ref), custom_call_target="tpu_custom_call" | custom-call | flops 5242880 | bytes 6291456 | tf_op jit(solution)/shard_map/cond/branch_1_fun/collect_targets/pallas_call | solution.py:314
  65.9 5.1 %all-to-all-start = ((bf16[32,20,16,128]{3,2,1,0:T(8,128)(2,1)}), bf16[32,20,16,128]{3,2,1,0:T(8,128)(2,1)}, u32[]{:S(2)}, u32[]{:S(2)}) async-start(bf16[32,20,16,128]{3,2,1,0:T(8,128)(2,1)} %bitcast.46), calls=%async_computation | async-start | bytes 5242880 | tf_op jit(solution)/shard_map/cond/branch_1_fun/all_to_all | solution.py:332
  71.7 36.1 %all-gather.8.cloned.1.call-done = bf16[7168,512]{1,0:T(8,128)(2,1)} async-done(((bf16[896,512]{1,0:T(8,128)(2,1)}), bf16[7168,512]{1,0:T(8,128)(2,1)}) %all-gather.8.cloned.1.call-update) | async-done | bytes 7340048 | tf_op jit(solution)/shard_map/cond/branch_1_fun/all_gather | solution.py:312
  107.8 3.1 %copy-done.11 = bf16[7168,512]{1,0:T(8,128)(2,1)S(1)} copy-done((bf16[7168,512]{1,0:T(8,128)(2,1)S(1)}, bf16[7168,512]{1,0:T(8,128)(2,1)}, u32[]{:S(2)}) %copy-start.11) | copy-done | bytes 7340056 | tf_op jit(solution)/shard_map/cond
  110.9 6.8 %student_logits.3 = (f32[8,512,512]{2,1,0:T(8,128)S(1)}, f32[8,512]{1,0:T(8,128)S(1)}) custom-call(bf16[512,1024]{1,0:T(8,128)(2,1)S(1)} %bitcast.96, bf16[8,896,512]{2,1,0:T(8,128)(2,1)S(1)} %bitcast.104, f32[16,128]{1,0:T(8,128)S(1)} %get-tuple-element.69.mass_ref), custom_call_target="tpu_custom_call" | custom-call | flops 3758096384 | bytes 18874368 | tf_op jit(solution)/shard_map/cond/branch_1_fun/student_logits/pallas_call | solution.py:343
  117.7 3.3 %copy-done.13 = f32[8,512,512]{2,1,0:T(8,128)} copy-done((f32[8,512,512]{2,1,0:T(8,128)}, f32[8,512,512]{2,1,0:T(8,128)S(1)}, u32[]{:S(2)}) %copy-start.13) | copy-done | bytes 8388632 | tf_op jit(solution)/shard_map/cond
  121.0 3.0 %collective-permute-start.6 = (f32[8,512]{1,0:T(8,128)S(1)}, f32[8,512]{1,0:T(8,128)S(1)}, u32[]{:S(2)}, u32[]{:S(2)}) collective-permute-start(f32[8,512]{1,0:T(8,128)S(1)} %get-tuple-element.70.refs_0_), channel_id=1, source_target_pairs={{0,56},{8,0},{16,8},{24,16},{32,24},{40,32},{48,40},{56,48},{64,12... | collective-permute-start | bytes 49160 | tf_op jit(solution)/shard_map/cond/branch_1_fun/ppermute | solution.py:291
  124.1 1.9 collective-permute-start.5
  126.9 3.7 %collective-permute-start.3 = (f32[8,512]{1,0:T(8,128)S(1)}, f32[8,512]{1,0:T(8,128)S(1)}, u32[]{:S(2)}, u32[]{:S(2)}) collective-permute-start(f32[8,512]{1,0:T(8,128)S(1)} %get-tuple-element.70.refs_0_), channel_id=1, source_target_pairs={{0,32},{8,40},{16,48},{24,56},{32,0},{40,8},{48,16},{56,24},{64,96... | collective-permute-start | bytes 49160 | tf_op jit(solution)/shard_map/cond/branch_1_fun/ppermute | solution.py:291
  130.5 3.0 %collective-permute-start.1 = (f32[8,512]{1,0:T(8,128)S(1)}, f32[8,512]{1,0:T(8,128)S(1)}, u32[]{:S(2)}, u32[]{:S(2)}) collective-permute-start(f32[8,512]{1,0:T(8,128)S(1)} %get-tuple-element.70.refs_0_), channel_id=1, source_target_pairs={{0,16},{8,24},{16,32},{24,40},{32,48},{40,56},{48,0},{56,8},{64,80... | collective-permute-start | bytes 49160 | tf_op jit(solution)/shard_map/cond/branch_1_fun/ppermute | solution.py:291
  137.8 2.5 %collective-permute-start.9 = (f32[16,512]{1,0:T(8,128)S(1)}, f32[16,512]{1,0:T(8,128)S(1)}, u32[]{:S(2)}, u32[]{:S(2)}) collective-permute-start(f32[16,512]{1,0:T(8,128)S(1)} %merge_stats.9.refs_0_), channel_id=1, source_target_pairs={{0,192},{8,200},{16,208},{24,216},{32,224},{40,232},{48,240},{56,2... | collective-permute-start | bytes 98312 | tf_op jit(solution)/shard_map/cond/branch_1_fun/ppermute | solution.py:291
  142.9 1.7 collective-permute-done.8.refs_2_
  145.5 17.8 %grads.3 = (bf16[8,896,512]{2,1,0:T(8,128)(2,1)}, bf16[32,16,1024]{2,1,0:T(8,128)(2,1)S(1)}, f32[16,128]{1,0:T(8,128)S(1)}) custom-call(s32[33]{0:T(128)S(1)} %get-tuple-element.58.place_ref, s32[32]{0:T(128)S(1)} %get-tuple-element.59.slot_ref, s32[32]{0:T(128)S(1)} %get-tuple-element.60.from_ref, f32[16,512]{1,0:T(8,128)} %copy-done.6, ...), custom_call_target="tpu_custom_call" | custom-call | flops 7516192768 | bytes 31457280 | tf_op jit(solution)/shard_map/cond/branch_1_fun/grads/pallas_call | solution.py:387
  166.6 4.3 %collective-permute-done.21.refs_2_ = bf16[128,1024]{1,0:T(8,128)(2,1)S(1)} collective-permute-done((bf16[128,1024]{1,0:T(8,128)(2,1)S(1)}, bf16[128,1024]{1,0:T(8,128)(2,1)S(1)}, u32[]{:S(2)}, u32[]{:S(2)}) %collective-permute-start.21) | collective-permute-done | bytes 262176 | tf_op jit(solution)/shard_map/ppermute | solution.py:291
  172.5 2.2 collective-permute-done.20.refs_1_
  175.5 4.8 %collective-permute-start.28 = (bf16[16,1024]{1,0:T(8,128)(2,1)S(1)}, bf16[16,1024]{1,0:T(8,128)(2,1)S(1)}, u32[]{:S(2)}, u32[]{:S(2)}) collective-permute-start(bf16[16,1024]{1,0:T(8,128)(2,1)S(1)} %get-tuple-element.149), channel_id=1, source_target_pairs={{0,48},{8,56},{16,0},{24,8},{32,16},{40,24},{48,32},{56,40},{64,11... | collective-permute-start | bytes 98312 | tf_op jit(solution)/shard_map/ppermute | solution.py:291
  181.4 2.1 collective-permute-start.25
  183.5 3.3 %collective-permute-start.24 = (bf16[16,1024]{1,0:T(8,128)(2,1)S(1)}, bf16[16,1024]{1,0:T(8,128)(2,1)S(1)}, u32[]{:S(2)}, u32[]{:S(2)}) collective-permute-start(bf16[16,1024]{1,0:T(8,128)(2,1)S(1)} %get-tuple-element.153), channel_id=1, source_target_pairs={{0,16},{8,24},{16,32},{24,40},{32,48},{40,56},{48,0},{56,8},{64,80... | collective-permute-start | bytes 98312 | tf_op jit(solution)/shard_map/ppermute | solution.py:291
  188.4 2.8 %collective-permute-done.23.refs_1_ = bf16[16,1024]{1,0:T(8,128)(2,1)S(1)} collective-permute-done((bf16[16,1024]{1,0:T(8,128)(2,1)S(1)}, bf16[16,1024]{1,0:T(8,128)(2,1)S(1)}, u32[]{:S(2)}, u32[]{:S(2)}) %collective-permute-start.23) | collective-permute-done | bytes 32800 | tf_op jit(solution)/shard_map/ppermute | solution.py:291
  191.4 19.5 %all-gather.2 = bf16[128,1024]{1,0:T(8,128)(2,1)S(1)} all-gather(bf16[16,1024]{1,0:T(8,128)(2,1)S(1)} %finish_rows.1), channel_id=4, replica_groups=mesh['ctx'=32,'voc'=8] {'voc'}, dimensions={0}, use_global_device_ids=true | all-gather | bytes 294912 | tf_op jit(solution)/shard_map/all_gather | solution.py:522
  212.2 4.2 %reduce-scatter.2.cloned.1.call-done = bf16[1,896,512]{2,1,0:T(8,128)(2,1)} async-done(((bf16[8,896,512]{2,1,0:T(8,128)(2,1)}), bf16[1,896,512]{2,1,0:T(8,128)(2,1)}) %reduce-scatter.2.cloned.1.call-update) | async-done | bytes 917520 | tf_op jit(solution)/shard_map/reduce_scatter | solution.py:503
  216.4 2.7 %bitcast_convert_fusion = f32[896,512]{1,0:T(8,128)} fusion(bf16[1,896,512]{2,1,0:T(8,128)(2,1)} %reduce-scatter.2.cloned.1.call-done), kind=kLoop, calls=%fused_computation.35 | loop fusion | flops 458752 | bytes 2752512 | tf_op jit(solution)/shard_map/convert_element_type | solution.py:504
  (95 shorter events, 30.2 us)
Async XLA Ops:
  16.5 42.9 %all-to-all-start.3 = ((bf16[8,65,16,128]{3,2,1,0:T(8,128)(2,1)}), bf16[8,65,16,128]{3,2,1,0:T(8,128)(2,1)S(1)}, u32[]{:S(2)}, u32[]{:S(2)}) async-start(bf16[8,65,16,128]{3,2,1,0:T(8,128)(2,1)} %teacher_map.1), calls=%async_computation.3 | async-start | bytes 4259840 | tf_op jit(solution)/shard_map/all_to_all | solution.py:469
  23.4 11.7 %collective-permute-start.16 = (bf16[16,1024]{1,0:T(8,128)(2,1)S(1)}, bf16[16,1024]{1,0:T(8,128)(2,1)S(1)}, u32[]{:S(2)}, u32[]{:S(2)}) collective-permute-start(bf16[16,1024]{1,0:T(8,128)(2,1)S(1)} %pad_maximum_fusion.refs_0_), channel_id=1, source_target_pairs={{0,56},{8,0},{16,8},{24,16},{32,24},{40,32},{48,40},{56,48},{64,12... | collective-permute-start | bytes 98312 | tf_op jit(solution)/shard_map/ppermute | solution.py:291
  28.2 9.1 %collective-permute-start.15 = (bf16[16,1024]{1,0:T(8,128)(2,1)S(1)}, bf16[16,1024]{1,0:T(8,128)(2,1)S(1)}, u32[]{:S(2)}, u32[]{:S(2)}) collective-permute-start(bf16[16,1024]{1,0:T(8,128)(2,1)S(1)} %pad_maximum_fusion.refs_0_), channel_id=1, source_target_pairs={{0,48},{8,56},{16,0},{24,8},{32,16},{40,24},{48,32},{56,40},{64,11... | collective-permute-start | bytes 98312 | tf_op jit(solution)/shard_map/ppermute | solution.py:291
  29.3 9.3 %collective-permute-start.14 = (bf16[16,1024]{1,0:T(8,128)(2,1)S(1)}, bf16[16,1024]{1,0:T(8,128)(2,1)S(1)}, u32[]{:S(2)}, u32[]{:S(2)}) collective-permute-start(bf16[16,1024]{1,0:T(8,128)(2,1)S(1)} %pad_maximum_fusion.refs_0_), channel_id=1, source_target_pairs={{0,40},{8,48},{16,56},{24,0},{32,8},{40,16},{48,24},{56,32},{64,10... | collective-permute-start | bytes 98312 | tf_op jit(solution)/shard_map/ppermute | solution.py:291
  29.8 8.9 %collective-permute-start.13 = (bf16[16,1024]{1,0:T(8,128)(2,1)S(1)}, bf16[16,1024]{1,0:T(8,128)(2,1)S(1)}, u32[]{:S(2)}, u32[]{:S(2)}) collective-permute-start(bf16[16,1024]{1,0:T(8,128)(2,1)S(1)} %pad_maximum_fusion.refs_0_), channel_id=1, source_target_pairs={{0,32},{8,40},{16,48},{24,56},{32,0},{40,8},{48,16},{56,24},{64,96... | collective-permute-start | bytes 98312 | tf_op jit(solution)/shard_map/ppermute | solution.py:291
  34.3 5.8 %collective-permute-start.12 = (bf16[16,1024]{1,0:T(8,128)(2,1)S(1)}, bf16[16,1024]{1,0:T(8,128)(2,1)S(1)}, u32[]{:S(2)}, u32[]{:S(2)}) collective-permute-start(bf16[16,1024]{1,0:T(8,128)(2,1)S(1)} %pad_maximum_fusion.refs_0_), channel_id=1, source_target_pairs={{0,24},{8,32},{16,40},{24,48},{32,56},{40,0},{48,8},{56,16},{64,88... | collective-permute-start | bytes 98312 | tf_op jit(solution)/shard_map/ppermute | solution.py:291
  35.1 5.4 %collective-permute-start.11 = (bf16[16,1024]{1,0:T(8,128)(2,1)S(1)}, bf16[16,1024]{1,0:T(8,128)(2,1)S(1)}, u32[]{:S(2)}, u32[]{:S(2)}) collective-permute-start(bf16[16,1024]{1,0:T(8,128)(2,1)S(1)} %pad_maximum_fusion.refs_0_), channel_id=1, source_target_pairs={{0,16},{8,24},{16,32},{24,40},{32,48},{40,56},{48,0},{56,8},{64,80... | collective-permute-start | bytes 98312 | tf_op jit(solution)/shard_map/ppermute | solution.py:291
  37.2 4.5 %collective-permute-start.10 = (bf16[16,1024]{1,0:T(8,128)(2,1)S(1)}, bf16[16,1024]{1,0:T(8,128)(2,1)S(1)}, u32[]{:S(2)}, u32[]{:S(2)}) collective-permute-start(bf16[16,1024]{1,0:T(8,128)(2,1)S(1)} %pad_maximum_fusion.refs_0_), channel_id=1, source_target_pairs={{0,8},{8,16},{16,24},{24,32},{32,40},{40,48},{48,56},{56,0},{64,72... | collective-permute-start | bytes 98312 | tf_op jit(solution)/shard_map/ppermute | solution.py:291
  41.7 7.8 %collective-permute-start.19 = (bf16[128,1024]{1,0:T(8,128)(2,1)S(1)}, bf16[128,1024]{1,0:T(8,128)(2,1)S(1)}, u32[]{:S(2)}, u32[]{:S(2)}) collective-permute-start(bf16[128,1024]{1,0:T(8,128)(2,1)S(1)} %stack_rows.1), channel_id=1, source_target_pairs={{0,192},{8,200},{16,208},{24,216},{32,224},{40,232},{48,240},{56,2... | collective-permute-start | bytes 786440 | tf_op jit(solution)/shard_map/ppermute | solution.py:291
  44.3 6.8 %collective-permute-start.18 = (bf16[128,1024]{1,0:T(8,128)(2,1)S(1)}, bf16[128,1024]{1,0:T(8,128)(2,1)S(1)}, u32[]{:S(2)}, u32[]{:S(2)}) collective-permute-start(bf16[128,1024]{1,0:T(8,128)(2,1)S(1)} %stack_rows.1), channel_id=1, source_target_pairs={{0,128},{8,136},{16,144},{24,152},{32,160},{40,168},{48,176},{56,1... | collective-permute-start | bytes 786440 | tf_op jit(solution)/shard_map/ppermute | solution.py:291
  44.8 14.6 %collective-permute-start.17 = (bf16[128,1024]{1,0:T(8,128)(2,1)S(1)}, bf16[128,1024]{1,0:T(8,128)(2,1)S(1)}, u32[]{:S(2)}, u32[]{:S(2)}) collective-permute-start(bf16[128,1024]{1,0:T(8,128)(2,1)S(1)} %stack_rows.1), channel_id=1, source_target_pairs={{0,64},{8,72},{16,80},{24,88},{32,96},{40,104},{48,112},{56,120},{... | collective-permute-start | bytes 786440 | tf_op jit(solution)/shard_map/ppermute | solution.py:291
  59.4 48.4 %all-gather.8.cloned.1.call-start = ((), (), s32[]{:S(2)}) async-start(), calls=%async_computation.6 | async-start | bytes 8257536 | tf_op jit(solution)/shard_map/cond/branch_1_fun/all_gather | solution.py:312
  65.9 77.0 %all-to-all-start = ((bf16[32,20,16,128]{3,2,1,0:T(8,128)(2,1)}), bf16[32,20,16,128]{3,2,1,0:T(8,128)(2,1)}, u32[]{:S(2)}, u32[]{:S(2)}) async-start(bf16[32,20,16,128]{3,2,1,0:T(8,128)(2,1)} %bitcast.46), calls=%async_computation | async-start | bytes 5242880 | tf_op jit(solution)/shard_map/cond/branch_1_fun/all_to_all | solution.py:332
  121.0 9.5 %collective-permute-start.6 = (f32[8,512]{1,0:T(8,128)S(1)}, f32[8,512]{1,0:T(8,128)S(1)}, u32[]{:S(2)}, u32[]{:S(2)}) collective-permute-start(f32[8,512]{1,0:T(8,128)S(1)} %get-tuple-element.70.refs_0_), channel_id=1, source_target_pairs={{0,56},{8,0},{16,8},{24,16},{32,24},{40,32},{48,40},{56,48},{64,12... | collective-permute-start | bytes 49160 | tf_op jit(solution)/shard_map/cond/branch_1_fun/ppermute | solution.py:291
  124.1 9.5 %collective-permute-start.5 = (f32[8,512]{1,0:T(8,128)S(1)}, f32[8,512]{1,0:T(8,128)S(1)}, u32[]{:S(2)}, u32[]{:S(2)}) collective-permute-start(f32[8,512]{1,0:T(8,128)S(1)} %get-tuple-element.70.refs_0_), channel_id=1, source_target_pairs={{0,48},{8,56},{16,0},{24,8},{32,16},{40,24},{48,32},{56,40},{64,11... | collective-permute-start | bytes 49160 | tf_op jit(solution)/shard_map/cond/branch_1_fun/ppermute | solution.py:291
  126.0 8.8 %collective-permute-start.4 = (f32[8,512]{1,0:T(8,128)S(1)}, f32[8,512]{1,0:T(8,128)S(1)}, u32[]{:S(2)}, u32[]{:S(2)}) collective-permute-start(f32[8,512]{1,0:T(8,128)S(1)} %get-tuple-element.70.refs_0_), channel_id=1, source_target_pairs={{0,40},{8,48},{16,56},{24,0},{32,8},{40,16},{48,24},{56,32},{64,10... | collective-permute-start | bytes 49160 | tf_op jit(solution)/shard_map/cond/branch_1_fun/ppermute | solution.py:291
  126.9 7.9 %collective-permute-start.3 = (f32[8,512]{1,0:T(8,128)S(1)}, f32[8,512]{1,0:T(8,128)S(1)}, u32[]{:S(2)}, u32[]{:S(2)}) collective-permute-start(f32[8,512]{1,0:T(8,128)S(1)} %get-tuple-element.70.refs_0_), channel_id=1, source_target_pairs={{0,32},{8,40},{16,48},{24,56},{32,0},{40,8},{48,16},{56,24},{64,96... | collective-permute-start | bytes 49160 | tf_op jit(solution)/shard_map/cond/branch_1_fun/ppermute | solution.py:291
  130.5 5.7 %collective-permute-start.2 = (f32[8,512]{1,0:T(8,128)S(1)}, f32[8,512]{1,0:T(8,128)S(1)}, u32[]{:S(2)}, u32[]{:S(2)}) collective-permute-start(f32[8,512]{1,0:T(8,128)S(1)} %get-tuple-element.70.refs_0_), channel_id=1, source_target_pairs={{0,24},{8,32},{16,40},{24,48},{32,56},{40,0},{48,8},{56,16},{64,88... | collective-permute-start | bytes 49160 | tf_op jit(solution)/shard_map/cond/branch_1_fun/ppermute | solution.py:291
  130.5 5.7 %collective-permute-start.1 = (f32[8,512]{1,0:T(8,128)S(1)}, f32[8,512]{1,0:T(8,128)S(1)}, u32[]{:S(2)}, u32[]{:S(2)}) collective-permute-start(f32[8,512]{1,0:T(8,128)S(1)} %get-tuple-element.70.refs_0_), channel_id=1, source_target_pairs={{0,16},{8,24},{16,32},{24,40},{32,48},{40,56},{48,0},{56,8},{64,80... | collective-permute-start | bytes 49160 | tf_op jit(solution)/shard_map/cond/branch_1_fun/ppermute | solution.py:291
  137.8 5.1 %collective-permute-start.9 = (f32[16,512]{1,0:T(8,128)S(1)}, f32[16,512]{1,0:T(8,128)S(1)}, u32[]{:S(2)}, u32[]{:S(2)}) collective-permute-start(f32[16,512]{1,0:T(8,128)S(1)} %merge_stats.9.refs_0_), channel_id=1, source_target_pairs={{0,192},{8,200},{16,208},{24,216},{32,224},{40,232},{48,240},{56,2... | collective-permute-start | bytes 98312 | tf_op jit(solution)/shard_map/cond/branch_1_fun/ppermute | solution.py:291
  140.3 4.3 %collective-permute-start.8 = (f32[16,512]{1,0:T(8,128)S(1)}, f32[16,512]{1,0:T(8,128)S(1)}, u32[]{:S(2)}, u32[]{:S(2)}) collective-permute-start(f32[16,512]{1,0:T(8,128)S(1)} %merge_stats.9.refs_0_), channel_id=1, source_target_pairs={{0,128},{8,136},{16,144},{24,152},{32,160},{40,168},{48,176},{56,1... | collective-permute-start | bytes 98312 | tf_op jit(solution)/shard_map/cond/branch_1_fun/ppermute | solution.py:291
  163.3 53.1 %reduce-scatter.2.cloned.1.call-start = ((), (), s32[]{:S(2)}) async-start(), calls=%async_computation.7 | async-start | bytes 8257536 | tf_op jit(solution)/shard_map/reduce_scatter | solution.py:503
  164.0 6.9 %collective-permute-start.21 = (bf16[128,1024]{1,0:T(8,128)(2,1)S(1)}, bf16[128,1024]{1,0:T(8,128)(2,1)S(1)}, u32[]{:S(2)}, u32[]{:S(2)}) collective-permute-start(bf16[128,1024]{1,0:T(8,128)(2,1)S(1)} %bitcast.117), channel_id=1, source_target_pairs={{0,128},{8,136},{16,144},{24,152},{32,160},{40,168},{48,176},{56,1... | collective-permute-start | bytes 786440 | tf_op jit(solution)/shard_map/ppermute | solution.py:291
  165.2 7.3 %collective-permute-start.22 = (bf16[128,1024]{1,0:T(8,128)(2,1)S(1)}, bf16[128,1024]{1,0:T(8,128)(2,1)S(1)}, u32[]{:S(2)}, u32[]{:S(2)}) collective-permute-start(bf16[128,1024]{1,0:T(8,128)(2,1)S(1)} %bitcast.116), channel_id=1, source_target_pairs={{0,192},{8,200},{16,208},{24,216},{32,224},{40,232},{48,240},{56,2... | collective-permute-start | bytes 786440 | tf_op jit(solution)/shard_map/ppermute | solution.py:291
  166.0 8.7 %collective-permute-start.20 = (bf16[128,1024]{1,0:T(8,128)(2,1)S(1)}, bf16[128,1024]{1,0:T(8,128)(2,1)S(1)}, u32[]{:S(2)}, u32[]{:S(2)}) collective-permute-start(bf16[128,1024]{1,0:T(8,128)(2,1)S(1)} %bitcast.115), channel_id=1, source_target_pairs={{0,64},{8,72},{16,80},{24,88},{32,96},{40,104},{48,112},{56,120},{... | collective-permute-start | bytes 786440 | tf_op jit(solution)/shard_map/ppermute | solution.py:291
  175.1 8.4 %collective-permute-start.29 = (bf16[16,1024]{1,0:T(8,128)(2,1)S(1)}, bf16[16,1024]{1,0:T(8,128)(2,1)S(1)}, u32[]{:S(2)}, u32[]{:S(2)}) collective-permute-start(bf16[16,1024]{1,0:T(8,128)(2,1)S(1)} %get-tuple-element.148), channel_id=1, source_target_pairs={{0,56},{8,0},{16,8},{24,16},{32,24},{40,32},{48,40},{56,48},{64,12... | collective-permute-start | bytes 98312 | tf_op jit(solution)/shard_map/ppermute | solution.py:291
  175.5 11.3 %collective-permute-start.28 = (bf16[16,1024]{1,0:T(8,128)(2,1)S(1)}, bf16[16,1024]{1,0:T(8,128)(2,1)S(1)}, u32[]{:S(2)}, u32[]{:S(2)}) collective-permute-start(bf16[16,1024]{1,0:T(8,128)(2,1)S(1)} %get-tuple-element.149), channel_id=1, source_target_pairs={{0,48},{8,56},{16,0},{24,8},{32,16},{40,24},{48,32},{56,40},{64,11... | collective-permute-start | bytes 98312 | tf_op jit(solution)/shard_map/ppermute | solution.py:291
  180.2 7.8 %collective-permute-start.27 = (bf16[16,1024]{1,0:T(8,128)(2,1)S(1)}, bf16[16,1024]{1,0:T(8,128)(2,1)S(1)}, u32[]{:S(2)}, u32[]{:S(2)}) collective-permute-start(bf16[16,1024]{1,0:T(8,128)(2,1)S(1)} %get-tuple-element.150), channel_id=1, source_target_pairs={{0,40},{8,48},{16,56},{24,0},{32,8},{40,16},{48,24},{56,32},{64,10... | collective-permute-start | bytes 98312 | tf_op jit(solution)/shard_map/ppermute | solution.py:291
  180.2 7.8 %collective-permute-start.26 = (bf16[16,1024]{1,0:T(8,128)(2,1)S(1)}, bf16[16,1024]{1,0:T(8,128)(2,1)S(1)}, u32[]{:S(2)}, u32[]{:S(2)}) collective-permute-start(bf16[16,1024]{1,0:T(8,128)(2,1)S(1)} %get-tuple-element.151), channel_id=1, source_target_pairs={{0,32},{8,40},{16,48},{24,56},{32,0},{40,8},{48,16},{56,24},{64,96... | collective-permute-start | bytes 98312 | tf_op jit(solution)/shard_map/ppermute | solution.py:291
  181.4 6.6 %collective-permute-start.25 = (bf16[16,1024]{1,0:T(8,128)(2,1)S(1)}, bf16[16,1024]{1,0:T(8,128)(2,1)S(1)}, u32[]{:S(2)}, u32[]{:S(2)}) collective-permute-start(bf16[16,1024]{1,0:T(8,128)(2,1)S(1)} %get-tuple-element.152), channel_id=1, source_target_pairs={{0,24},{8,32},{16,40},{24,48},{32,56},{40,0},{48,8},{56,16},{64,88... | collective-permute-start | bytes 98312 | tf_op jit(solution)/shard_map/ppermute | solution.py:291
  183.5 4.9 %collective-permute-start.24 = (bf16[16,1024]{1,0:T(8,128)(2,1)S(1)}, bf16[16,1024]{1,0:T(8,128)(2,1)S(1)}, u32[]{:S(2)}, u32[]{:S(2)}) collective-permute-start(bf16[16,1024]{1,0:T(8,128)(2,1)S(1)} %get-tuple-element.153), channel_id=1, source_target_pairs={{0,16},{8,24},{16,32},{24,40},{32,48},{40,56},{48,0},{56,8},{64,80... | collective-permute-start | bytes 98312 | tf_op jit(solution)/shard_map/ppermute | solution.py:291
  186.8 4.4 %collective-permute-start.23 = (bf16[16,1024]{1,0:T(8,128)(2,1)S(1)}, bf16[16,1024]{1,0:T(8,128)(2,1)S(1)}, u32[]{:S(2)}, u32[]{:S(2)}) collective-permute-start(bf16[16,1024]{1,0:T(8,128)(2,1)S(1)} %get-tuple-element.154), channel_id=1, source_target_pairs={{0,8},{8,16},{16,24},{24,32},{32,40},{40,48},{48,56},{56,0},{64,72... | collective-permute-start | bytes 98312 | tf_op jit(solution)/shard_map/ppermute | solution.py:291
  (12 other events, 157.9 us)
Sparse Core Ops, SparseCore 0:
  62.1 45.6 all-gather.7
Sparse Core Ops, SparseCore 1:
  166.3 50.0 reduce-scatter.1
